TPU v7x, 32 devices: a whole 2x2x4 slice. The times are simulated.
32 devices in a mesh: dp: 16 (over z, y, x), chan: 2 (over core).
Axes of the slice: x: 2, y: 2, z: 4, core: 2. Of those that a mesh axis runs over, the one named last changes fastest.
Arguments:
- features: bfloat16 [24576, 2048], P('dp', 'chan'), may hold values from -6 to 6
- boxes: int32 [48, 2, 4], P('dp'), may hold values from 0 to 22, as said below
- w_branch: bfloat16 [4, 2048, 512], P(None, 'chan'), may hold values from -0.125 to 0.125
- gain_branch: float32 [4, 512], P(None, 'chan'), may hold values from 0.5 to 1.5
- bias_branch: float32 [4, 512], P(None, 'chan'), may hold values from -3 to 3
- w_fx: bfloat16 [9, 2048, 512], P(None, 'chan'), may hold values from -0.03125 to 0.03125
- w_fb: bfloat16 [9, 4, 512, 512], P(None, None, 'chan'), may hold values from -0.03125 to 0.03125
- gain_join: float32 [512], replicated, may hold values from 0.5 to 1.5
- bias_join: float32 [512], replicated, may hold values from -3 to 3
- w_cls: bfloat16 [512, 150], replicated, may hold values from -0.25 to 0.25
- b_cls: float32 [150], replicated, may hold values from -4 to 4
- grad_logits: bfloat16 [24576, 150], P('dp'), may hold values from -6 to 6
Outputs:
- logits: bfloat16 [24576, 150], P('dp')
- grad_features: bfloat16 [24576, 2048], P('dp', 'chan')
- grad_w_branch: float32 [4, 2048, 512], P(None, 'chan', 'dp')
- grad_gain_branch: float32 [4, 512], P(None, 'chan')
- grad_bias_branch: float32 [4, 512], P(None, 'chan')
- grad_w_fx: float32 [9, 2048, 512], P(None, 'chan', 'dp')
- grad_w_fb: float32 [9, 4, 512, 512], P(None, None, 'chan', 'dp')
- grad_gain_join: float32 [512], replicated
- grad_bias_join: float32 [512], replicated
- grad_w_cls: float32 [512, 150], replicated
- grad_b_cls: float32 [150], replicated
Inputs may be any that keep to these rules, and one draw needn't show every extreme that they name: Each canvas holds 2 disjoint boxes (top, left, height, width) inside the 16 x 32 canvas, side by side; heights at least 8, widths at least 10; the rest is padding.
All inputs are finite; a program needn't handle non-finite values.
Results may differ from a plain program's by a relative error of at most 0.017.
Values may be sent and summed in bfloat16 or wider, within the bound.
A program may use at most 320 MiB of HBM per device.

v0:
```python
import jax
import jax.numpy as jnp
from jax import lax
from jax.sharding import PartitionSpec as P

CH = 16
CW = 32


EPS = 1e-05
BINS = (1, 2, 3, 6)
HIGH = lax.Precision.HIGHEST


def for_sending(array):

    def short(part):
        return part.astype(jnp.bfloat16) if part.dtype == jnp.float32 else part

    return jax.tree.map(short, array)


def box_tables(boxes):
    canv_count = boxes.shape[0]
    box_count = boxes.shape[1]
    places = jnp.arange(CH * CW, dtype=jnp.int32)
    place_y = places // CW
    place_x = places % CW
    top_edge = boxes[:, :, 0][:, :, None]
    left_edge = boxes[:, :, 1][:, :, None]
    height = boxes[:, :, 2][:, :, None]
    width = boxes[:, :, 3][:, :, None]
    rel_y = place_y[None, None, :] - top_edge
    rel_x = place_x[None, None, :] - left_edge
    inside = (rel_y >= 0) & (rel_y < height) & (rel_x >= 0) & (rel_x < width)
    box_ids = jnp.arange(box_count, dtype=jnp.int32)[None, :, None]
    labels = jnp.max(jnp.where(inside, box_ids, -1), axis=1)
    pools, counts, lifts = ([], [], [])
    for grid_size in BINS:
        cell_ids = jnp.arange(grid_size, dtype=jnp.int32)

        def member(relative, extent):
            start = cell_ids[None, None, :] * extent // grid_size
            stop = ((cell_ids[None, None, :] + 1) * extent + grid_size - 1) // grid_size
            inbin = (relative[:, :, None, :] >= start[..., None]) & (
                relative[:, :, None, :] < stop[..., None]
            )
            return (inbin, stop - start)

        def weights(relative, extent):
            numer = jnp.clip(relative, 0, extent - 1) * (grid_size - 1)
            denom = extent - 1
            low_cell = numer // denom
            frac = (numer - low_cell * denom).astype(jnp.float32) / denom.astype(jnp.float32)
            high_cell = jnp.minimum(low_cell + 1, grid_size - 1)
            first = (cell_ids == low_cell[..., None]).astype(jnp.float32) * (1.0 - frac)[..., None]
            second = (cell_ids == high_cell[..., None]).astype(jnp.float32) * frac[..., None]
            return first + second

        in_rows, len_rows = member(rel_y, height)
        in_cols, len_cols = member(rel_x, width)
        select = inside[:, :, None, None, :] & in_rows[:, :, :, None, :] & in_cols[:, :, None, :, :]
        pools.append(
            select.reshape(canv_count, box_count * grid_size * grid_size, CH * CW).astype(
                jnp.float32
            )
        )
        counts.append(
            (len_rows[:, :, :, None] * len_cols[:, :, None, :])
            .reshape(canv_count, -1)
            .astype(jnp.float32)
        )
        row_wts = weights(rel_y, height)
        col_wts = weights(rel_x, width)
        lifted = (
            inside.astype(jnp.float32)[..., None, None]
            * row_wts[..., :, None]
            * col_wts[..., None, :]
        )
        lifted = jnp.transpose(lifted, (0, 2, 1, 3, 4)).reshape(
            canv_count, CH * CW, box_count * grid_size * grid_size
        )
        lifts.append(lifted)
    return (labels, pools, counts, lifts)


def near_masks(labels):
    canv_count = labels.shape[0]
    label_grid = labels.reshape(canv_count, CH, CW)
    padded = jnp.pad(label_grid, ((0, 0), (1, 1), (1, 1)), constant_values=-2)
    result = []
    for offset in range(9):
        row_off, col_off = (offset // 3, offset % 3)
        nearby = padded[:, row_off : row_off + CH, col_off : col_off + CW]
        result.append(((nearby == label_grid) & (label_grid >= 0)).reshape(canv_count, CH * CW))
    return jnp.stack(result, -1).astype(jnp.float32)


def shift_in(values, offset, canv_count):
    depth = values.shape[-1]
    grid = values.reshape(canv_count, CH, CW, depth)
    padded = jnp.pad(grid, ((0, 0), (1, 1), (1, 1), (0, 0)))
    row_off, col_off = (offset // 3, offset % 3)
    return padded[:, row_off : row_off + CH, col_off : col_off + CW, :].reshape(
        canv_count * CH * CW, depth
    )


def shift_out(values, offset, canv_count):
    depth = values.shape[-1]
    grid = values.reshape(canv_count, CH, CW, depth)
    padded = jnp.pad(grid, ((0, 0), (1, 1), (1, 1), (0, 0)))
    row_off, col_off = (2 - offset // 3, 2 - offset % 3)
    return padded[:, row_off : row_off + CH, col_off : col_off + CW, :].reshape(
        canv_count * CH * CW, depth
    )


def place_in(vector, start, total):
    blank = jnp.zeros((total,) + vector.shape[1:], jnp.float32)
    return lax.dynamic_update_slice_in_dim(blank, vector, start, 0)


def per_device(
    features,
    boxes,
    w_branch,
    gain_branch,
    bias_branch,
    w_fx,
    w_fb,
    gain_join,
    bias_join,
    w_cls,
    b_cls,
    grad_logits,
):
    canv_count = boxes.shape[0]
    box_count = boxes.shape[1]
    pixels = canv_count * CH * CW
    cin_local = features.shape[1]
    mid_total = gain_join.shape[0]
    branch_width = gain_branch.shape[1]
    chan_index = lax.axis_index("chan")
    dp_count = lax.axis_size("dp")
    labels, pools, counts, lifts = box_tables(boxes)
    valid = (labels >= 0).astype(jnp.float32).reshape(pixels)
    gates_full = near_masks(labels).reshape(pixels, 9)
    masks = gates_full.astype(jnp.bfloat16)
    feat_grid = features.reshape(canv_count, CH * CW, cin_local)
    pooled_all, partials = ([], [])
    for level in range(4):
        summed = jnp.einsum(
            "ncp,npd->ncd",
            pools[level].astype(jnp.bfloat16),
            feat_grid,
            preferred_element_type=jnp.float32,
        )
        pooled = (summed / counts[level][..., None]).astype(jnp.bfloat16).reshape(-1, cin_local)
        pooled_all.append(pooled)
        partials.append(jnp.dot(pooled, w_branch[level], preferred_element_type=jnp.float32))
    branch_z = jax.tree.map(
        lambda part: part.astype(jnp.float32),
        lax.psum_scatter(for_sending(tuple(partials)), "chan", scatter_dimension=1, tiled=True),
    )
    first_sums = jnp.stack([jnp.sum(zval, 0) for zval in branch_z])
    second_sums = jnp.stack([jnp.sum(zval * zval, 0) for zval in branch_z])
    first_tot, second_tot = lax.psum((first_sums, second_sums), "dp")
    branch_norm, branch_rstd, branch_act, branch_rows, spreads, terms = ([], [], [], [], [], [])
    for level in range(4):
        grid_size = BINS[level]
        rows_all = float(canv_count * dp_count * box_count * grid_size * grid_size)
        average = first_tot[level] / rows_all
        variance = second_tot[level] / rows_all - average * average
        rstd = lax.rsqrt(variance + EPS)
        normed = (branch_z[level] - average) * rstd
        activ = gain_branch[level] * normed + bias_branch[level]
        spread = jax.nn.silu(activ).astype(jnp.bfloat16)
        spreads.append(spread)
        terms.append(
            jnp.einsum("rb,dbm->drm", spread, w_fb[:, level], preferred_element_type=jnp.float32)
        )
        branch_norm.append(normed)
        branch_rstd.append(rstd)
        branch_act.append(activ)
        branch_rows.append(rows_all)
    masked_x = features * valid[:, None].astype(jnp.bfloat16)
    join_part = jnp.zeros((pixels, mid_total), jnp.float32)
    for offset in range(9):
        gate = masks[:, offset : offset + 1]
        gate_full = gates_full[:, offset : offset + 1]
        moved_x = shift_in(masked_x, offset, canv_count) * gate
        branch_pix = jnp.zeros((canv_count, CH * CW, mid_total), jnp.float32)
        for level in range(4):
            cell_term = terms[level][offset].reshape(canv_count, -1, mid_total)
            branch_pix = branch_pix + jnp.einsum(
                "npc,ncm->npm", lifts[level], cell_term, precision=HIGH
            )
        join_part = join_part + jnp.dot(moved_x, w_fx[offset], preferred_element_type=jnp.float32)
        join_part = (
            join_part
            + shift_in(branch_pix.reshape(pixels, mid_total), offset, canv_count) * gate_full
        )
    joined = lax.psum_scatter(
        join_part.astype(jnp.bfloat16), "chan", scatter_dimension=1, tiled=True
    ).astype(jnp.float32)
    col_start = chan_index * joined.shape[1]
    share = (chan_index == 0).astype(jnp.float32)
    width_own = joined.shape[1]
    valid_own = valid[:, None]
    part_first = place_in(jnp.sum(joined * valid_own, 0), col_start, mid_total)
    part_second = place_in(jnp.sum(joined * joined * valid_own, 0), col_start, mid_total)
    count_own = jnp.sum(valid_own) * share
    total_first, total_second, total_count = lax.psum(
        (part_first, part_second, count_own), ("dp", "chan")
    )
    average = lax.dynamic_slice_in_dim(total_first, col_start, width_own) / total_count
    variance = (
        lax.dynamic_slice_in_dim(total_second, col_start, width_own) / total_count
        - average * average
    )
    rstd = lax.rsqrt(variance + EPS)
    gain_own = lax.dynamic_slice_in_dim(gain_join, col_start, width_own)
    bias_own = lax.dynamic_slice_in_dim(bias_join, col_start, width_own)
    normed = (joined - average) * rstd
    activ = gain_own * normed + bias_own
    hidden = (jax.nn.silu(activ) * valid_own).astype(jnp.bfloat16)
    w_rows = lax.dynamic_slice_in_dim(w_cls, col_start, width_own)
    score_part = jnp.dot(hidden, w_rows, preferred_element_type=jnp.float32)
    logits = (lax.psum(score_part.astype(jnp.bfloat16), "chan").astype(jnp.float32) + b_cls).astype(
        jnp.bfloat16
    )
    d_hidden = jnp.einsum("pk,mk->pm", grad_logits, w_rows, preferred_element_type=jnp.float32)
    d_wcls = jnp.einsum("pm,pk->mk", hidden, grad_logits, preferred_element_type=jnp.float32)
    d_bcls = jnp.sum(grad_logits.astype(jnp.float32), 0) * share
    sigma = jax.nn.sigmoid(activ)
    d_act = d_hidden * valid_own * sigma * (1.0 + activ * (1.0 - sigma))
    d_gain_own = jnp.sum(d_act * normed, 0)
    d_bias_own = jnp.sum(d_act, 0)
    grad_gain_join, grad_bias_join, grad_w_cls, grad_b_cls = lax.psum(
        (
            place_in(d_gain_own, col_start, mid_total),
            place_in(d_bias_own, col_start, mid_total),
            place_in(d_wcls, col_start, mid_total),
            d_bcls,
        ),
        ("dp", "chan"),
    )
    mean_gain = lax.dynamic_slice_in_dim(grad_gain_join, col_start, width_own) / total_count
    mean_bias = lax.dynamic_slice_in_dim(grad_bias_join, col_start, width_own) / total_count
    d_joined = (gain_own * rstd * (d_act - mean_bias - normed * mean_gain) * valid_own).astype(
        jnp.bfloat16
    )
    d_full = lax.all_gather(d_joined, "chan", axis=1, tiled=True)
    dx_acc = jnp.zeros((pixels, cin_local), jnp.float32)
    dwx_list = []
    cell_lists = [[], [], [], []]
    for offset in range(9):
        gate = masks[:, offset : offset + 1]
        gated_grad = d_full * gate
        back_x = jnp.einsum(
            "pm,cm->pc", gated_grad, w_fx[offset], preferred_element_type=jnp.float32
        )
        dx_acc = dx_acc + shift_out(back_x, offset, canv_count)
        moved_x = shift_in(masked_x, offset, canv_count) * gate
        dwx_list.append(
            jnp.einsum("pc,pm->cm", moved_x, d_full, preferred_element_type=jnp.float32)
        )
        spread_back = (
            shift_out(gated_grad, offset, canv_count)
            .astype(jnp.float32)
            .reshape(canv_count, CH * CW, mid_total)
        )
        for level in range(4):
            cell_grad = jnp.einsum("npc,npm->ncm", lifts[level], spread_back, precision=HIGH)
            cell_lists[level].append(cell_grad.astype(jnp.bfloat16).reshape(-1, mid_total))
    grad_fx_local = jnp.stack(dwx_list)
    cell_grads = [jnp.stack(cell_lists[level]) for level in range(4)]
    d_spreads = [
        jnp.einsum(
            "drm,dbm->rb", cell_grads[level], w_fb[:, level], preferred_element_type=jnp.float32
        )
        for level in range(4)
    ]
    grad_fb_local = jnp.stack(
        [
            jnp.einsum(
                "rb,drm->dbm", spreads[level], cell_grads[level], preferred_element_type=jnp.float32
            )
            for level in range(4)
        ],
        1,
    )
    d_acts, d_gains, d_biases = ([], [], [])
    for level in range(4):
        sig_branch = jax.nn.sigmoid(branch_act[level])
        d_activ = d_spreads[level] * sig_branch * (1.0 + branch_act[level] * (1.0 - sig_branch))
        d_acts.append(d_activ)
        d_gains.append(jnp.sum(d_activ * branch_norm[level], 0))
        d_biases.append(jnp.sum(d_activ, 0))
    grad_gain_branch, grad_bias_branch = lax.psum((jnp.stack(d_gains), jnp.stack(d_biases)), "dp")
    d_branch = []
    for level in range(4):
        d_zval = (
            gain_branch[level]
            * branch_rstd[level]
            * (
                d_acts[level]
                - grad_bias_branch[level] / branch_rows[level]
                - branch_norm[level] * grad_gain_branch[level] / branch_rows[level]
            )
        )
        d_branch.append(d_zval.astype(jnp.bfloat16))
    d_branch_full = lax.all_gather(for_sending(tuple(d_branch)), "chan", axis=1, tiled=True)
    grad_x = dx_acc * valid[:, None]
    grad_x = grad_x.reshape(canv_count, CH * CW, cin_local)
    dwbr_list = []
    for level in range(4):
        d_pooled = jnp.einsum(
            "re,de->rd", d_branch_full[level], w_branch[level], preferred_element_type=jnp.float32
        )
        dwbr_list.append(
            jnp.einsum(
                "rd,re->de",
                pooled_all[level],
                d_branch_full[level],
                preferred_element_type=jnp.float32,
            )
        )
        d_pooled = d_pooled.reshape(canv_count, -1, cin_local) / counts[level][..., None]
        grad_x = grad_x + jnp.einsum("ncp,ncd->npd", pools[level], d_pooled, precision=HIGH)
    grad_br_local = jnp.stack(dwbr_list)
    flat_fb = grad_fb_local.reshape(9, 4 * branch_width, mid_total)
    out_fx, out_fb, out_br = (
        lax.psum_scatter(grad_fx_local, "dp", scatter_dimension=2, tiled=True),
        lax.psum_scatter(flat_fb, "dp", scatter_dimension=2, tiled=True),
        lax.psum_scatter(grad_br_local, "dp", scatter_dimension=2, tiled=True),
    )
    out_fb = out_fb.reshape(9, 4, branch_width, out_fb.shape[-1])
    grad_features = grad_x.reshape(pixels, cin_local).astype(jnp.bfloat16)
    return (
        logits,
        grad_features,
        out_br,
        grad_gain_branch,
        grad_bias_branch,
        out_fx,
        out_fb,
        grad_gain_join,
        grad_bias_join,
        grad_w_cls,
        grad_b_cls,
    )


def solution(mesh):
    placed = (
        P("dp", "chan"),
        P("dp", None, None),
        P(None, "chan", None),
        P(None, "chan"),
        P(None, "chan"),
        P(None, "chan", None),
        P(None, None, "chan", None),
        P(),
        P(),
        P(),
        P(),
        P("dp", None),
    )
    return jax.shard_map(
        per_device,
        mesh=mesh,
        in_specs=placed,
        out_specs=(
            P("dp", None),
            P("dp", "chan"),
            P(None, "chan", "dp"),
            P(None, "chan"),
            P(None, "chan"),
            P(None, "chan", "dp"),
            P(None, None, "chan", "dp"),
            P(),
            P(),
            P(),
            P(),
        ),
        check_vma=False,
    )
```

profile of v0, /device:TPU:8, one launch (start us, length us, event | category | flops | bytes accessed | tf_op | source)
XLA Modules:
  0.0 2384.0 jit_solution(12160779382936579670)
XLA Ops:
  10.1 4.3 fusion.424
  49.2 14.5 pad_slice_fusion.8
  67.7 36.5 %all-reduce.30 = (f32[4,256]{1,0:T(4,128)S(1)}, f32[4,256]{1,0:T(4,128)S(1)}) all-reduce(f32[4,256]{1,0:T(4,128)S(1)} %pad_maximum_fusion.3, f32[4,256]{1,0:T(4,128)S(1)} %pad_maximum_fusion.2), channel_id=1, replica_groups=mesh['dp'=16,'chan'=2] {'dp'}, use_global_device_ids=true, to_apply=%region_14.16 | all-reduce | flops 2048 | bytes 16384 | tf_op jit(solution)/shard_map/psum | solution.py:168
  107.0 4.3 fusion.255
  111.3 4.3 fusion.254
  115.6 4.3 fusion.253
  120.0 4.3 fusion.252
  124.3 4.4 fusion.251
  128.7 4.5 fusion.250
  133.2 4.3 fusion.249
  137.5 4.4 fusion.248
  141.9 4.3 fusion.247
  167.7 4.3 fusion.416
  172.7 3.7 fusion.336
  176.5 5.8 add_add_fusion.7
  185.1 4.3 fusion.414
  190.2 3.8 fusion.334
  194.0 5.3 add_add_fusion.6
  202.4 4.5 fusion.412
  207.6 3.7 fusion.332
  211.4 5.2 add_add_fusion.5
  218.7 4.3 fusion.410
  223.1 4.8 fusion.330
  227.9 4.3 fusion.408
  235.2 5.2 add_add_fusion.3
  242.6 4.3 fusion.406
  250.2 5.2 add_add_fusion.2
  257.4 4.3 fusion.404
  264.7 5.4 add_add_fusion.1
  272.1 4.5 fusion.322
  279.4 5.1 add_add_fusion
  305.2 5.9 convolution_add_fusion.8
  311.1 4.4 fusion.16
  328.7 3.7 fusion.11
  335.7 4.4 fusion.17
  341.1 10.7 reduce-scatter.16.cloned.1.call-done
  353.8 40.4 %all-reduce.28 = (f32[512]{0:T(512)S(1)}, f32[]{:T(128)}, f32[512]{0:T(512)S(1)}) all-reduce(f32[512]{0:T(512)S(1)} %dynamic_update_slice.15, f32[]{:T(128)S(6)} %mul.1581, f32[512]{0:T(512)S(1)} %dynamic_update_slice.16), channel_id=1, replica_groups=mesh['dp'=16,'chan'=2] {'dp','chan'}, use_global_device_ids=true, to_apply=%region_17.19 | all-reduce | flops 1025 | bytes 8200 | tf_op jit(solution)/shard_map/psum | solution.py:214
  398.9 39.4 %all-reduce.27 = (f32[512]{0:T(512)S(1)}, f32[512]{0:T(512)S(1)}, f32[150]{0:T(256)}) all-reduce(f32[512]{0:T(512)S(1)} %dynamic_update_slice.18, f32[512]{0:T(512)S(1)} %dynamic_update_slice.17, f32[150]{0:T(256)S(1)} %broadcast_multiply_fusion.21), channel_id=1, replica_groups=mesh['dp'=16,'chan'=2] {'dp','chan'}, use_global_device_ids=true, to_apply=%region_26.28 | all-reduce | flops 1174 | bytes 9392 | tf_op jit(solution)/shard_map/psum | solution.py:240
  444.3 10.6 all-gather.2.cloned.1.call-done
  455.0 5.6 broadcast_multiply_fusion.9
  539.9 35.9 %all-reduce.29 = (f32[4,256]{1,0:T(4,128)S(1)}, f32[4,256]{1,0:T(4,128)S(1)}) all-reduce(f32[4,256]{1,0:T(4,128)S(1)} %pad_maximum_fusion.5, f32[4,256]{1,0:T(4,128)S(1)} %pad_maximum_fusion.4), channel_id=1, replica_groups=mesh['dp'=16,'chan'=2] {'dp'}, use_global_device_ids=true, to_apply=%region_36.38 | all-reduce | flops 2048 | bytes 16384 | tf_op jit(solution)/shard_map/psum | solution.py:301
  585.5 3.8 pad_maximum_fusion.1
  589.3 10.5 copy.373
  606.8 7.4 copy.375
  614.1 30.4 %copy.376 = f32[9,1024,512]{1,0,2:T(8,128)} copy(f32[9,1024,512]{2,1,0:T(8,128)} %bitcast.823) | data formatting | bytes 37748736 | tf_op jit(solution)/shard_map/reshape | solution.py:333
  646.6 7.5 pad_slice_fusion.9
  689.5 30.2 %copy.374 = f32[9,1024,512]{1,0,2:T(8,128)} copy(f32[9,1024,512]{2,1,0:T(8,128)} %bitcast_dynamic-update-slice_fusion) | data formatting | bytes 37748736 | tf_op jit(solution)/shard_map/stack | solution.py:277
  724.6 5.9 fusion.153
  730.5 5.9 fusion.155
  736.4 5.8 fusion.157
  742.3 5.8 fusion.159
  753.0 6.2 fusion.147
  759.2 5.9 fusion.149
  765.2 6.0 fusion.151
  771.2 5.8 fusion.165
  785.0 7.2 pad_slice_fusion.1
  792.2 6.9 pad_slice_fusion.2
  802.5 4.8 fusion.256
  807.3 12.2 fusion.2
  819.5 16.4 fusion.8
  835.9 21.5 all-reduce.39.cloned.1.call-done
  859.6 684.4 %reduce-scatter.20.cloned.1.call-done = f32[9,1024,32]{1,0,2:T(8,128)} async-done(((f32[9,1024,512]{1,0,2:T(8,128)}), f32[9,1024,32]{1,0,2:T(8,128)}) %reduce-scatter.20.cloned.1.call-update) | async-done | bytes 1179664 | tf_op jit(solution)/shard_map/reduce_scatter | solution.py:336
  1547.1 688.2 %reduce-scatter.18.cloned.1.call-done = f32[9,1024,32]{1,0,2:T(8,128)} async-done(((f32[9,1024,512]{1,0,2:T(8,128)}), f32[9,1024,32]{1,0,2:T(8,128)}) %reduce-scatter.18.cloned.1.call-update) | async-done | bytes 1179664 | tf_op jit(solution)/shard_map/reduce_scatter | solution.py:335
  2238.7 136.7 %all-reduce.37.cloned.1.call-done = f32[512,150]{0,1:T(8,128)} async-done(((f32[512,150]{0,1:T(8,128)}), f32[512,150]{0,1:T(8,128)}) %all-reduce.37.cloned.1.call-update) | async-done | bytes 307216 | tf_op jit(solution)/shard_map/psum | solution.py:240
  (919 shorter events, 305.3 us)
Async XLA Ops:
  7.2 387.7 %copy-start = (bf16[512,150]{0,1:T(8,128)(2,1)S(1)}, bf16[512,150]{0,1:T(8,128)(2,1)}, u32[]{:S(2)}) copy-start(bf16[512,150]{0,1:T(8,128)(2,1)} %param.23) | copy-start | bytes 460804
  7.2 57.2 %reduce-scatter.8.cloned.1.call-start = ((), (), s32[]{:S(2)}) async-start(), calls=%async_computation.7 | async-start | bytes 12288 | tf_op jit(solution)/shard_map/reduce_scatter | solution.py:164
  9.1 31.2 %copy-start.100 = (s32[3,2]{1,0:T(4,128)}, s32[3,2]{1,0:T(4,128)S(1)}, u32[]{:S(2)}) copy-start(s32[3,2]{1,0:T(4,128)S(1)} %copy.307) | copy-start | bytes 76
  9.2 32.8 %copy-start.102 = (s32[3,2]{1,0:T(4,128)}, s32[3,2]{1,0:T(4,128)S(1)}, u32[]{:S(2)}) copy-start(s32[3,2]{1,0:T(4,128)S(1)} %copy.311) | copy-start | bytes 76
  14.4 470.1 %copy-start.76 = (pred[3,2,512]{2,1,0:T(4,128)(4,1)}, pred[3,2,512]{2,1,0:T(4,128)(4,1)S(1)}, u32[]{:S(2)}) copy-start(pred[3,2,512]{2,1,0:T(4,128)(4,1)S(1)} %get-tuple-element.238) | copy-start | bytes 9220
  19.0 46.1 %reduce-scatter.10.cloned.1.call-start = ((), (), s32[]{:S(2)}) async-start(), calls=%async_computation.8 | async-start | bytes 36864 | tf_op jit(solution)/shard_map/reduce_scatter | solution.py:164
  22.8 43.1 %reduce-scatter.12.cloned.1.call-start = ((), (), s32[]{:S(2)}) async-start(), calls=%async_computation.9 | async-start | bytes 86016 | tf_op jit(solution)/shard_map/reduce_scatter | solution.py:164
  28.1 38.5 %reduce-scatter.14.cloned.1.call-start = ((), (), s32[]{:S(2)}) async-start(), calls=%async_computation.10 | async-start | bytes 331776 | tf_op jit(solution)/shard_map/reduce_scatter | solution.py:164
  37.1 314.7 %reduce-scatter.16.cloned.1.call-start = ((), (), s32[]{:S(2)}) async-start(), calls=%async_computation.11 | async-start | bytes 2359296 | tf_op jit(solution)/shard_map/reduce_scatter | solution.py:204
  40.2 64.7 %copy-start.243 = (f32[1,256]{1,0:T(1,128)}, f32[1,256]{1,0:T(1,128)S(1)}, u32[]{:S(2)}) copy-start(f32[1,256]{1,0:T(1,128)S(1)} %get-tuple-element.234) | copy-start | bytes 3076
  40.2 106.0 %copy-start.248 = (f32[1,256]{1,0:T(1,128)}, f32[1,256]{1,0:T(1,128)S(1)}, u32[]{:S(2)}) copy-start(f32[1,256]{1,0:T(1,128)S(1)} %get-tuple-element.233) | copy-start | bytes 3076
  40.2 108.2 %copy-start.241 = (f32[1,256]{1,0:T(1,128)}, f32[1,256]{1,0:T(1,128)S(1)}, u32[]{:S(2)}) copy-start(f32[1,256]{1,0:T(1,128)S(1)} %get-tuple-element.236) | copy-start | bytes 3076
  43.9 98.1 %copy-start.19 = (f32[3,512,8]{1,2,0:T(8,128)}, f32[3,512,8]{1,2,0:T(8,128)S(1)}, u32[]{:S(2)}) copy-start(f32[3,512,8]{1,2,0:T(8,128)S(1)} %mul.1452) | copy-start | bytes 147460
  44.0 104.4 %copy-start.239 = (f32[1,256]{1,0:T(1,128)}, f32[1,256]{1,0:T(1,128)S(1)}, u32[]{:S(2)}) copy-start(f32[1,256]{1,0:T(1,128)S(1)} %slice.492) | copy-start | bytes 3076
  104.8 41.4 %copy-start.232 = (f32[1,256]{1,0:T(1,128)}, f32[1,256]{1,0:T(1,128)S(1)}, u32[]{:S(2)}) copy-start(f32[1,256]{1,0:T(1,128)S(1)} %get-tuple-element.105) | copy-start | bytes 3076
  104.9 41.3 %copy-start.234 = (f32[1,256]{1,0:T(1,128)}, f32[1,256]{1,0:T(1,128)S(1)}, u32[]{:S(2)}) copy-start(f32[1,256]{1,0:T(1,128)S(1)} %get-tuple-element.227) | copy-start | bytes 3076
  104.9 41.3 %copy-start.246 = (f32[1,256]{1,0:T(1,128)}, f32[1,256]{1,0:T(1,128)S(1)}, u32[]{:S(2)}) copy-start(f32[1,256]{1,0:T(1,128)S(1)} %get-tuple-element.226) | copy-start | bytes 3076
  104.9 43.6 %copy-start.220 = (f32[1,256]{1,0:T(1,128)}, f32[1,256]{1,0:T(1,128)S(1)}, u32[]{:S(2)}) copy-start(f32[1,256]{1,0:T(1,128)S(1)} %get-tuple-element.193) | copy-start | bytes 3076
  104.9 43.6 %copy-start.222 = (f32[1,256]{1,0:T(1,128)}, f32[1,256]{1,0:T(1,128)S(1)}, u32[]{:S(2)}) copy-start(f32[1,256]{1,0:T(1,128)S(1)} %get-tuple-element.228) | copy-start | bytes 3076
  115.6 30.6 %slice-start = ((s8[9437184]{0:T(1024)(128)(4,1)}), s8[4194304]{0:T(1024)(128)(4,1)S(1)}, s32[]{:S(2)}) async-start(s8[9437184]{0:T(1024)(128)(4,1)} %bitcast.885), calls=%async_computation.18 | async-start | bytes 8388608
  124.3 22.0 slice-start.1
  335.7 16.1 copy-start.131
  335.7 58.5 %copy-start.271 = (f32[512]{0:T(512)S(1)}, f32[512]{0:T(512)}, u32[]{:S(2)}) copy-start(f32[512]{0:T(512)} %param.21) | copy-start | bytes 6148
  340.2 114.8 %all-gather.2.cloned.1.call-start = ((), (), s32[]{:S(2)}) async-start(), calls=%async_computation.13 | async-start | bytes 2359296 | tf_op jit(solution)/shard_map/all_gather | solution.py:254
  394.9 44.8 %copy-start.60 = (bf16[1536,256]{1,0:T(8,128)(2,1)S(1)}, bf16[1536,256]{1,0:T(8,128)(2,1)}, u32[]{:S(2)}) copy-start(bf16[1536,256]{1,0:T(8,128)(2,1)} %reduce-scatter.16.cloned.1.call-done) | copy-start | bytes 2359300
  439.7 15.2 copy-start.157
  439.7 15.2 copy-start.160
  439.7 15.2 copy-start.163
  439.7 15.2 copy-start.166
  439.7 15.2 copy-start.169
  439.7 15.2 copy-start.172
  439.7 15.2 copy-start.175
  443.0 279.7 %all-reduce.35.cloned.1.call-start = ((), (), s32[]{:S(2)}) async-start(), calls=%async_computation.12 | async-start | bytes 933888 | tf_op jit(solution)/shard_map/psum | solution.py:230
  444.2 413.2 %all-reduce.39.cloned.1.call-start = ((), (), s32[]{:S(2)}) async-start(), calls=%async_computation.17 | async-start | bytes 16777216
  460.6 15.9 copy-start.44
  460.6 18.4 copy-start.46
  460.6 21.3 copy-start.48
  460.6 23.2 copy-start.50
  460.6 48.0 %copy-start.6 = (bf16[1536,512]{1,0:T(8,128)(2,1)}, bf16[1536,512]{1,0:T(8,128)(2,1)S(1)}, u32[]{:S(2)}) copy-start(bf16[1536,512]{1,0:T(8,128)(2,1)S(1)} %get-tuple-element.153) | copy-start | bytes 4718596
  466.0 22.4 copy-start.8
  469.1 17.8 copy-start.9
  472.4 18.7 copy-start.10
  477.3 16.6 copy-start.11
  479.8 15.5 copy-start.13
  510.1 15.3 copy-start.211
  510.1 15.3 copy-start.210
  510.1 15.3 copy-start.209
  510.1 15.4 copy-start.80
  513.2 15.7 copy-start.134
  537.2 38.7 %copy-start.257 = (f32[1,256]{1,0:T(1,128)S(1)}, f32[1,256]{1,0:T(1,128)}, u32[]{:S(2)}) copy-start(f32[1,256]{1,0:T(1,128)} %get-tuple-element.104) | copy-start | bytes 3076
  537.3 40.7 %copy-start.99 = (bf16[3,72,1024]{2,1,0:T(8,128)(2,1)S(1)}, bf16[3,72,1024]{2,1,0:T(8,128)(2,1)}, u32[]{:S(2)}) copy-start(bf16[3,72,1024]{2,1,0:T(8,128)(2,1)} %copy-done.98) | copy-start | bytes 1327108
  537.3 41.2 %copy-start.216 = (f32[1,256]{1,0:T(1,128)S(1)}, f32[1,256]{1,0:T(1,128)}, u32[]{:S(2)}) copy-start(f32[1,256]{1,0:T(1,128)} %get-tuple-element.189) | copy-start | bytes 3076
  537.3 41.2 %copy-start.217 = (f32[1,256]{1,0:T(1,128)S(1)}, f32[1,256]{1,0:T(1,128)}, u32[]{:S(2)}) copy-start(f32[1,256]{1,0:T(1,128)} %get-tuple-element.230) | copy-start | bytes 3076
  537.3 41.2 %copy-start.259 = (f32[1,256]{1,0:T(1,128)S(1)}, f32[1,256]{1,0:T(1,128)}, u32[]{:S(2)}) copy-start(f32[1,256]{1,0:T(1,128)} %get-tuple-element.188) | copy-start | bytes 3076
  537.3 43.0 %copy-start.226 = (f32[1,256]{1,0:T(1,128)S(1)}, f32[1,256]{1,0:T(1,128)}, u32[]{:S(2)}) copy-start(f32[1,256]{1,0:T(1,128)} %copy-done.224) | copy-start | bytes 3076
  537.3 43.0 %copy-start.229 = (f32[1,256]{1,0:T(1,128)S(1)}, f32[1,256]{1,0:T(1,128)}, u32[]{:S(2)}) copy-start(f32[1,256]{1,0:T(1,128)} %copy-done.227) | copy-start | bytes 3076
  537.3 43.0 %copy-start.258 = (f32[1,256]{1,0:T(1,128)S(1)}, f32[1,256]{1,0:T(1,128)}, u32[]{:S(2)}) copy-start(f32[1,256]{1,0:T(1,128)} %get-tuple-element.190) | copy-start | bytes 3076
  537.3 44.9 %copy-start.97 = (bf16[24,1024]{1,0:T(8,128)(2,1)S(1)}, bf16[24,1024]{1,0:T(8,128)(2,1)}, u32[]{:S(2)}) copy-start(bf16[24,1024]{1,0:T(8,128)(2,1)} %copy-done.96) | copy-start | bytes 147460
  539.9 42.8 %copy-start.256 = (f32[1,256]{1,0:T(1,128)S(1)}, f32[1,256]{1,0:T(1,128)}, u32[]{:S(2)}) copy-start(f32[1,256]{1,0:T(1,128)} %get-tuple-element.192) | copy-start | bytes 3076
  539.9 44.6 %copy-start.87 = (bf16[54,1024]{1,0:T(8,128)(2,1)S(1)}, bf16[54,1024]{1,0:T(8,128)(2,1)}, u32[]{:S(2)}) copy-start(bf16[54,1024]{1,0:T(8,128)(2,1)} %reshape.900) | copy-start | bytes 331780
  599.9 944.0 %reduce-scatter.20.cloned.1.call-start = ((), (), s32[]{:S(2)}) async-start(), calls=%async_computation.15 | async-start | bytes 35651584 | tf_op jit(solution)/shard_map/reduce_scatter | solution.py:336
  644.6 1590.8 %reduce-scatter.18.cloned.1.call-start = ((), (), s32[]{:S(2)}) async-start(), calls=%async_computation.14 | async-start | bytes 35651584 | tf_op jit(solution)/shard_map/reduce_scatter | solution.py:335
  719.7 1655.7 %all-reduce.37.cloned.1.call-start = ((), (), s32[]{:S(2)}) async-start(), calls=%async_computation.16 | async-start | bytes 622592 | tf_op jit(solution)/shard_map/psum | solution.py:240
  1543.9 833.1 %copy-start.1 = (bf16[512,150]{0,1:T(8,128)(2,1)S(1)}, bf16[512,150]{0,1:T(8,128)(2,1)}, u32[]{:S(2)}) copy-start(bf16[512,150]{0,1:T(8,128)(2,1)} %param.23) | copy-start | bytes 460804
  (225 other events, 1160.5 us)
Sparse Core Ops, SparseCore 0:
  19.2 8.7 reduce-scatter.7
  30.7 8.5 reduce-scatter.9
  42.1 8.5 reduce-scatter.11
  53.4 8.7 reduce-scatter.13
  340.3 11.5 reduce-scatter.15
  443.1 11.7 all-gather.1
  458.0 19.8 all-reduce.34
  600.0 257.3 all-reduce.38
  859.9 684.0 reduce-scatter.19
  1546.3 689.0 reduce-scatter.17
  2242.2 133.1 all-reduce.36
where the time goes:
time: 2390 us; the launch traced here: 2380 us
  waiting for transfers between devices  1550 us (65%)
  matrix products  380 us (16%)
  local copies, waits for them, and re-layouts  197 us (8%)
  blocking collectives  160 us (7%)
  other arithmetic  74.4 us (3%)
    reduce_scatter x1, waiting for transfers between devices, per_device(): lax.psum_scatter(grad_fx_local, 'dp', scatter_dimension=2, tiled=True)  688 us
    reduce_scatter x1, waiting for transfers between devices, per_device(): lax.psum_scatter(flat_fb, 'dp', scatter_dimension=2, tiled=True)  684 us
    dot_general x36, matrix products, per_device(): jnp.einsum('npc,ncm->npm', lifts[level], cell_term, precision=HIGH)  152 us
    psum x1, waiting for transfers between devices, per_device(): lax.psum((place_in(d_gain_own, col_start, mid_total), place_in(d_bias_own...  137 us
    dot_general x9, matrix products, per_device(): jnp.einsum('pm,cm->pc', gated_grad, w_fx[offset], preferred_element_type=...  50.6 us
  transfers between devices with their start and end apart: 11, of which 6 were waited for; matrix products, arithmetic and copies ran while one was open for 16% of the time, Pallas kernels for 0%

commit v1 on v0

v1 whole, which is shorter than its diff:
```python
import functools

import jax
import jax.numpy as jnp
import numpy as np
from jax import lax
from jax.experimental import pallas as pl
from jax.experimental.pallas import tpu as pltpu
from jax.sharding import PartitionSpec as P

CH = 16
CW = 32
PX = CH * CW
EPS = 1e-05
BINS = (1, 2, 3, 6)
CELLS = 128
PLANE = 4
F32 = jnp.float32
BF16 = jnp.bfloat16
MESH = pl.DeviceIdType.MESH
VMEM_SPEC = pl.BlockSpec(memory_space=pltpu.VMEM)
SMEM_SPEC = pl.BlockSpec(memory_space=pltpu.SMEM)
ANY_SPEC = pl.BlockSpec(memory_space=pl.ANY)
NT = (((1,), (1,)), ((), ()))
TN = (((0,), (0,)), ((), ()))


COST_UNIT = 1_000_000_000
COSTS = {
    "pool": 12, "branch_sums": 2, "branch_act": 2, "join": 42, "join_sums": 4, "head": 5, "join_grad": 5,
    "branch_back": 16, "branch_dz": 2, "lifts": 10, "wgrad_fb": 15, "wgrad_fx0": 24, "wgrad_fx1": 24, "wgrad_br": 6,
    "dx": 33, "grad_x": 9,
}


def params(**extra):
    return pltpu.CompilerParams(vmem_limit_bytes=56 * 2**20, **extra)


def dot(a, b):
    return jnp.dot(a, b, preferred_element_type=F32)


def dot_nt(a, b):
    return lax.dot_general(a, b, NT, preferred_element_type=F32)


def dot_tn(a, b):
    return lax.dot_general(a, b, TN, preferred_element_type=F32)


def cell_table(box_count):
    table = np.zeros((8, CELLS), np.float32)
    table[1] = 1.0
    table[4] = 9.0
    at = 0
    for level, bins in enumerate(BINS):
        for box in range(box_count):
            for i in range(bins):
                for j in range(bins):
                    table[:6, at] = (box, bins, i, j, level, 1.0)
                    at += 1
    return table


def box_at(boxes_ref, canvas, box, box_count):
    base = (canvas * box_count + box) * 4
    return [boxes_ref[base + part] for part in range(4)]


def by_box(boxes_ref, canvas, which, box_count):
    sides = None
    for box in range(box_count):
        mine = [side.astype(F32) for side in box_at(boxes_ref, canvas, box, box_count)]
        if sides is None:
            sides = [jnp.full(which.shape, side, F32) for side in mine]
        else:
            sides = [jnp.where(which == box, new, old) for new, old in zip(mine, sides)]
    return sides


def within(relative, extent):
    return (relative >= 0) & (relative < extent)


def pixel_gates(boxes_ref, canvas, box_count, shape, axis):
    place = lax.broadcasted_iota(jnp.int32, shape, axis)
    row = place >> 5
    col = place & (CW - 1)
    rel = []
    for box in range(box_count):
        top, left, height, width = box_at(boxes_ref, canvas, box, box_count)
        rel.append((row - top, col - left, height, width))

    def gate(dy, dx):
        total = None
        for y, x, height, width in rel:
            hit = within(y, height) & within(x, width)
            if dy:
                hit = hit & within(y + dy, height)
            if dx:
                hit = hit & within(x + dx, width)
            value = jnp.where(hit, 1.0, 0.0)
            total = value if total is None else total + value
        return total

    return gate


def wide(column_block, times):
    return jnp.concatenate([column_block] * times, axis=1)


def member_bounds(table_at, height, width):
    bins, i, j = table_at(1), table_at(2), table_at(3)

    def start(at, extent):
        return jnp.floor((at * extent + 0.5) / bins)

    def stop(at, extent):
        return jnp.floor(((at + 1) * extent + bins - 0.5) / bins)

    return start(i, height), stop(i, height), start(j, width), stop(j, width)


def members(boxes_ref, canvas, box_count, table_at, shape, axis):
    top, left, height, width = by_box(boxes_ref, canvas, table_at(0), box_count)
    r0, r1, c0, c1 = member_bounds(table_at, height, width)
    place = lax.broadcasted_iota(jnp.int32, shape, axis)
    row = (place >> 5).astype(F32) - top
    col = (place & (CW - 1)).astype(F32) - left
    hit = (row >= r0) & (row < r1) & (col >= c0) & (col < c1) & (table_at(5) > 0)
    return jnp.where(hit, 1.0, 0.0), (r1 - r0) * (c1 - c0)


def gated_lifts(boxes_ref, canvas, box_count, lanes_ref):
    def table_at(row):
        return lanes_ref[row : row + 1, :]

    top, left, height, width = by_box(boxes_ref, canvas, table_at(0), box_count)
    place = lax.broadcasted_iota(jnp.int32, (PX, CELLS), 0)
    row = (place >> 5).astype(F32) - top
    col = (place & (CW - 1)).astype(F32) - left

    def side(relative, extent, cell):
        scale = (table_at(1) - 1.0) / (extent - 1.0)
        own = within(relative, extent)
        found = []
        for step in (-1, 0, 1):
            moved = relative + step
            weight = jnp.maximum(0.0, 1.0 - jnp.abs(moved * scale - cell))
            found.append(jnp.where(own & within(moved, extent), weight, 0.0))
        return found

    rows = [found * table_at(5) for found in side(row, height, table_at(2))]
    cols = side(col, width, table_at(3))
    return [rows[d // 3] * cols[d % 3] for d in range(9)]


def pltranspose(block):
    return jnp.transpose(block, (1, 0))


def lifts_kernel(box_count, boxes_ref, lanes_ref, out_ref):
    lifts = gated_lifts(boxes_ref, pl.program_id(0), box_count, lanes_ref)
    for d in range(9):
        out_ref[0, :, d * CELLS : (d + 1) * CELLS] = lifts[d].astype(BF16)


def pool_kernel(canv, box_count, boxes_ref, lanes_ref, cells_ref, x_ref, w_ref, pooled_ref, lift_ref, own_ref, send_ref, first_ref, last_ref, kept, zs):
    n = pl.program_id(0)
    span = first_ref.shape[1]
    first_ref[...] = x_ref[:, :span]
    last_ref[...] = x_ref[:, span:]

    def table_at(row):
        return cells_ref[:, row : row + 1]

    select, count = members(boxes_ref, n, box_count, table_at, (CELLS, PX), 1)
    pooled = (dot(select.astype(BF16), x_ref[...]) / count).astype(BF16)
    pooled_ref[...] = pooled
    kept[pl.ds(pl.multiple_of(n * CELLS, CELLS), CELLS), :] = pooled
    lifts = gated_lifts(boxes_ref, n, box_count, lanes_ref)
    for d in range(9):
        lift_ref[0, :, d * CELLS : (d + 1) * CELLS] = lifts[d].astype(BF16)

    @pl.when(n == canv - 1)
    def _():
        half = own_ref.shape[1]
        for level in range(4):
            part = dot(kept[...], w_ref[level])
            for m in range(canv):
                rows = slice(m * CELLS, (m + 1) * CELLS)
                mine = jnp.where(table_at(4) == level, part[rows], 0.0)
                zs[rows, :] = mine if level == 0 else zs[rows, :] + mine
        chan = lax.axis_index("chan")
        own_ref[...] = zs[:, pl.ds(pl.multiple_of(chan * half, half), half)]
        send_ref[...] = zs[:, pl.ds(pl.multiple_of((1 - chan) * half, half), half)].astype(BF16)


def branch_sums_kernel(canv, cells_ref, own_ref, got_ref, z_ref, part_ref):
    z = own_ref[...] + got_ref[...].astype(F32)
    z_ref[...] = z
    for level in range(4):
        first = second = 0.0
        for n in range(canv):
            mine = jnp.where(cells_ref[:, 4:5] == level, z[n * CELLS : (n + 1) * CELLS], 0.0)
            first = first + jnp.sum(mine, 0, keepdims=True)
            second = second + jnp.sum(mine * mine, 0, keepdims=True)
        part_ref[level : level + 1, :] = first
        part_ref[4 + level : 5 + level, :] = second


def exchange_kernel(total, own_ref, out_ref, slots, send_sem, recv_sem):
    me = lax.axis_index("dp")
    chan = lax.axis_index("chan")
    barrier = pltpu.get_barrier_semaphore()

    def signal(step, carry):
        pl.semaphore_signal(barrier, inc=1, device_id=(lax.rem(me + step, total), chan), device_id_type=MESH)
        return carry

    lax.fori_loop(1, total, signal, 0)
    slots[me] = own_ref[...]
    pl.semaphore_wait(barrier, total - 1)

    def copy_to(step):
        return pltpu.make_async_remote_copy(
            src_ref=own_ref,
            dst_ref=slots.at[me],
            send_sem=send_sem.at[step],
            recv_sem=recv_sem.at[me],
            device_id=(lax.rem(me + step, total), chan),
            device_id_type=MESH,
        )

    def copy_from(step):
        other = lax.rem(me + total - step, total)
        return pltpu.make_async_remote_copy(
            src_ref=own_ref,
            dst_ref=slots.at[other],
            send_sem=send_sem.at[step],
            recv_sem=recv_sem.at[other],
            device_id=(other, chan),
            device_id_type=MESH,
        )

    def start(step, carry):
        copy_to(step).start()
        return carry

    def finish(step, carry):
        copy_from(step).wait_recv()
        return carry

    def sent(step, carry):
        copy_to(step).wait_send()
        return carry

    lax.fori_loop(1, total, start, 0)
    lax.fori_loop(1, total, finish, 0)
    lax.fori_loop(1, total, sent, 0)
    value = slots[0]
    for other in range(1, total):
        value = value + slots[other]
    out_ref[...] = value


def dp_sum(part, total, number, after=()):
    return launch(
        functools.partial(exchange_kernel, total),
        after=after,
        out_shape=jax.ShapeDtypeStruct(part.shape, F32),
        in_specs=[VMEM_SPEC],
        out_specs=VMEM_SPEC,
        scratch_shapes=[
            pltpu.VMEM((total,) + part.shape, F32),
            pltpu.SemaphoreType.DMA((total,)),
            pltpu.SemaphoreType.DMA((total,)),
        ],
        compiler_params=pltpu.CompilerParams(collective_id=number, has_side_effects=True),
        name="dp_sum%d" % number,
    )(part)


def branch_stat(total_ref, level, rows_all):
    mean = total_ref[level : level + 1, :] / rows_all
    var = total_ref[4 + level : 5 + level, :] / rows_all - mean * mean
    return mean, lax.rsqrt(var + EPS)


def branch_act_kernel(canv, rows_all, cells_ref, z_ref, total_ref, gain_ref, bias_ref, y_ref, norm_ref, act_ref):
    for n in range(canv):
        rows = slice(n * CELLS, (n + 1) * CELLS)
        z = z_ref[rows]
        norm = act = 0.0
        for level in range(4):
            mean, rstd = branch_stat(total_ref, level, rows_all[level])
            here = jnp.where(cells_ref[:, 4:5] == level, 1.0, 0.0)
            mine = (z - mean) * rstd
            norm = norm + here * mine
            act = act + here * (gain_ref[level : level + 1, :] * mine + bias_ref[level : level + 1, :])
        norm_ref[rows] = norm
        act_ref[rows] = act
        y_ref[rows] = (act * jax.nn.sigmoid(act)).astype(BF16)

def expand(y, cells_ref, keep):
    width = y.shape[1]
    for n in range(y.shape[0] // CELLS):
        rows = slice(n * CELLS, (n + 1) * CELLS)
        block = y[rows].astype(F32)
        for level in range(4):
            mine = jnp.where(cells_ref[:, 4:5] == level, block, 0.0)
            keep[rows, level * width : (level + 1) * width] = mine.astype(BF16)


def join_kernel(canv, box_count, boxes_ref, cells_ref, x_ref, y_ref, lift_ref, wfx_ref, wfb_ref, own_ref, send_ref, q, gy, zp, ye):
    d = pl.program_id(0)
    dy = d // 3
    dx = d % 3
    mid = wfx_ref.shape[2]
    reps = mid // CELLS

    @pl.when(d == 0)
    def _():
        q[...] = jnp.zeros_like(q)
        zp[...] = jnp.zeros_like(zp)
        expand(y_ref[...], cells_ref, ye)
        for n in range(canv):
            gate = pixel_gates(boxes_ref, n, box_count, (PX, CELLS), 0)
            for step in range(3):
                gy[step, n] = gate(step - 1, 0)

    wfb = wfb_ref[0].reshape(ye.shape[1], mid)
    terms = dot(ye[...], wfb).astype(BF16)
    for n in range(canv):
        zp[n, CW : CW + PX] = dot(x_ref[n * PX : (n + 1) * PX], wfx_ref[0])
        q[1, n] += dot(lift_ref[n], terms[n * CELLS : (n + 1) * CELLS])
    for n in range(canv):
        moved = zp[n, pl.ds(pl.multiple_of(dy * CW, CW), PX)]
        q[dx, n] += wide(gy[dy, n], reps) * moved

    @pl.when(d == 8)
    def _():
        half = own_ref.shape[1]
        chan = lax.axis_index("chan")
        for n in range(canv):
            gate = pixel_gates(boxes_ref, n, box_count, (PX, CELLS), 0)
            f = q[1, n] + wide(gate(0, -1), reps) * pltpu.roll(q[0, n], 1, 0)
            f = f + wide(gate(0, 1), reps) * pltpu.roll(q[2, n], PX - 1, 0)
            zp[n, CW : CW + PX] = f
            rows = slice(n * PX, (n + 1) * PX)
            own_ref[rows] = zp[n, CW : CW + PX, pl.ds(pl.multiple_of(chan * half, half), half)]
            send_ref[rows] = zp[n, CW : CW + PX, pl.ds(pl.multiple_of((1 - chan) * half, half), half)].astype(BF16)


def join_sums_kernel(canv, box_count, boxes_ref, own_ref, got_ref, f_ref, part_ref):
    n = pl.program_id(0)
    f = own_ref[...] + got_ref[...].astype(F32)
    f_ref[...] = f

    @pl.when(n == 0)
    def _():
        part_ref[...] = jnp.zeros_like(part_ref)

    area = 0
    for box in range(box_count):
        side = box_at(boxes_ref, n, box, box_count)
        area = area + side[2] * side[3]
    part_ref[0:1, :] += jnp.sum(f, 0, keepdims=True)
    part_ref[1:2, :] += jnp.sum(f * f, 0, keepdims=True)
    part_ref[2:3, :] += jnp.full((1, f.shape[1]), area.astype(F32), F32)


def join_stat(total_ref):
    count = total_ref[2:3, :]
    mean = total_ref[0:1, :] / count
    var = total_ref[1:2, :] / count - mean * mean
    return mean, lax.rsqrt(var + EPS), count


def head_kernel(box_count, boxes_ref, f_ref, total_ref, gain_ref, bias_ref, w_ref, g_ref, score_ref, db_ref, part_ref, dw_ref):
    n = pl.program_id(0)
    half = f_ref.shape[1]
    chan = lax.axis_index("chan")
    w = w_ref[pl.ds(pl.multiple_of(chan * half, half), half), :]
    own = pl.ds(pl.multiple_of(chan * half, half), half)
    valid = wide(pixel_gates(boxes_ref, n, box_count, (PX, CELLS), 0)(0, 0), half // CELLS)
    mean, rstd, _ = join_stat(total_ref)
    norm = (f_ref[...] - mean) * rstd
    act = gain_ref[:, own] * norm + bias_ref[:, own]
    sig = jax.nn.sigmoid(act)
    hidden = (act * sig * valid).astype(BF16)
    g = g_ref[...]
    score_ref[...] = dot(hidden, w).astype(BF16)
    db = dot_nt(g, w) * valid * sig * (1.0 + act * (1.0 - sig))
    db_ref[...] = db

    @pl.when(n == 0)
    def _():
        part_ref[...] = jnp.zeros_like(part_ref)
        dw_ref[...] = jnp.zeros_like(dw_ref)

    part_ref[0:1, :] += jnp.sum(db * norm, 0, keepdims=True)
    part_ref[1:2, :] += jnp.sum(db, 0, keepdims=True)
    part_ref[2:3, : g.shape[1]] += jnp.sum(g.astype(F32), 0, keepdims=True)
    dw_ref[...] += dot_tn(hidden, g)


def split_rows(rows, groups, each, own_a, send_a, own_b, send_b, send_d=None):
    me = lax.axis_index("dp")
    x_bit = me % 2
    y_bit = (me // 2) % 2

    def piece(group, y, x):
        return rows[pl.ds(pl.multiple_of(((group * 2 + y) * 2 + x) * each, each), each), :].astype(BF16)

    for group in range(groups):
        for bit in range(2):
            at = (bit * groups + group) * each
            own_a[at : at + each] = piece(group, bit, x_bit)
            send_a[at : at + each] = piece(group, bit, 1 - x_bit)
            own_b[at : at + each] = piece(group, y_bit, bit)
            send_b[at : at + each] = piece(group, 1 - y_bit, bit)
        if send_d is not None:
            send_d[group * each : (group + 1) * each] = piece(group, 1 - y_bit, 1 - x_bit)


def join_grad_kernel(box_count, each, boxes_ref, f_ref, db_ref, total_ref, sums_ref, gain_ref, df_ref, pack_ref, send_a, send_b, send_d, flip):
    n = pl.program_id(0)
    half = f_ref.shape[1]
    own = pl.ds(pl.multiple_of(lax.axis_index("chan") * half, half), half)
    valid = wide(pixel_gates(boxes_ref, n, box_count, (PX, CELLS), 0)(0, 0), half // CELLS)
    mean, rstd, count = join_stat(total_ref)
    norm = (f_ref[...] - mean) * rstd
    df = gain_ref[:, own] * rstd * (db_ref[...] - sums_ref[1:2, :] / count - norm * (sums_ref[0:1, :] / count)) * valid
    df_ref[...] = df.astype(BF16)
    flip[...] = pltranspose(df)
    pack_ref[0:half] = flip[...].astype(BF16)
    own_a = pack_ref.at[half : half + half // 2]
    own_b = pack_ref.at[half + half // 2 : 2 * half]
    split_rows(flip, half // (4 * each), each, own_a, send_a, own_b, send_b, send_d)


def dx_kernel(canv, box_count, boxes_ref, own_ref, got_ref, w_ref, out_ref, acc, gy, e3):
    d = pl.program_id(0)
    dy = d // 3
    dx = d % 3
    half = own_ref.shape[1]
    reps = half // CELLS
    chan = lax.axis_index("chan")

    @pl.when(d == 0)
    def _():
        e3[...] = jnp.zeros_like(e3)
        for n in range(canv):
            gate = pixel_gates(boxes_ref, n, box_count, (PX, CELLS), 0)
            for step in range(3):
                gy[step, n] = gate(1 - step, 0).astype(BF16)
            rows = slice(n * PX, (n + 1) * PX)
            for side, ref in enumerate((own_ref, got_ref)):
                df = ref[rows].astype(F32)
                e3[side, 1, n, CW : CW + PX] = df.astype(BF16)
                e3[side, 0, n, CW : CW + PX] = (wide(gate(0, 1), reps) * pltpu.roll(df, PX - 1, 0)).astype(BF16)
                e3[side, 2, n, CW : CW + PX] = (wide(gate(0, -1), reps) * pltpu.roll(df, 1, 0)).astype(BF16)

    for n in range(canv):
        total = None
        for side, which in ((0, chan), (1, 1 - chan)):
            e = e3[side, dx, n, pl.ds(pl.multiple_of((2 - dy) * CW, CW), PX)] * wide(gy[dy, n], reps)
            w = w_ref[0, :, pl.ds(pl.multiple_of(which * half, half), half)]
            part = dot_nt(e, w)
            total = part if total is None else total + part

        @pl.when(d == 0)
        def _():
            acc[n] = total

        @pl.when(d > 0)
        def _():
            acc[n] += total

    @pl.when(d == 8)
    def _():
        for n in range(canv):
            out_ref[n * PX : (n + 1) * PX] = acc[n].astype(BF16)


def branch_back_kernel(canv, boxes_unused, cells_ref, lanes_ref, own_ref, got_ref, lift_ref, w_ref, norm_ref, act_ref, da_ref, part_ref, acc):
    d = pl.program_id(0)
    half = own_ref.shape[0]
    chan = lax.axis_index("chan")

    @pl.when(d == 0)
    def _():
        acc[...] = jnp.zeros_like(acc)

    for ref, which in ((own_ref, chan), (got_ref, 1 - chan)):
        cells = [dot(ref[:, n * PX : (n + 1) * PX], lift_ref[n]).astype(BF16) for n in range(canv)]
        w = w_ref[0, :, :, pl.ds(pl.multiple_of(which * half, half), half)].reshape(acc.shape[0], half)
        acc[...] += dot(w, jnp.concatenate(cells, axis=1))

    @pl.when(d == 8)
    def _():
        width = norm_ref.shape[1]
        levels = jnp.concatenate([lanes_ref[4:5, :]] * canv, axis=1)
        dy = 0.0
        for level in range(4):
            dy = dy + jnp.where(levels == level, acc[level * width : (level + 1) * width], 0.0)
        dy = pltranspose(dy)
        act = act_ref[...]
        sig = jax.nn.sigmoid(act)
        da = dy * sig * (1.0 + act * (1.0 - sig))
        da_ref[...] = da
        for level in range(4):
            gain = bias = 0.0
            for n in range(canv):
                rows = slice(n * CELLS, (n + 1) * CELLS)
                mine = jnp.where(cells_ref[:, 4:5] == level, da[rows], 0.0)
                gain = gain + jnp.sum(mine * norm_ref[rows], 0, keepdims=True)
                bias = bias + jnp.sum(mine, 0, keepdims=True)
            part_ref[level : level + 1, :] = gain
            part_ref[4 + level : 5 + level, :] = bias


def branch_dz_kernel(canv, rows_all, each, cells_ref, da_ref, norm_ref, total_ref, sums_ref, gain_ref, dz_ref, pack_ref, send_a, send_b, flip):
    for n in range(canv):
        rows = slice(n * CELLS, (n + 1) * CELLS)
        dz = 0.0
        for level in range(4):
            _, rstd = branch_stat(total_ref, level, rows_all[level])
            here = jnp.where(cells_ref[:, 4:5] == level, 1.0, 0.0)
            mean_gain = sums_ref[level : level + 1, :] / rows_all[level]
            mean_bias = sums_ref[4 + level : 5 + level, :] / rows_all[level]
            mine = gain_ref[level : level + 1, :] * rstd * (da_ref[rows] - mean_bias - norm_ref[rows] * mean_gain)
            dz = dz + here * mine
        dz_ref[rows] = dz.astype(BF16)
        flip[:, rows] = pltranspose(dz)
    half = flip.shape[0]
    split_rows(flip, half // (4 * each), each, pack_ref.at[0 : half // 2], send_a, pack_ref.at[half // 2 : half], send_b)


def grad_x_kernel(canv, box_count, boxes_ref, lanes_ref, cells_ref, own_ref, got_ref, w_ref, dx_ref, out_ref, kept):
    n = pl.program_id(0)
    half = own_ref.shape[1]
    chan = lax.axis_index("chan")

    @pl.when(n == 0)
    def _():
        total = 0.0
        for level in range(4):
            for ref, which in ((own_ref, chan), (got_ref, 1 - chan)):
                mine = [
                    jnp.where(cells_ref[:, 4:5] == level, ref[m * CELLS : (m + 1) * CELLS].astype(F32), 0.0).astype(BF16)
                    for m in range(canv)
                ]
                w = w_ref[level, :, pl.ds(pl.multiple_of(which * half, half), half)]
                total = total + dot_nt(jnp.concatenate(mine, axis=0), w)
        for m in range(canv):
            top, left, height, width = by_box(boxes_ref, m, cells_ref[:, 0:1], box_count)
            r0, r1, c0, c1 = member_bounds(lambda row: cells_ref[:, row : row + 1], height, width)
            kept[m] = (total[m * CELLS : (m + 1) * CELLS] / ((r1 - r0) * (c1 - c0))).astype(BF16)

    select, _ = members(boxes_ref, n, box_count, lambda row: lanes_ref[row : row + 1, :], (PX, CELLS), 0)
    out_ref[...] = (dx_ref[...].astype(F32) + dot(select.astype(BF16), kept[n])).astype(BF16)


def put_rows(out, index, own_ref, other_ref, scale=None):
    chan = lax.axis_index("chan")
    size = own_ref.shape[0]
    for ref, which in ((own_ref, chan), (other_ref, 1 - chan)):
        value = ref[...] if scale is None else (ref[...].astype(F32) * scale).astype(BF16)
        out[index, pl.ds(pl.multiple_of(which * size, size), size), :] = value


def wgrad_kernel(
    canv, box_count, bit_of, boxes0, boxes1, cells_ref, own0, other0, own1, other1, x0, x1, keep_ref, send_ref, pooled_ref, acc, lhs, xd
):
    pixels = x0.shape[0]
    reps = x0.shape[1] // CELLS
    for source, (boxes_ref, own_ref, other_ref, x_ref) in enumerate(((boxes0, own0, other0, x0), (boxes1, own1, other1, x1))):
        down = []
        for n in range(canv):
            rows = slice(n * PX, (n + 1) * PX)
            into = slice(CW + n * PX, CW + (n + 1) * PX)
            gate = pixel_gates(boxes_ref, n, box_count, (PX, CELLS), 0)
            x = x_ref[rows].astype(F32)
            xd[0, into] = (wide(gate(0, -1), reps) * pltpu.roll(x, 1, 0)).astype(BF16)
            xd[1, into] = x_ref[rows]
            xd[2, into] = (wide(gate(0, 1), reps) * pltpu.roll(x, PX - 1, 0)).astype(BF16)
            across = pixel_gates(boxes_ref, n, box_count, (8, PX), 1)
            down.append([across(step, 0)[0:1, :] for step in (-1, 0, 1)])
        if source == 0:
            for step in range(3):
                xd[step, 0:CW] = jnp.zeros((CW, x0.shape[1]), BF16)
                xd[step, CW + pixels : 2 * CW + pixels] = jnp.zeros((CW, x0.shape[1]), BF16)
        else:
            for n in range(canv):
                select, count = members(
                    boxes_ref, n, box_count, lambda row: cells_ref[:, row : row + 1], (CELLS, PX), 1
                )
                sums = dot(select.astype(BF16), x_ref[n * PX : (n + 1) * PX])
                pooled_ref[n * CELLS : (n + 1) * CELLS] = (sums / count).astype(BF16)
        for step in range(3):
            put_rows(lhs, step, own_ref, other_ref, jnp.concatenate([found[step] for found in down], axis=1))

        def offset(d, carry):
            dy = d // 3
            part = dot(lhs[dy], xd[d % 3, pl.ds(pl.multiple_of(dy * CW, CW), pixels), :])
            if source == 0:
                acc[d] = part
            else:
                acc[d] += part
            return carry

        lax.fori_loop(0, 9, offset, 0)
    split_out(9, bit_of, acc, keep_ref, send_ref)


def split_out(count, bit_of, acc, keep_ref, send_ref):
    bit = (lax.axis_index("dp") // bit_of) % 2
    size = keep_ref.shape[2]

    def one(d, carry):
        for half in range(2):
            for ref, which in ((keep_ref, bit), (send_ref, 1 - bit)):
                ref[d, half] = acc[d, pl.ds(pl.multiple_of((half * 2 + which) * size, size), size), :].astype(BF16)
        return carry

    lax.fori_loop(0, count, one, 0)


def wgrad_fb_kernel(
    canv, cells_ref, own0, oth0, own1, oth1, own2, oth2, own3, oth3, lift0_ref, lift1_ref, y_ref, out_ref, ye, lhs
):
    d = pl.program_id(0)

    @pl.when(d == 0)
    def _():
        expand(y_ref[...], cells_ref, ye)
        me = lax.axis_index("dp")
        x_bit, y_bit = me % 2, (me // 2) % 2
        size = own3.shape[0]
        sources = ((own0, oth0, y_bit), (own1, oth1, y_bit), (own2, oth2, x_bit), (own3, oth3, 0))
        for source, (own_ref, oth_ref, bit) in enumerate(sources):
            mine = pl.ds(pl.multiple_of(bit * size, size), size)
            put_rows(lhs, source, own_ref.at[mine], oth_ref.at[mine])

    cells = []
    for n in range(PLANE * canv):
        lift = lift0_ref[n] if n < canv else lift1_ref[n - canv]
        grads = lhs[n // canv, :, (n % canv) * PX : (n % canv + 1) * PX]
        cells.append(dot(grads, lift).astype(BF16))
    result = dot(jnp.concatenate(cells, axis=1), ye[...])
    parts, _, each, _ = out_ref.shape
    for part in range(parts):
        out_ref[part, 0] = result[part * each : (part + 1) * each].astype(BF16)


def wgrad_br_kernel(canv, lanes_ref, own_ref, oth_ref, owna, otha, ownb, othb, pooled_ref, poola, poolb, keepa, senda, keepb, sendb, acc, lhs):
    levels = jnp.concatenate([lanes_ref[4:5, :]] * canv, axis=1)
    size = owna.shape[0]
    wide_by = poola.shape[1]
    sides = ((0, owna, otha, poola, keepa, senda, 2), (1, ownb, othb, poolb, keepb, sendb, 1))
    for side, own1, oth1, pool1, keep_ref, send_ref, bit_of in sides:
        mine = slice(side * size, (side + 1) * size)
        put_rows(lhs, 0, own_ref.at[mine], oth_ref.at[mine])
        put_rows(lhs, 1, own1, oth1)
        pool0 = pooled_ref[:, side * wide_by : (side + 1) * wide_by]
        for level in range(4):
            left = [jnp.where(levels == level, lhs[source].astype(F32), 0.0).astype(BF16) for source in range(2)]
            acc[level] = dot(left[0], pool0) + dot(left[1], pool1[...])
        split_out(4, bit_of, acc, keep_ref, send_ref)


def launch(kernel, in_specs, after=(), **rest):
    used = len(in_specs)
    extra = len(after)

    def body(*refs):
        kernel(*refs[:used], *refs[used + extra :])

    cost = pl.CostEstimate(flops=COST_UNIT * COSTS.get(rest["name"], 10), bytes_accessed=0, transcendentals=0)
    call = pl.pallas_call(body, cost_estimate=cost, in_specs=list(in_specs) + [ANY_SPEC] * extra, **rest)
    return lambda *operands: call(*operands, *after)


def whole(shape):
    return pl.BlockSpec(shape, lambda i: (0,) * len(shape))


def shaped(shape, kind):
    return jax.ShapeDtypeStruct(shape, kind)


def per_device(features, boxes, w_branch, gain_branch, bias_branch, w_fx, w_fb, gain_join, bias_join, w_cls, b_cls, grad_logits):
    canv, box_count = boxes.shape[:2]
    pixels, cin = features.shape
    mid = gain_join.shape[0]
    half = mid // lax.axis_size("chan")
    bw = gain_branch.shape[1]
    br = w_branch.shape[2]
    ncls = w_cls.shape[1]
    dp = lax.axis_size("dp")
    parts = dp // PLANE
    each = mid // dp
    cols = parts * each
    rows = canv * CELLS
    chan = lax.axis_index("chan")
    me = lax.axis_index("dp")
    rows_all = [float(canv * dp * box_count * s * s) for s in BINS]
    lanes_np = cell_table(box_count)
    lanes = jnp.asarray(lanes_np)
    cells = jnp.asarray(np.concatenate([lanes_np.T, np.zeros((CELLS, CELLS - 8), np.float32)], 1))

    def to_mate(array, mate):
        return lax.ppermute(array, "dp", [(i, i ^ mate) for i in range(dp)])

    def swap(array):
        return lax.ppermute(array, "chan", [(0, 1), (1, 0)])

    def to_part(array, step):
        return lax.ppermute(array, "dp", [(i, ((i // PLANE + step) % parts) * PLANE + i % PLANE) for i in range(dp)])

    flat = boxes.reshape(-1)
    flat_of = [flat] + [to_mate(flat, m) for m in (1, 2, 3)]
    flat_mates = jnp.concatenate(flat_of[1:])

    pooled, lifts, z_own, z_send, x_first, x_last = launch(
        functools.partial(pool_kernel, canv, box_count),
        grid=(canv,),
        in_specs=[
            SMEM_SPEC,
            whole(lanes.shape),
            whole(cells.shape),
            pl.BlockSpec((PX, cin), lambda i: (i, 0)),
            whole(w_branch.shape),
        ],
        out_specs=[
            pl.BlockSpec((CELLS, cin), lambda i: (i, 0)),
            pl.BlockSpec((1, PX, 9 * CELLS), lambda i: (i, 0, 0)),
            whole((rows, bw)),
            whole((rows, bw)),
            pl.BlockSpec((PX, cin // 2), lambda i: (i, 0)),
            pl.BlockSpec((PX, cin // 2), lambda i: (i, 0)),
        ],
        out_shape=[
            shaped((rows, cin), BF16),
            shaped((canv, PX, 9 * CELLS), BF16),
            shaped((rows, bw), F32),
            shaped((rows, bw), BF16),
            shaped((pixels, cin // 2), BF16),
            shaped((pixels, cin // 2), BF16),
        ],
        scratch_shapes=[pltpu.VMEM((rows, cin), BF16), pltpu.VMEM((rows, br), F32)],
        compiler_params=params(),
        name="pool",
    )(flat, lanes, cells, features, w_branch)
    z_got = swap(z_send)
    z, z_part = launch(
        functools.partial(branch_sums_kernel, canv),
        in_specs=[VMEM_SPEC] * 3,
        out_specs=[VMEM_SPEC] * 2,
        out_shape=[shaped((rows, bw), F32), shaped((8, bw), F32)],
        compiler_params=params(),
        name="branch_sums",
    )(cells, z_own, z_got)
    z_total = dp_sum(z_part, dp, 0)
    y, z_norm, z_act = launch(
        functools.partial(branch_act_kernel, canv, rows_all),
        in_specs=[VMEM_SPEC] * 5,
        out_specs=[VMEM_SPEC] * 3,
        out_shape=[shaped((rows, bw), BF16), shaped((rows, bw), F32), shaped((rows, bw), F32)],
        compiler_params=params(),
        name="branch_act",
    )(cells, z, z_total, gain_branch, bias_branch)
    x_mate = to_mate(x_first, 1)
    y_mate = to_mate(x_last, 2)
    y_all = jnp.concatenate([y] + [to_mate(y, m) for m in (1, 2, 3)], 0)

    f_own, f_send = launch(
        functools.partial(join_kernel, canv, box_count),
        grid=(9,),
        in_specs=[
            SMEM_SPEC,
            whole(cells.shape),
            whole((pixels, cin)),
            whole((rows, bw)),
            pl.BlockSpec((canv, PX, CELLS), lambda i: (0, 0, i)),
            pl.BlockSpec((1, cin, mid), lambda i: (i, 0, 0)),
            pl.BlockSpec((1, 4, bw, mid), lambda i: (i, 0, 0, 0)),
        ],
        out_specs=[whole((pixels, half)), whole((pixels, half))],
        out_shape=[shaped((pixels, half), F32), shaped((pixels, half), BF16)],
        scratch_shapes=[
            pltpu.VMEM((3, canv, PX, mid), F32),
            pltpu.VMEM((3, canv, PX, CELLS), F32),
            pltpu.VMEM((canv, PX + 2 * CW, mid), F32),
            pltpu.VMEM((rows, 4 * bw), BF16),
        ],
        compiler_params=params(),
        name="join",
    )(flat, cells, features, y, lifts, w_fx, w_fb)
    f_got = swap(f_send)
    by_canvas = pl.BlockSpec((PX, half), lambda i: (i, 0))
    f, f_part = launch(
        functools.partial(join_sums_kernel, canv, box_count),
        grid=(canv,),
        in_specs=[SMEM_SPEC, by_canvas, by_canvas],
        out_specs=[by_canvas, whole((8, half))],
        out_shape=[shaped((pixels, half), F32), shaped((8, half), F32)],
        compiler_params=params(),
        name="join_sums",
        after=(x_mate, y_mate, y_all),
    )(flat, f_own, f_got)
    f_total = dp_sum(f_part, dp, 1)
    gain_row = gain_join.reshape(1, mid)
    bias_row = bias_join.reshape(1, mid)
    score, db, db_part, dw_cls = launch(
        functools.partial(head_kernel, box_count),
        grid=(canv,),
        in_specs=[
            SMEM_SPEC,
            by_canvas,
            whole((8, half)),
            whole((1, mid)),
            whole((1, mid)),
            whole((mid, ncls)),
            pl.BlockSpec((PX, ncls), lambda i: (i, 0)),
        ],
        out_specs=[pl.BlockSpec((PX, ncls), lambda i: (i, 0)), by_canvas, whole((8, half)), whole((half, ncls))],
        out_shape=[
            shaped((pixels, ncls), BF16),
            shaped((pixels, half), F32),
            shaped((8, half), F32),
            shaped((half, ncls), F32),
        ],
        compiler_params=params(),
        name="head",
    )(flat, f, f_total, gain_row, bias_row, w_cls, grad_logits)
    db_total = dp_sum(db_part, dp, 2)
    logits = (score.astype(F32) + swap(score).astype(F32) + b_cls).astype(BF16)
    quarter = half // 2
    df, pack, send_a, send_b, send_d = launch(
        functools.partial(join_grad_kernel, box_count, each),
        grid=(canv,),
        in_specs=[SMEM_SPEC, by_canvas, by_canvas, whole((8, half)), whole((8, half)), whole((1, mid))],
        out_specs=[by_canvas]
        + [pl.BlockSpec((size, PX), lambda i: (0, i)) for size in (2 * half, quarter, quarter, quarter // 2)],
        out_shape=[shaped((pixels, half), BF16)]
        + [shaped((size, pixels), BF16) for size in (2 * half, quarter, quarter, quarter // 2)],
        scratch_shapes=[pltpu.VMEM((half, PX), F32)],
        compiler_params=params(),
        name="join_grad",
    )(flat, f, db, f_total, db_total, gain_row)
    got_a, got_b, got_d = to_mate(send_a, 1), to_mate(send_b, 2), to_mate(send_d, 3)
    pack_other = swap(pack)
    df_got = swap(df)
    other_a, other_b, other_d = swap(got_a), swap(got_b), swap(got_d)
    half_rows = pl.BlockSpec((half, pixels), lambda i: (0, 0))

    da, da_part = launch(
        functools.partial(branch_back_kernel, canv),
        grid=(9,),
        in_specs=[
            SMEM_SPEC,
            whole(cells.shape),
            whole(lanes.shape),
            half_rows,
            half_rows,
            pl.BlockSpec((canv, PX, CELLS), lambda i: (0, 0, i)),
            pl.BlockSpec((1, 4, bw, mid), lambda i: (i, 0, 0, 0)),
            whole((rows, bw)),
            whole((rows, bw)),
        ],
        out_specs=[whole((rows, bw)), whole((8, bw))],
        out_shape=[shaped((rows, bw), F32), shaped((8, bw), F32)],
        scratch_shapes=[pltpu.VMEM((4 * bw, rows), F32)],
        compiler_params=params(),
        name="branch_back",
    )(flat, cells, lanes, pack, pack_other, lifts, w_fb, z_norm, z_act)
    da_total = dp_sum(da_part, dp, 3, (other_a, other_b, other_d))
    dz, zpack, zsend_a, zsend_b = launch(
        functools.partial(branch_dz_kernel, canv, rows_all, each),
        in_specs=[VMEM_SPEC] * 6,
        out_specs=[VMEM_SPEC] * 4,
        out_shape=[
            shaped((rows, bw), BF16),
            shaped((bw, rows), BF16),
            shaped((quarter, rows), BF16),
            shaped((quarter, rows), BF16),
        ],
        scratch_shapes=[pltpu.VMEM((bw, rows), F32)],
        compiler_params=params(),
        name="branch_dz",
    )(cells, da, z_norm, z_total, da_total, gain_branch)
    zgot_a, zgot_b = to_mate(zsend_a, 1), to_mate(zsend_b, 2)
    dz_got, zpack_other, zother_a, zother_b = swap(dz), swap(zpack), swap(zgot_a), swap(zgot_b)

    steps = PLANE * canv
    lifts_mates = launch(
        functools.partial(lifts_kernel, box_count),
        grid=(steps - canv,),
        in_specs=[SMEM_SPEC, whole(lanes.shape)],
        out_specs=pl.BlockSpec((1, PX, 9 * CELLS), lambda i: (i, 0, 0)),
        out_shape=shaped((steps - canv, PX, 9 * CELLS), BF16),
        compiler_params=params(),
        name="lifts",
    )(flat_mates, lanes)
    quarter_at = [pl.BlockSpec((quarter, pixels), lambda i, at=at: (at, 0)) for at in (2, 0, 0)]
    fb_parts = launch(
        functools.partial(wgrad_fb_kernel, canv),
        grid=(9,),
        in_specs=[
            whole(cells.shape),
            quarter_at[0],
            quarter_at[0],
            quarter_at[1],
            quarter_at[1],
            quarter_at[2],
            quarter_at[2],
            whole((quarter // 2, pixels)),
            whole((quarter // 2, pixels)),
            pl.BlockSpec((canv, PX, CELLS), lambda i: (0, 0, i)),
            pl.BlockSpec((steps - canv, PX, CELLS), lambda i: (0, 0, i)),
            whole((steps * CELLS, bw)),
        ],
        out_specs=pl.BlockSpec((parts, 1, each, 4 * bw), lambda i: (0, i, 0, 0)),
        out_shape=shaped((parts, 9, each, 4 * bw), BF16),
        scratch_shapes=[pltpu.VMEM((steps * CELLS, 4 * bw), BF16), pltpu.VMEM((PLANE, cols, pixels), BF16)],
        compiler_params=params(),
        name="wgrad_fb",
        after=(da_total,),
    )(cells, pack, pack_other, got_a, other_a, got_b, other_b, got_d, other_d, lifts, lifts_mates, y_all)

    span = cin // 2

    def wgrad(side, bit_of, boxes_mate, got, other, x_got, after):
        own = pl.BlockSpec((quarter, pixels), lambda i: (2 + side, 0))
        return launch(
            functools.partial(wgrad_kernel, canv, box_count, bit_of),
            grid=(1,),
            in_specs=[
                SMEM_SPEC,
                SMEM_SPEC,
                whole(cells.shape),
                own,
                own,
                whole((quarter, pixels)),
                whole((quarter, pixels)),
                pl.BlockSpec((pixels, span), lambda i: (0, side)),
                whole((pixels, span)),
            ],
            out_specs=[whole((9, 2, quarter // 2, span))] * 2 + [whole((rows, span))],
            out_shape=[shaped((9, 2, quarter // 2, span), BF16)] * 2 + [shaped((rows, span), BF16)],
            scratch_shapes=[
                pltpu.VMEM((9, half, span), F32),
                pltpu.VMEM((3, half, pixels), BF16),
                pltpu.VMEM((3, pixels + 2 * CW, span), BF16),
            ],
            compiler_params=params(),
            name="wgrad_fx%d" % side,
            after=after,
        )(flat, boxes_mate, cells, pack, pack_other, got, other, features, x_got)

    keep_fa, send_fa, pool_a = wgrad(0, 2, flat_of[1], got_a, other_a, x_mate, (fb_parts,))
    keep_fb, send_fb, pool_b = wgrad(1, 1, flat_of[2], got_b, other_b, y_mate, (send_fa,))
    quarter_shape = (4, 2, quarter // 2, span)
    keep_ba, send_ba, keep_bb, send_bb = launch(
        functools.partial(wgrad_br_kernel, canv),
        in_specs=[VMEM_SPEC] * 10,
        out_specs=[VMEM_SPEC] * 4,
        out_shape=[shaped(quarter_shape, BF16)] * 4,
        scratch_shapes=[pltpu.VMEM((4, half, span), F32), pltpu.VMEM((2, half, rows), BF16)],
        compiler_params=params(),
        name="wgrad_br",
    )(lanes, zpack, zpack_other, zgot_a, zother_a, zgot_b, zother_b, pooled, pool_a, pool_b)

    def across_groups(pick):
        group = me // PLANE
        total = pick(group)
        for step in range(1, parts):
            total = total + to_part(pick((group + step) % parts).astype(BF16), step).astype(F32)
        return total

    def through_mate(keep, send, mate):
        got = to_mate(send, mate)
        shape = (keep.shape[0], parts, each, span)

        def pick(part):
            mine = [lax.dynamic_index_in_dim(a.reshape(shape), part, 1, keepdims=False) for a in (keep, got)]
            return mine[0].astype(F32) + mine[1].astype(F32)

        return across_groups(pick)

    sum_fb = across_groups(lambda part: lax.dynamic_index_in_dim(fb_parts, part, 0, keepdims=False).astype(F32))
    out_fb = jnp.transpose(sum_fb.reshape(9, each, 4, bw), (0, 2, 3, 1))
    out_fx = [through_mate(keep_fa, send_fa, 2), through_mate(keep_fb, send_fb, 1)]
    out_fx = jnp.transpose(jnp.concatenate(out_fx, 2), (0, 2, 1))
    out_br = [through_mate(keep_ba, send_ba, 2), through_mate(keep_bb, send_bb, 1)]
    out_br = jnp.transpose(jnp.concatenate(out_br, 2), (0, 2, 1))

    dx = launch(
        functools.partial(dx_kernel, canv, box_count),
        grid=(9,),
        in_specs=[
            SMEM_SPEC,
            whole((pixels, half)),
            whole((pixels, half)),
            pl.BlockSpec((1, cin, mid), lambda i: (i, 0, 0)),
        ],
        out_specs=whole((pixels, cin)),
        out_shape=shaped((pixels, cin), BF16),
        scratch_shapes=[
            pltpu.VMEM((canv, PX, cin), F32),
            pltpu.VMEM((3, canv, PX, CELLS), BF16),
            pltpu.VMEM((2, 3, canv, PX + 2 * CW, half), BF16),
        ],
        compiler_params=params(),
        name="dx",
        after=(send_bb,),
    )(flat, df, df_got, w_fx)
    grad_features = launch(
        functools.partial(grad_x_kernel, canv, box_count),
        grid=(canv,),
        in_specs=[
            SMEM_SPEC,
            whole(lanes.shape),
            whole(cells.shape),
            whole((rows, bw)),
            whole((rows, bw)),
            whole(w_branch.shape),
            pl.BlockSpec((PX, cin), lambda i: (i, 0)),
        ],
        out_specs=pl.BlockSpec((PX, cin), lambda i: (i, 0)),
        out_shape=shaped((pixels, cin), BF16),
        scratch_shapes=[pltpu.VMEM((canv, CELLS, cin), BF16)],
        compiler_params=params(),
        name="grad_x",
    )(flat, lanes, cells, dz, dz_got, w_branch, dx)

    small = db_total[:2]
    small_got = swap(small)
    small_all = jnp.concatenate([jnp.where(chan == 0, small, small_got), jnp.where(chan == 0, small_got, small)], 1)
    placed = jnp.zeros((mid, ncls), F32)
    grad_w_cls = lax.psum(lax.dynamic_update_slice_in_dim(placed, dw_cls, chan * half, 0), ("dp", "chan"))
    return (
        logits,
        grad_features,
        out_br,
        da_total[:4],
        da_total[4:],
        out_fx,
        out_fb,
        small_all[0],
        small_all[1],
        grad_w_cls,
        db_total[2, :ncls],
    )


def solution(mesh):
    return jax.shard_map(
        per_device,
        mesh=mesh,
        in_specs=(
            P("dp", "chan"),
            P("dp", None, None),
            P(None, "chan", None),
            P(None, "chan"),
            P(None, "chan"),
            P(None, "chan", None),
            P(None, None, "chan", None),
            P(),
            P(),
            P(),
            P(),
            P("dp", None),
        ),
        out_specs=(
            P("dp", None),
            P("dp", "chan"),
            P(None, "chan", "dp"),
            P(None, "chan"),
            P(None, "chan"),
            P(None, "chan", "dp"),
            P(None, None, "chan", "dp"),
            P(),
            P(),
            P(),
            P(),
        ),
        check_vma=False,
    )
```

time: 2390 us -> 455 us (0.19)
  waiting for transfers between devices: 1550 us -> 88.6 us
  matrix products: 380 us -> 0 us
  Pallas kernels: 0 us -> 275 us
  local copies, waits for them, and re-layouts: 197 us -> 12.8 us
  blocking collectives: 160 us -> 0 us
  other arithmetic: 74.4 us -> 9.12 us
  starting transfers between devices: 0.67 us -> 48.9 us
    reduce_scatter x7 -> x0, waiting for transfers between devices: 1380 us -> none  [the longest x1 688 us: per_device(): lax.psum_scatter(grad_fx_local, 'dp', scatter_dimension=2, tiled=True)]
    dot_general x134 -> x0, matrix products: 380 us -> none  [the longest x36 152 us: per_device(): jnp.einsum('npc,ncm->npm', lifts[level], cell_term, precision=HIGH)]
    pallas_call x0 -> x20, Pallas kernels: none -> 275 us  [launch(): return lambda *operands: call(*operands, *after)]
    psum x4 -> x0, blocking collectives: 152 us -> none  [the longest x1 40.4 us: per_device(): lax.psum((part_first, part_second, count_own), ('dp', 'chan'))]
    psum x2 -> x1, waiting for transfers between devices: 137 us -> 0.01 us  [per_device(): lax.psum(lax.dynamic_update_slice_in_dim(placed, dw_cls, chan * half, 0),...]
    ppermute x0 -> x45, waiting for transfers between devices: none -> 88.6 us  [the longest x15 45.5 us: to_part(): lax.ppermute(array, 'dp', [(i, (i // PLANE + step) % parts * PLANE + i %...]
    another operation x55 -> x0, local copies, waits for them, and re-layouts: 69.4 us -> none  [the longest x1 30.2 us: per_device(): grad_fx_local = jnp.stack(dwx_list)]
    slice x32 -> x3, local copies, waits for them, and re-layouts: 52 us -> 1.21 us  [the longest x1 0.61 us: per_device(): db_total[2, :ncls]]
  transfers between devices with their start and end apart: 11 -> 46, of which waited for: 6 -> 17; matrix products, arithmetic and copies ran while one was open for 16% -> 3% of each run, Pallas kernels for 0% -> 51%
where the time goes in v1:
time: 455 us; the launch traced here: 450 us
  Pallas kernels  275 us (60%)
  waiting for transfers between devices  88.6 us (19%)
  starting transfers between devices  48.9 us (11%)
  between operations  15 us (3%)
  local copies, waits for them, and re-layouts  12.8 us (3%)
  other arithmetic  9.12 us (2%)
    pallas_call x20, Pallas kernels, launch(): return lambda *operands: call(*operands, *after)  275 us
    ppermute x15, waiting for transfers between devices, to_part(): lax.ppermute(array, 'dp', [(i, (i // PLANE + step) % parts * PLANE + i %...  45.5 us
    ppermute x17, waiting for transfers between devices, to_mate(): return lax.ppermute(array, 'dp', [(i, i ^ mate) for i in range(dp)])  42.8 us
    ppermute x15, starting transfers between devices, to_part(): lax.ppermute(array, 'dp', [(i, (i // PLANE + step) % parts * PLANE + i %...  25.3 us
    ppermute x17, starting transfers between devices, to_mate(): return lax.ppermute(array, 'dp', [(i, i ^ mate) for i in range(dp)])  21 us
  transfers between devices with their start and end apart: 46, of which 17 were waited for; matrix products, arithmetic and copies ran while one was open for 3% of the time, Pallas kernels for 51%

profile of v1, /device:TPU:8, one launch (start us, length us, event | category | flops | bytes accessed | tf_op | source)
XLA Modules:
  0.0 449.9 jit_solution(11717779699807179766)
XLA Ops:
  7.2 1.3 reshape.145.refs_0_
  8.6 12.4 %pool.1 = (bf16[384,1024]{1,0:T(8,128)(2,1)}, bf16[3,512,1152]{2,1,0:T(8,128)(2,1)}, f32[384,256]{1,0:T(8,128)}, bf16[384,256]{1,0:T(8,128)(2,1)}, bf16[1536,512]{1,0:T(8,128)(2,1)}, /*index=5*/bf16[1536,512]{1,0:T(8,128)(2,1)}) custom-call(s32[24]{0:T(128)} %reshape.145.refs_0_, f32[8,128]{1,0:T(8,128)} %constant.166.clone.refs_1_.refs_2_.refs_0_, ...), custom_call_target="tpu_custom_call" | custom-call | flops 12000000000 | tf_op jit(solution)/shard_map/pool/pallas_call | solution.py:685
  20.9 1.6 collective-permute-start.2
  22.5 1.5 collective-permute-start.3
  24.7 2.0 branch_sums.1
  26.7 34.8 %dp_sum0.1.refs_2_.refs_3_ = f32[8,256]{1,0:T(8,128)} custom-call(f32[8,256]{1,0:T(8,128)} %get-tuple-element.54.refs_0_), custom_call_target="tpu_custom_call" | custom-call | flops 10000000000 | tf_op jit(solution)/shard_map/dp_sum0/pallas_call | solution.py:685
  61.5 2.5 branch_act.1
  64.0 41.7 %join.1 = (f32[1536,256]{1,0:T(8,128)}, bf16[1536,256]{1,0:T(8,128)(2,1)}) custom-call(s32[24]{0:T(128)} %reshape.145.refs_0_, f32[128,128]{1,0:T(8,128)} %constant.167.clone.refs_2_.refs_0_.refs_1_, bf16[1536,1024]{1,0:T(8,128)(2,1)} %refs_7_.3, bf16[384,256]{1,0:T(8,128)(2,1)} %get-tuple-element.55.refs_3_, ...), custom_call_target="tpu_custom_call" | custom-call | flops 41999998976 | tf_op jit(solution)/shard_map/join/pallas_call | solution.py:685
  105.8 1.3 collective-permute-start.22
  108.1 1.2 copy.63.refs_6_
  110.1 1.3 collective-permute-start.24
  111.5 1.3 collective-permute-start.4
  112.7 1.8 collective-permute-done.24
  115.1 1.1 collective-permute-start.5
  116.3 1.7 collective-permute-done.4
  117.9 1.6 collective-permute-start.6
  119.5 5.5 %collective-permute-done.5 = bf16[384,256]{1,0:T(8,128)(2,1)S(1)} collective-permute-done((bf16[384,256]{1,0:T(8,128)(2,1)S(1)}, bf16[384,256]{1,0:T(8,128)(2,1)S(1)}, u32[]{:S(2)}, u32[]{:S(2)}) %collective-permute-start.5) | collective-permute-done | bytes 196640 | tf_op jit(solution)/shard_map/ppermute | solution.py:717
  126.7 3.9 join_sums.1
  130.7 9.5 %dp_sum1.1.refs_2_.refs_3_ = f32[8,256]{1,0:T(8,128)} custom-call(f32[8,256]{1,0:T(8,128)} %get-tuple-element.62.refs_0_), custom_call_target="tpu_custom_call" | custom-call | flops 10000000000 | tf_op jit(solution)/shard_map/dp_sum1/pallas_call | solution.py:685
  140.2 4.9 %head.1 = (bf16[1536,150]{1,0:T(8,128)(2,1)}, f32[1536,256]{1,0:T(8,128)}, f32[8,256]{1,0:T(8,128)}, f32[256,150]{1,0:T(8,128)}) custom-call(s32[24]{0:T(128)} %reshape.145.refs_0_, f32[1536,256]{1,0:T(8,128)} %get-tuple-element.61.refs_1_, f32[8,256]{1,0:T(8,128)} %dp_sum1.1.refs_2_.refs_3_, f32[1,512]{1,0:T(1,128)} %bitcast.163, f32[1,512]{1,0:T(1,128)} %bitcast.162, ...), custom_call_target="tpu_custom_call" | custom-call | flops 5000000000 | tf_op jit(solution)/shard_map/head/pallas_call | solution.py:685
  145.0 9.7 %dp_sum2.1.refs_4_ = f32[8,256]{1,0:T(8,128)} custom-call(f32[8,256]{1,0:T(8,128)} %get-tuple-element.65.refs_0_), custom_call_target="tpu_custom_call" | custom-call | flops 10000000000 | tf_op jit(solution)/shard_map/dp_sum2/pallas_call | solution.py:685
  154.7 5.1 %join_grad.1 = (bf16[1536,256]{1,0:T(8,128)(2,1)}, bf16[512,1536]{1,0:T(8,128)(2,1)}, bf16[128,1536]{1,0:T(8,128)(2,1)}, bf16[128,1536]{1,0:T(8,128)(2,1)}, bf16[64,1536]{1,0:T(8,128)(2,1)}) custom-call(s32[24]{0:T(128)} %reshape.145.refs_0_, f32[1536,256]{1,0:T(8,128)} %get-tuple-element.61.refs_1_, f32[1536,256]{1,0:T(8,128)} %get-tuple-element.64.refs_2_, ...), custom_call_target="tpu_custom_call" | custom-call | flops 5000000000 | tf_op jit(solution)/shard_map/join_grad/pallas_call | solution.py:685
  160.7 10.4 %lifts.1.refs_10_ = bf16[9,512,1152]{2,1,0:T(8,128)(2,1)} custom-call(s32[72]{0:T(128)} %pad_add_fusion.refs_0_, f32[8,128]{1,0:T(8,128)} %constant.166.clone.refs_1_.refs_2_.refs_0_), custom_call_target="tpu_custom_call" | custom-call | flops 10000000000 | tf_op jit(solution)/shard_map/lifts/pallas_call | solution.py:685
  171.3 1.5 collective-permute-start.9
  174.6 1.2 collective-permute-start.13
  176.4 12.0 %collective-permute-done.13.refs_7_ = bf16[64,1536]{1,0:T(8,128)(2,1)S(1)} collective-permute-done((bf16[64,1536]{1,0:T(8,128)(2,1)S(1)}, bf16[64,1536]{1,0:T(8,128)(2,1)S(1)}, u32[]{:S(2)}, u32[]{:S(2)}) %collective-permute-start.13) | collective-permute-done | bytes 196640 | tf_op jit(solution)/shard_map/ppermute | solution.py:717
  190.1 1.0 copy.100
  191.1 16.0 %branch_back.1 = (f32[384,256]{1,0:T(8,128)}, f32[8,256]{1,0:T(8,128)}) custom-call(s32[24]{0:T(128)} %reshape.145.refs_0_, f32[128,128]{1,0:T(8,128)} %constant.167.clone.refs_2_.refs_0_.refs_1_, f32[8,128]{1,0:T(8,128)} %constant.166.clone.refs_1_.refs_2_.refs_0_, bf16[512,1536]{1,0:T(8,128)(2,1)} %get-tuple-element.66.refs_3_.refs_1_, ...), custom_call_target="tpu_custom_call" | custom-call | flops 16000000000 | tf_op jit(solution)/shard_map/branch_back/pallas_call | solution.py:685
  207.1 10.2 %dp_sum3.1.refs_4_.refs_12_ = f32[8,256]{1,0:T(8,128)} custom-call(f32[8,256]{1,0:T(8,128)} %get-tuple-element.70.refs_0_, bf16[128,1536]{1,0:T(8,128)(2,1)} %collective-permute-done.10.refs_1_.refs_4_.refs_6_, bf16[128,1536]{1,0:T(8,128)(2,1)} %collective-permute-done.12.refs_2_.refs_6_, bf16[64,1536]{1,0:T(8,128)(2,1)} %collective-permute-done.14.refs_3_.refs_8_), custom_call_target="tpu_custom_call" | custom-call | flops 10000000000 | tf_op jit(solution)/shard_map/dp_sum3/pallas_call | solution.py:685
  217.2 15.3 %wgrad_fb.1.refs_9_ = bf16[4,9,32,1024]{3,2,1,0:T(8,128)(2,1)} custom-call(f32[128,128]{1,0:T(8,128)} %constant.167.clone.refs_2_.refs_0_.refs_1_, bf16[512,1536]{1,0:T(8,128)(2,1)} %get-tuple-element.66.refs_3_.refs_1_, bf16[512,1536]{1,0:T(8,128)(2,1)} %collective-permute-done.8.refs_4_.refs_2_, bf16[128,1536]{1,0:T(8,128)(2,1)} %copy-done.21, ...), custom_call_target="tpu_custom_call" | custom-call | flops 15000000512 | tf_op jit(solution)/shard_map/wgrad_fb/pallas_call | solution.py:685
  232.5 23.7 %wgrad_fx0.1 = (bf16[9,2,64,512]{3,2,1,0:T(8,128)(2,1)}, bf16[9,2,64,512]{3,2,1,0:T(8,128)(2,1)}, bf16[384,512]{1,0:T(8,128)(2,1)}) custom-call(s32[24]{0:T(128)} %reshape.145.refs_0_, s32[24]{0:T(128)} %copy-done.17, f32[128,128]{1,0:T(8,128)} %constant.167.clone.refs_2_.refs_0_.refs_1_, bf16[512,1536]{1,0:T(8,128)(2,1)} %get-tuple-element.66.refs_3_.refs_1_, ...), custom_call_target="tpu_custom_call" | custom-call | flops 24000000000 | tf_op jit(solution)/shard_map/wgrad_fx0/pallas_call | solution.py:685
  256.1 1.2 collective-permute-start.33
  257.3 2.5 branch_dz.1
  259.8 1.3 collective-permute-start.18
  261.9 23.8 %wgrad_fx1.1 = (bf16[9,2,64,512]{3,2,1,0:T(8,128)(2,1)}, bf16[9,2,64,512]{3,2,1,0:T(8,128)(2,1)}, bf16[384,512]{1,0:T(8,128)(2,1)}) custom-call(s32[24]{0:T(128)} %reshape.145.refs_0_, s32[24]{0:T(128)} %copy-done.16, f32[128,128]{1,0:T(8,128)} %constant.167.clone.refs_2_.refs_0_.refs_1_, bf16[512,1536]{1,0:T(8,128)(2,1)} %get-tuple-element.66.refs_3_.refs_1_, ...), custom_call_target="tpu_custom_call" | custom-call | flops 24000000000 | tf_op jit(solution)/shard_map/wgrad_fx1/pallas_call | solution.py:685
  287.8 1.4 collective-permute-start.41
  289.2 1.7 collective-permute-start.42
  291.6 6.0 %wgrad_br.1 = (bf16[4,2,64,512]{3,2,1,0:T(8,128)(2,1)}, bf16[4,2,64,512]{3,2,1,0:T(8,128)(2,1)}, bf16[4,2,64,512]{3,2,1,0:T(8,128)(2,1)}, bf16[4,2,64,512]{3,2,1,0:T(8,128)(2,1)}) custom-call(f32[8,128]{1,0:T(8,128)} %constant.166.clone.refs_1_.refs_2_.refs_0_, bf16[256,384]{1,0:T(8,128)(2,1)} %get-tuple-element.76.refs_1_, bf16[256,384]{1,0:T(8,128)(2,1)} %copy-done.25, ...), custom_call_target="tpu_custom_call" | custom-call | flops 6000000000 | tf_op jit(solution)/shard_map/wgrad_br/pallas_call | solution.py:685
  297.6 1.5 collective-permute-start.25
  299.1 32.7 %dx.1.refs_6_ = bf16[1536,1024]{1,0:T(8,128)(2,1)} custom-call(s32[24]{0:T(128)} %reshape.145.refs_0_, bf16[1536,256]{1,0:T(8,128)(2,1)} %get-tuple-element.75.refs_1_, bf16[1536,256]{1,0:T(8,128)(2,1)} %collective-permute-done.16.refs_2_, bf16[9,1024,512]{2,1,0:T(8,128)(2,1)} %refs_3_.5, bf16[4,2,64,512]{3,2,1,0:T(8,128)(2,1)} %get-tuple-element.83.refs_4_), custom_call_target="tpu_custom_call" | custom-call | flops 32999999488 | tf_op jit(solution)/shard_map/dx/pallas_call | solution.py:685
  331.8 1.3 collective-permute-start.43
  334.0 1.3 collective-permute-start.29
  335.3 8.4 %grad_x.1 = bf16[1536,1024]{1,0:T(8,128)(2,1)} custom-call(s32[24]{0:T(128)} %reshape.145.refs_0_, f32[8,128]{1,0:T(8,128)} %constant.166.clone.refs_1_.refs_2_.refs_0_, f32[128,128]{1,0:T(8,128)} %constant.167.clone.refs_2_.refs_0_.refs_1_, bf16[384,256]{1,0:T(8,128)(2,1)} %get-tuple-element.74.refs_3_, bf16[384,256]{1,0:T(8,128)(2,1)} %copy-done.26, ...), custom_call_target="tpu_custom_call" | custom-call | flops 8999999488 | tf_op jit(solution)/shard_map/grad_x/pallas_call | solution.py:685
  343.7 1.1 fusion.16
  346.6 3.5 collective-permute-start.27
  350.1 21.8 %collective-permute-done.29 = bf16[4,2,64,512]{3,2,1,0:T(8,128)(2,1)} collective-permute-done((bf16[4,2,64,512]{3,2,1,0:T(8,128)(2,1)}, bf16[4,2,64,512]{3,2,1,0:T(8,128)(2,1)}, u32[]{:S(2)}, u32[]{:S(2)}) %collective-permute-start.29) | collective-permute-done | bytes 524320 | tf_op jit(solution)/shard_map/ppermute | solution.py:717
  371.9 1.1 collective-permute-start.28
  373.4 1.1 copy.135
  374.6 1.2 fusion.19
  376.8 2.3 collective-permute-start.31
  379.1 1.0 fusion.15
  380.4 2.1 collective-permute-start.34
  382.5 1.6 collective-permute-done.30
  384.9 3.8 collective-permute-done.31
  388.7 9.1 %collective-permute-start.36 = (bf16[9,32,512]{2,1,0:T(8,128)(2,1)S(1)}, bf16[9,32,512]{2,1,0:T(8,128)(2,1)S(1)}, u32[]{:S(2)}, u32[]{:S(2)}) collective-permute-start(bf16[9,32,512]{2,1,0:T(8,128)(2,1)S(1)} %get-tuple-element.118), channel_id=1, source_target_pairs={{0,24},{2,26},{4,28},{6,30},{8,0},{10,2},{12,4},{14,6},{16,8},{18,... | collective-permute-start | bytes 884744 | tf_op jit(solution)/shard_map/ppermute | solution.py:723
  397.9 4.0 collective-permute-done.32
  401.9 1.0 fusion.13
  403.4 4.1 collective-permute-done.34
  408.3 18.1 %collective-permute-done.35 = bf16[9,32,512]{2,1,0:T(8,128)(2,1)S(1)} collective-permute-done((bf16[9,32,512]{2,1,0:T(8,128)(2,1)S(1)}, bf16[9,32,512]{2,1,0:T(8,128)(2,1)S(1)}, u32[]{:S(2)}, u32[]{:S(2)}) %collective-permute-start.35) | collective-permute-done | bytes 294944 | tf_op jit(solution)/shard_map/ppermute | solution.py:723
  427.4 5.4 %collective-permute-done.38 = bf16[9,32,512]{2,1,0:T(8,128)(2,1)S(1)} collective-permute-done((bf16[9,32,512]{2,1,0:T(8,128)(2,1)S(1)}, bf16[9,32,512]{2,1,0:T(8,128)(2,1)S(1)}, u32[]{:S(2)}, u32[]{:S(2)}) %collective-permute-start.38) | collective-permute-done | bytes 294944 | tf_op jit(solution)/shard_map/ppermute | solution.py:723
  432.8 4.8 %collective-permute-done.39 = bf16[9,32,512]{2,1,0:T(8,128)(2,1)S(1)} collective-permute-done((bf16[9,32,512]{2,1,0:T(8,128)(2,1)S(1)}, bf16[9,32,512]{2,1,0:T(8,128)(2,1)S(1)}, u32[]{:S(2)}, u32[]{:S(2)}) %collective-permute-start.39) | collective-permute-done | bytes 294944 | tf_op jit(solution)/shard_map/ppermute | solution.py:723
  437.5 2.0 collective-permute-done.40
  439.8 1.1 maximum_bitcast_fusion
  440.9 1.7 copy.141
  (147 shorter events, 20.7 us)
Async XLA Ops:
  7.2 433.7 %all-reduce.2.cloned.1.call-start = ((), (), s32[]{:S(2)}) async-start(), calls=%async_computation | async-start | bytes 622592 | tf_op jit(solution)/shard_map/psum | solution.py:1046
  20.9 3.1 collective-permute-start
  20.9 104.2 %collective-permute-start.2 = (bf16[1536,512]{1,0:T(8,128)(2,1)}, bf16[1536,512]{1,0:T(8,128)(2,1)}, u32[]{:S(2)}, u32[]{:S(2)}) collective-permute-start(bf16[1536,512]{1,0:T(8,128)(2,1)} %get-tuple-element.59), channel_id=1, source_target_pairs={{0,2},{2,0},{4,6},{6,4},{8,10},{10,8},{12,14},{14,12},{16,18},{18,... | collective-permute-start | bytes 4718600 | tf_op jit(solution)/shard_map/ppermute | solution.py:717
  22.5 102.6 %collective-permute-start.3 = (bf16[1536,512]{1,0:T(8,128)(2,1)}, bf16[1536,512]{1,0:T(8,128)(2,1)S(1)}, u32[]{:S(2)}, u32[]{:S(2)}) collective-permute-start(bf16[1536,512]{1,0:T(8,128)(2,1)} %get-tuple-element.60), channel_id=1, source_target_pairs={{0,4},{2,6},{4,0},{6,2},{8,12},{10,14},{12,8},{14,10},{16,20},{18,... | collective-permute-start | bytes 4718600 | tf_op jit(solution)/shard_map/ppermute | solution.py:717
  64.0 41.8 %copy-start.15 = (s32[24]{0:T(128)S(1)}, s32[24]{0:T(128)}, u32[]{:S(2)}) copy-start(s32[24]{0:T(128)} %reshape.145.refs_0_) | copy-start | bytes 292
  64.0 44.0 %copy-start.7 = (bf16[1536,150]{0,1:T(8,128)(2,1)S(1)}, bf16[1536,150]{0,1:T(8,128)(2,1)}, u32[]{:S(2)}) copy-start(bf16[1536,150]{0,1:T(8,128)(2,1)} %param.25) | copy-start | bytes 1382404
  105.7 3.5 copy-start.10
  105.8 5.7 %copy-start.9 = (bf16[384,256]{1,0:T(8,128)(2,1)S(1)}, bf16[384,256]{1,0:T(8,128)(2,1)}, u32[]{:S(2)}) copy-start(bf16[384,256]{1,0:T(8,128)(2,1)} %get-tuple-element.55.refs_3_) | copy-start | bytes 589828
  105.8 19.3 %collective-permute-start.1 = (bf16[1536,256]{1,0:T(8,128)(2,1)}, bf16[1536,256]{1,0:T(8,128)(2,1)S(1)}, u32[]{:S(2)}, u32[]{:S(2)}) collective-permute-start(bf16[1536,256]{1,0:T(8,128)(2,1)} %get-tuple-element.58), channel_id=1, source_target_pairs={{0,1},{1,0},{2,3},{3,2},{4,5},{5,4},{6,7},{7,6},{8,9},{9,8},{10,11... | collective-permute-start | bytes 2359304 | tf_op jit(solution)/shard_map/ppermute | solution.py:720
  105.8 4.3 collective-permute-start.22
  107.1 4.3 collective-permute-start.23
  110.1 20.6 %copy-start.17 = (s32[24]{0:T(128)}, s32[24]{0:T(128)S(1)}, u32[]{:S(2)}) copy-start(s32[24]{0:T(128)S(1)} %collective-permute-done.22.refs_1_) | copy-start | bytes 292
  110.1 4.4 collective-permute-start.24
  111.5 19.2 %copy-start.16 = (s32[24]{0:T(128)}, s32[24]{0:T(128)S(1)}, u32[]{:S(2)}) copy-start(s32[24]{0:T(128)S(1)} %collective-permute-done.23.refs_1_) | copy-start | bytes 292
  111.5 6.5 %collective-permute-start.4 = (bf16[384,256]{1,0:T(8,128)(2,1)S(1)}, bf16[384,256]{1,0:T(8,128)(2,1)S(1)}, u32[]{:S(2)}, u32[]{:S(2)}) collective-permute-start(bf16[384,256]{1,0:T(8,128)(2,1)S(1)} %copy-done.9), channel_id=1, source_target_pairs={{0,2},{2,0},{4,6},{6,4},{8,10},{10,8},{12,14},{14,12},{16,18},{18,... | collective-permute-start | bytes 589832 | tf_op jit(solution)/shard_map/ppermute | solution.py:717
  115.1 9.9 %collective-permute-start.5 = (bf16[384,256]{1,0:T(8,128)(2,1)S(1)}, bf16[384,256]{1,0:T(8,128)(2,1)S(1)}, u32[]{:S(2)}, u32[]{:S(2)}) collective-permute-start(bf16[384,256]{1,0:T(8,128)(2,1)S(1)} %copy-done.9), channel_id=1, source_target_pairs={{0,4},{2,6},{4,0},{6,2},{8,12},{10,14},{12,8},{14,10},{16,20},{18,... | collective-permute-start | bytes 589832 | tf_op jit(solution)/shard_map/ppermute | solution.py:717
  117.9 7.1 %collective-permute-start.6 = (bf16[384,256]{1,0:T(8,128)(2,1)S(1)}, bf16[384,256]{1,0:T(8,128)(2,1)S(1)}, u32[]{:S(2)}, u32[]{:S(2)}) collective-permute-start(bf16[384,256]{1,0:T(8,128)(2,1)S(1)} %copy-done.9), channel_id=1, source_target_pairs={{0,6},{2,4},{4,2},{6,0},{8,14},{10,12},{12,10},{14,8},{16,22},{18,... | collective-permute-start | bytes 589832 | tf_op jit(solution)/shard_map/ppermute | solution.py:717
  154.7 5.2 %copy-start = (bf16[1536,150]{1,0:T(8,128)(2,1)S(1)}, bf16[1536,150]{1,0:T(8,128)(2,1)}, u32[]{:S(2)}) copy-start(bf16[1536,150]{1,0:T(8,128)(2,1)} %get-tuple-element.63) | copy-start | bytes 1382404
  159.8 31.2 %collective-permute-start.8 = (bf16[512,1536]{1,0:T(8,128)(2,1)}, bf16[512,1536]{1,0:T(8,128)(2,1)}, u32[]{:S(2)}, u32[]{:S(2)}) collective-permute-start(bf16[512,1536]{1,0:T(8,128)(2,1)} %get-tuple-element.66.refs_3_.refs_1_), channel_id=1, source_target_pairs={{0,1},{1,0},{2,3},{3,2},{4,5},{5,4},{6,7},{7,6},{8,9},{9,8},{10,11... | collective-permute-start | bytes 4718600 | tf_op jit(solution)/shard_map/ppermute | solution.py:720
  160.2 11.0 %copy-start.13 = (f32[8,256]{1,0:T(8,128)S(1)}, f32[8,256]{1,0:T(8,128)}, u32[]{:S(2)}) copy-start(f32[8,256]{1,0:T(8,128)} %dp_sum2.1.refs_4_) | copy-start | bytes 24580
  160.2 13.5 %copy-start.8 = (f32[256,150]{1,0:T(8,128)S(1)}, f32[256,150]{1,0:T(8,128)}, u32[]{:S(2)}) copy-start(f32[256,150]{1,0:T(8,128)} %get-tuple-element.90) | copy-start | bytes 460804
  160.2 28.8 %collective-permute-start.7 = (bf16[1536,150]{0,1:T(8,128)(2,1)S(1)}, bf16[1536,150]{0,1:T(8,128)(2,1)S(1)}, u32[]{:S(2)}, u32[]{:S(2)}) collective-permute-start(bf16[1536,150]{0,1:T(8,128)(2,1)S(1)} %copy.64), channel_id=1, source_target_pairs={{0,1},{1,0},{2,3},{3,2},{4,5},{5,4},{6,7},{7,6},{8,9},{9,8},{10,11... | collective-permute-start | bytes 1382408 | tf_op jit(solution)/shard_map/ppermute | solution.py:720
  171.2 3.4 copy-start.24
  171.2 3.4 collective-permute-start.44
  171.3 17.1 %collective-permute-start.9 = (bf16[128,1536]{1,0:T(8,128)(2,1)}, bf16[128,1536]{1,0:T(8,128)(2,1)S(1)}, u32[]{:S(2)}, u32[]{:S(2)}) collective-permute-start(bf16[128,1536]{1,0:T(8,128)(2,1)} %get-tuple-element.71), channel_id=1, source_target_pairs={{0,2},{2,0},{4,6},{6,4},{8,10},{10,8},{12,14},{14,12},{16,18},{18,... | collective-permute-start | bytes 1179656 | tf_op jit(solution)/shard_map/ppermute | solution.py:717
  172.8 16.1 %collective-permute-start.11 = (bf16[128,1536]{1,0:T(8,128)(2,1)}, bf16[128,1536]{1,0:T(8,128)(2,1)S(1)}, u32[]{:S(2)}, u32[]{:S(2)}) collective-permute-start(bf16[128,1536]{1,0:T(8,128)(2,1)} %get-tuple-element.72), channel_id=1, source_target_pairs={{0,4},{2,6},{4,0},{6,2},{8,12},{10,14},{12,8},{14,10},{16,20},{18,... | collective-permute-start | bytes 1179656 | tf_op jit(solution)/shard_map/ppermute | solution.py:717
  173.7 16.0 %copy-start.14 = (f32[150]{0:T(256)S(1)}, f32[150]{0:T(256)}, u32[]{:S(2)}) copy-start(f32[150]{0:T(256)} %param.24) | copy-start | bytes 1804
  174.6 13.8 %collective-permute-start.13 = (bf16[64,1536]{1,0:T(8,128)(2,1)S(1)}, bf16[64,1536]{1,0:T(8,128)(2,1)S(1)}, u32[]{:S(2)}, u32[]{:S(2)}) collective-permute-start(bf16[64,1536]{1,0:T(8,128)(2,1)S(1)} %copy-done.24), channel_id=1, source_target_pairs={{0,6},{2,4},{4,2},{6,0},{8,14},{10,12},{12,10},{14,8},{16,22},{18,... | collective-permute-start | bytes 589832 | tf_op jit(solution)/shard_map/ppermute | solution.py:717
  188.4 109.3 %collective-permute-start.16 = (bf16[1536,256]{1,0:T(8,128)(2,1)}, bf16[1536,256]{1,0:T(8,128)(2,1)}, u32[]{:S(2)}, u32[]{:S(2)}) collective-permute-start(bf16[1536,256]{1,0:T(8,128)(2,1)} %get-tuple-element.75.refs_1_), channel_id=1, source_target_pairs={{0,1},{1,0},{2,3},{3,2},{4,5},{5,4},{6,7},{7,6},{8,9},{9,8},{10,11... | collective-permute-start | bytes 2359304 | tf_op jit(solution)/shard_map/ppermute | solution.py:720
  188.4 18.6 %collective-permute-start.14 = (bf16[64,1536]{1,0:T(8,128)(2,1)S(1)}, bf16[64,1536]{1,0:T(8,128)(2,1)}, u32[]{:S(2)}, u32[]{:S(2)}) collective-permute-start(bf16[64,1536]{1,0:T(8,128)(2,1)S(1)} %collective-permute-done.13.refs_7_), channel_id=1, source_target_pairs={{0,1},{1,0},{2,3},{3,2},{4,5},{5,4},{6,7},{7,6},{8,9},{9,8},{10,11... | collective-permute-start | bytes 589832 | tf_op jit(solution)/shard_map/ppermute | solution.py:720
  189.0 18.1 %collective-permute-start.10 = (bf16[128,1536]{1,0:T(8,128)(2,1)S(1)}, bf16[128,1536]{1,0:T(8,128)(2,1)}, u32[]{:S(2)}, u32[]{:S(2)}) collective-permute-start(bf16[128,1536]{1,0:T(8,128)(2,1)S(1)} %collective-permute-done.9.refs_3_.refs_5_), channel_id=1, source_target_pairs={{0,1},{1,0},{2,3},{3,2},{4,5},{5,4},{6,7},{7,6},{8,9},{9,8},{10,11... | collective-permute-start | bytes 1179656 | tf_op jit(solution)/shard_map/ppermute | solution.py:720
  189.0 18.1 %collective-permute-start.12 = (bf16[128,1536]{1,0:T(8,128)(2,1)S(1)}, bf16[128,1536]{1,0:T(8,128)(2,1)}, u32[]{:S(2)}, u32[]{:S(2)}) collective-permute-start(bf16[128,1536]{1,0:T(8,128)(2,1)S(1)} %collective-permute-done.11.refs_5_), channel_id=1, source_target_pairs={{0,1},{1,0},{2,3},{3,2},{4,5},{5,4},{6,7},{7,6},{8,9},{9,8},{10,11... | collective-permute-start | bytes 1179656 | tf_op jit(solution)/shard_map/ppermute | solution.py:720
  256.1 123.9 %collective-permute-start.33 = (bf16[9,2,64,512]{3,2,1,0:T(8,128)(2,1)}, bf16[9,2,64,512]{3,2,1,0:T(8,128)(2,1)S(1)}, u32[]{:S(2)}, u32[]{:S(2)}) collective-permute-start(bf16[9,2,64,512]{3,2,1,0:T(8,128)(2,1)} %get-tuple-element.81.refs_9_), channel_id=1, source_target_pairs={{0,4},{2,6},{4,0},{6,2},{8,12},{10,14},{12,8},{14,10},{16,20},{18,... | collective-permute-start | bytes 3538952 | tf_op jit(solution)/shard_map/ppermute | solution.py:717
  259.8 26.5 %collective-permute-start.18 = (bf16[128,384]{1,0:T(8,128)(2,1)}, bf16[128,384]{1,0:T(8,128)(2,1)S(1)}, u32[]{:S(2)}, u32[]{:S(2)}) collective-permute-start(bf16[128,384]{1,0:T(8,128)(2,1)} %get-tuple-element.77), channel_id=1, source_target_pairs={{0,2},{2,0},{4,6},{6,4},{8,10},{10,8},{12,14},{14,12},{16,18},{18,... | collective-permute-start | bytes 294920 | tf_op jit(solution)/shard_map/ppermute | solution.py:717
  261.2 25.7 %collective-permute-start.20 = (bf16[128,384]{1,0:T(8,128)(2,1)}, bf16[128,384]{1,0:T(8,128)(2,1)S(1)}, u32[]{:S(2)}, u32[]{:S(2)}) collective-permute-start(bf16[128,384]{1,0:T(8,128)(2,1)} %get-tuple-element.78), channel_id=1, source_target_pairs={{0,4},{2,6},{4,0},{6,2},{8,12},{10,14},{12,8},{14,10},{16,20},{18,... | collective-permute-start | bytes 294920 | tf_op jit(solution)/shard_map/ppermute | solution.py:717
  261.9 23.8 %copy-start.12 = (f32[8,256]{1,0:T(8,128)S(1)}, f32[8,256]{1,0:T(8,128)}, u32[]{:S(2)}) copy-start(f32[8,256]{1,0:T(8,128)} %dp_sum3.1.refs_4_.refs_12_) | copy-start | bytes 24580
  261.9 29.1 %collective-permute-start.17 = (bf16[256,384]{1,0:T(8,128)(2,1)}, bf16[256,384]{1,0:T(8,128)(2,1)S(1)}, u32[]{:S(2)}, u32[]{:S(2)}) collective-permute-start(bf16[256,384]{1,0:T(8,128)(2,1)} %get-tuple-element.76.refs_1_), channel_id=1, source_target_pairs={{0,1},{1,0},{2,3},{3,2},{4,5},{5,4},{6,7},{7,6},{8,9},{9,8},{10,11... | collective-permute-start | bytes 589832 | tf_op jit(solution)/shard_map/ppermute | solution.py:720
  261.9 25.1 %copy-start.1 = (bf16[4,9,32,1024]{3,2,1,0:T(8,128)(2,1)S(1)}, bf16[4,9,32,1024]{3,2,1,0:T(8,128)(2,1)}, u32[]{:S(2)}) copy-start(bf16[4,9,32,1024]{3,2,1,0:T(8,128)(2,1)} %wgrad_fb.1.refs_9_) | copy-start | bytes 7077892
  286.3 4.6 %copy-start.22 = (bf16[384,256]{1,0:T(8,128)(2,1)S(1)}, bf16[384,256]{1,0:T(8,128)(2,1)}, u32[]{:S(2)}) copy-start(bf16[384,256]{1,0:T(8,128)(2,1)} %get-tuple-element.74.refs_3_) | copy-start | bytes 589828
  286.3 1.5 collective-permute-start.19
  286.9 2.3 collective-permute-start.21
  287.8 3.2 copy-start.30
  287.8 45.3 %collective-permute-start.41 = (bf16[9,32,1024]{2,1,0:T(8,128)(2,1)S(1)}, bf16[9,32,1024]{2,1,0:T(8,128)(2,1)S(1)}, u32[]{:S(2)}, u32[]{:S(2)}) collective-permute-start(bf16[9,32,1024]{2,1,0:T(8,128)(2,1)S(1)} %get-tuple-element.113), channel_id=1, source_target_pairs={{0,8},{2,10},{4,12},{6,14},{8,16},{10,18},{12,20},{14,22},{16,24},... | collective-permute-start | bytes 1769480 | tf_op jit(solution)/shard_map/ppermute | solution.py:723
  289.2 55.6 %collective-permute-start.42 = (bf16[9,32,1024]{2,1,0:T(8,128)(2,1)S(1)}, bf16[9,32,1024]{2,1,0:T(8,128)(2,1)S(1)}, u32[]{:S(2)}, u32[]{:S(2)}) collective-permute-start(bf16[9,32,1024]{2,1,0:T(8,128)(2,1)S(1)} %get-tuple-element.115), channel_id=1, source_target_pairs={{0,16},{2,18},{4,20},{6,22},{8,24},{10,26},{12,28},{14,30},{16,0},... | collective-permute-start | bytes 1769480 | tf_op jit(solution)/shard_map/ppermute | solution.py:723
  291.0 40.9 %collective-permute-start.15 = (bf16[384,256]{1,0:T(8,128)(2,1)S(1)}, bf16[384,256]{1,0:T(8,128)(2,1)S(1)}, u32[]{:S(2)}, u32[]{:S(2)}) collective-permute-start(bf16[384,256]{1,0:T(8,128)(2,1)S(1)} %copy-done.22), channel_id=1, source_target_pairs={{0,1},{1,0},{2,3},{3,2},{4,5},{5,4},{6,7},{7,6},{8,9},{9,8},{10,11... | collective-permute-start | bytes 589832 | tf_op jit(solution)/shard_map/ppermute | solution.py:720
  297.6 36.3 %collective-permute-start.25 = (bf16[4,2,64,512]{3,2,1,0:T(8,128)(2,1)}, bf16[4,2,64,512]{3,2,1,0:T(8,128)(2,1)}, u32[]{:S(2)}, u32[]{:S(2)}) collective-permute-start(bf16[4,2,64,512]{3,2,1,0:T(8,128)(2,1)} %get-tuple-element.85), channel_id=1, source_target_pairs={{0,4},{2,6},{4,0},{6,2},{8,12},{10,14},{12,8},{14,10},{16,20},{18,... | collective-permute-start | bytes 1572872 | tf_op jit(solution)/shard_map/ppermute | solution.py:717
  331.8 14.8 %collective-permute-start.43 = (bf16[9,32,1024]{2,1,0:T(8,128)(2,1)S(1)}, bf16[9,32,1024]{2,1,0:T(8,128)(2,1)S(1)}, u32[]{:S(2)}, u32[]{:S(2)}) collective-permute-start(bf16[9,32,1024]{2,1,0:T(8,128)(2,1)S(1)} %get-tuple-element.114), channel_id=1, source_target_pairs={{0,24},{2,26},{4,28},{6,30},{8,0},{10,2},{12,4},{14,6},{16,8},{18,... | collective-permute-start | bytes 1769480 | tf_op jit(solution)/shard_map/ppermute | solution.py:723
  333.2 10.5 %copy-start.6 = (bf16[4,2,64,512]{3,2,1,0:T(8,128)(2,1)S(1)}, bf16[4,2,64,512]{3,2,1,0:T(8,128)(2,1)}, u32[]{:S(2)}) copy-start(bf16[4,2,64,512]{3,2,1,0:T(8,128)(2,1)} %get-tuple-element.84) | copy-start | bytes 1572868
  333.2 69.7 %collective-permute-start.37 = (bf16[9,2,64,512]{3,2,1,0:T(8,128)(2,1)}, bf16[9,2,64,512]{3,2,1,0:T(8,128)(2,1)S(1)}, u32[]{:S(2)}, u32[]{:S(2)}) collective-permute-start(bf16[9,2,64,512]{3,2,1,0:T(8,128)(2,1)} %get-tuple-element.89), channel_id=1, source_target_pairs={{0,2},{2,0},{4,6},{6,4},{8,10},{10,8},{12,14},{14,12},{16,18},{18,... | collective-permute-start | bytes 3538952 | tf_op jit(solution)/shard_map/ppermute | solution.py:717
  334.0 37.9 %collective-permute-start.29 = (bf16[4,2,64,512]{3,2,1,0:T(8,128)(2,1)}, bf16[4,2,64,512]{3,2,1,0:T(8,128)(2,1)}, u32[]{:S(2)}, u32[]{:S(2)}) collective-permute-start(bf16[4,2,64,512]{3,2,1,0:T(8,128)(2,1)} %get-tuple-element.83.refs_4_), channel_id=1, source_target_pairs={{0,2},{2,0},{4,6},{6,4},{8,10},{10,8},{12,14},{14,12},{16,18},{18,... | collective-permute-start | bytes 1572872 | tf_op jit(solution)/shard_map/ppermute | solution.py:717
  344.9 30.9 %collective-permute-start.26 = (bf16[4,32,512]{2,1,0:T(8,128)(2,1)S(1)}, bf16[4,32,512]{2,1,0:T(8,128)(2,1)S(1)}, u32[]{:S(2)}, u32[]{:S(2)}) collective-permute-start(bf16[4,32,512]{2,1,0:T(8,128)(2,1)S(1)} %get-tuple-element.122), channel_id=1, source_target_pairs={{0,8},{2,10},{4,12},{6,14},{8,16},{10,18},{12,20},{14,22},{16,24},... | collective-permute-start | bytes 393224 | tf_op jit(solution)/shard_map/ppermute | solution.py:723
  346.6 30.2 %collective-permute-start.27 = (bf16[4,32,512]{2,1,0:T(8,128)(2,1)S(1)}, bf16[4,32,512]{2,1,0:T(8,128)(2,1)S(1)}, u32[]{:S(2)}, u32[]{:S(2)}) collective-permute-start(bf16[4,32,512]{2,1,0:T(8,128)(2,1)S(1)} %get-tuple-element.123), channel_id=1, source_target_pairs={{0,16},{2,18},{4,20},{6,22},{8,24},{10,26},{12,28},{14,30},{16,0},... | collective-permute-start | bytes 393224 | tf_op jit(solution)/shard_map/ppermute | solution.py:723
  371.9 7.2 %collective-permute-start.28 = (bf16[4,32,512]{2,1,0:T(8,128)(2,1)S(1)}, bf16[4,32,512]{2,1,0:T(8,128)(2,1)S(1)}, u32[]{:S(2)}, u32[]{:S(2)}) collective-permute-start(bf16[4,32,512]{2,1,0:T(8,128)(2,1)S(1)} %get-tuple-element.124), channel_id=1, source_target_pairs={{0,24},{2,26},{4,28},{6,30},{8,0},{10,2},{12,4},{14,6},{16,8},{18,... | collective-permute-start | bytes 393224 | tf_op jit(solution)/shard_map/ppermute | solution.py:723
  374.6 5.5 %copy-start.3 = (bf16[9,2,64,512]{3,2,1,0:T(8,128)(2,1)S(1)}, bf16[9,2,64,512]{3,2,1,0:T(8,128)(2,1)}, u32[]{:S(2)}) copy-start(bf16[9,2,64,512]{3,2,1,0:T(8,128)(2,1)} %get-tuple-element.87) | copy-start | bytes 3538948
  375.8 8.3 %collective-permute-start.30 = (bf16[4,32,512]{2,1,0:T(8,128)(2,1)S(1)}, bf16[4,32,512]{2,1,0:T(8,128)(2,1)S(1)}, u32[]{:S(2)}, u32[]{:S(2)}) collective-permute-start(bf16[4,32,512]{2,1,0:T(8,128)(2,1)S(1)} %get-tuple-element.125), channel_id=1, source_target_pairs={{0,8},{2,10},{4,12},{6,14},{8,16},{10,18},{12,20},{14,22},{16,24},... | collective-permute-start | bytes 393224 | tf_op jit(solution)/shard_map/ppermute | solution.py:723
  376.8 12.0 %collective-permute-start.31 = (bf16[4,32,512]{2,1,0:T(8,128)(2,1)S(1)}, bf16[4,32,512]{2,1,0:T(8,128)(2,1)S(1)}, u32[]{:S(2)}, u32[]{:S(2)}) collective-permute-start(bf16[4,32,512]{2,1,0:T(8,128)(2,1)S(1)} %get-tuple-element.126), channel_id=1, source_target_pairs={{0,16},{2,18},{4,20},{6,22},{8,24},{10,26},{12,28},{14,30},{16,0},... | collective-permute-start | bytes 393224 | tf_op jit(solution)/shard_map/ppermute | solution.py:723
  379.1 22.8 %collective-permute-start.32 = (bf16[4,32,512]{2,1,0:T(8,128)(2,1)S(1)}, bf16[4,32,512]{2,1,0:T(8,128)(2,1)S(1)}, u32[]{:S(2)}, u32[]{:S(2)}) collective-permute-start(bf16[4,32,512]{2,1,0:T(8,128)(2,1)S(1)} %get-tuple-element.127), channel_id=1, source_target_pairs={{0,24},{2,26},{4,28},{6,30},{8,0},{10,2},{12,4},{14,6},{16,8},{18,... | collective-permute-start | bytes 393224 | tf_op jit(solution)/shard_map/ppermute | solution.py:723
  380.1 22.8 %copy-start.4 = (bf16[9,2,64,512]{3,2,1,0:T(8,128)(2,1)S(1)}, bf16[9,2,64,512]{3,2,1,0:T(8,128)(2,1)}, u32[]{:S(2)}) copy-start(bf16[9,2,64,512]{3,2,1,0:T(8,128)(2,1)} %get-tuple-element.88) | copy-start | bytes 3538948
  380.4 27.1 %collective-permute-start.34 = (bf16[9,32,512]{2,1,0:T(8,128)(2,1)S(1)}, bf16[9,32,512]{2,1,0:T(8,128)(2,1)S(1)}, u32[]{:S(2)}, u32[]{:S(2)}) collective-permute-start(bf16[9,32,512]{2,1,0:T(8,128)(2,1)S(1)} %get-tuple-element.116), channel_id=1, source_target_pairs={{0,8},{2,10},{4,12},{6,14},{8,16},{10,18},{12,20},{14,22},{16,24},... | collective-permute-start | bytes 884744 | tf_op jit(solution)/shard_map/ppermute | solution.py:723
  384.1 42.4 %collective-permute-start.35 = (bf16[9,32,512]{2,1,0:T(8,128)(2,1)S(1)}, bf16[9,32,512]{2,1,0:T(8,128)(2,1)S(1)}, u32[]{:S(2)}, u32[]{:S(2)}) collective-permute-start(bf16[9,32,512]{2,1,0:T(8,128)(2,1)S(1)} %get-tuple-element.117), channel_id=1, source_target_pairs={{0,16},{2,18},{4,20},{6,22},{8,24},{10,26},{12,28},{14,30},{16,0},... | collective-permute-start | bytes 884744 | tf_op jit(solution)/shard_map/ppermute | solution.py:723
  388.7 38.5 %collective-permute-start.36 = (bf16[9,32,512]{2,1,0:T(8,128)(2,1)S(1)}, bf16[9,32,512]{2,1,0:T(8,128)(2,1)S(1)}, u32[]{:S(2)}, u32[]{:S(2)}) collective-permute-start(bf16[9,32,512]{2,1,0:T(8,128)(2,1)S(1)} %get-tuple-element.118), channel_id=1, source_target_pairs={{0,24},{2,26},{4,28},{6,30},{8,0},{10,2},{12,4},{14,6},{16,8},{18,... | collective-permute-start | bytes 884744 | tf_op jit(solution)/shard_map/ppermute | solution.py:723
  403.2 29.6 %collective-permute-start.38 = (bf16[9,32,512]{2,1,0:T(8,128)(2,1)S(1)}, bf16[9,32,512]{2,1,0:T(8,128)(2,1)S(1)}, u32[]{:S(2)}, u32[]{:S(2)}) collective-permute-start(bf16[9,32,512]{2,1,0:T(8,128)(2,1)S(1)} %get-tuple-element.119), channel_id=1, source_target_pairs={{0,8},{2,10},{4,12},{6,14},{8,16},{10,18},{12,20},{14,22},{16,24},... | collective-permute-start | bytes 884744 | tf_op jit(solution)/shard_map/ppermute | solution.py:723
  403.3 34.3 %collective-permute-start.39 = (bf16[9,32,512]{2,1,0:T(8,128)(2,1)S(1)}, bf16[9,32,512]{2,1,0:T(8,128)(2,1)S(1)}, u32[]{:S(2)}, u32[]{:S(2)}) collective-permute-start(bf16[9,32,512]{2,1,0:T(8,128)(2,1)S(1)} %get-tuple-element.120), channel_id=1, source_target_pairs={{0,16},{2,18},{4,20},{6,22},{8,24},{10,26},{12,28},{14,30},{16,0},... | collective-permute-start | bytes 884744 | tf_op jit(solution)/shard_map/ppermute | solution.py:723
  407.5 32.1 %collective-permute-start.40 = (bf16[9,32,512]{2,1,0:T(8,128)(2,1)S(1)}, bf16[9,32,512]{2,1,0:T(8,128)(2,1)S(1)}, u32[]{:S(2)}, u32[]{:S(2)}) collective-permute-start(bf16[9,32,512]{2,1,0:T(8,128)(2,1)S(1)} %get-tuple-element.121), channel_id=1, source_target_pairs={{0,24},{2,26},{4,28},{6,30},{8,0},{10,2},{12,4},{14,6},{16,8},{18,... | collective-permute-start | bytes 884744 | tf_op jit(solution)/shard_map/ppermute | solution.py:723
  (14 other events, 16.0 us)
Sparse Core Ops, SparseCore 0:
  174.7 146.9 all-reduce.1

commit v2 on v1

--- a/solution.py
+++ b/solution.py
@@ -96,9 +96,9 @@
         total = None
         for y, x, height, width in rel:
             hit = within(y, height) & within(x, width)
-            if dy:
+            if not isinstance(dy, int) or dy:
                 hit = hit & within(y + dy, height)
-            if dx:
+            if not isinstance(dx, int) or dx:
                 hit = hit & within(x + dx, width)
             value = jnp.where(hit, 1.0, 0.0)
             total = value if total is None else total + value
@@ -109,6 +109,19 @@
 
 def wide(column_block, times):
     return jnp.concatenate([column_block] * times, axis=1)
+
+
+def rows_down(boxes_ref, canvas, box_count, x_ref, xs, at):
+    gate = pixel_gates(boxes_ref, canvas, box_count, (PX, CELLS), 0)
+    reps = xs.shape[2] // CELLS
+    blank = jnp.zeros((CW, xs.shape[2]), BF16)
+    up = wide(gate(-1, 0).astype(BF16), reps)
+    down = wide(gate(1, 0).astype(BF16), reps)
+    xs[0, at : at + CW] = blank
+    xs[0, at + CW : at + PX] = x_ref[at : at + PX - CW] * up[CW:]
+    xs[1, at : at + PX] = x_ref[at : at + PX] * wide(gate(0, 0).astype(BF16), reps)
+    xs[2, at : at + PX - CW] = x_ref[at + CW : at + PX] * down[: PX - CW]
+    xs[2, at + PX - CW : at + PX] = blank
 
 
 def member_bounds(table_at, height, width):
@@ -133,16 +146,14 @@
     return jnp.where(hit, 1.0, 0.0), (r1 - r0) * (c1 - c0)
 
 
-def gated_lifts(boxes_ref, canvas, box_count, lanes_ref):
+def gated_lifts(boxes_ref, canvas, box_count, lanes_ref, store):
     def table_at(row):
         return lanes_ref[row : row + 1, :]
 
     top, left, height, width = by_box(boxes_ref, canvas, table_at(0), box_count)
-    place = lax.broadcasted_iota(jnp.int32, (PX, CELLS), 0)
-    row = (place >> 5).astype(F32) - top
-    col = (place & (CW - 1)).astype(F32) - left
-
-    def side(relative, extent, cell):
+
+    def side(size, edge, extent, cell):
+        relative = lax.broadcasted_iota(jnp.int32, (size, CELLS), 0).astype(F32) - edge
         scale = (table_at(1) - 1.0) / (extent - 1.0)
         own = within(relative, extent)
         found = []
@@ -152,19 +163,15 @@
             found.append(jnp.where(own & within(moved, extent), weight, 0.0))
         return found
 
-    rows = [found * table_at(5) for found in side(row, height, table_at(2))]
-    cols = side(col, width, table_at(3))
-    return [rows[d // 3] * cols[d % 3] for d in range(9)]
+    rows = [found * table_at(5) for found in side(CH, top, height, table_at(2))]
+    cols = side(CW, left, width, table_at(3))
+    for d in range(9):
+        for y in range(CH):
+            store(d, y, (rows[d // 3][y : y + 1] * cols[d % 3]).astype(BF16))
 
 
 def pltranspose(block):
     return jnp.transpose(block, (1, 0))
-
-
-def lifts_kernel(box_count, boxes_ref, lanes_ref, out_ref):
-    lifts = gated_lifts(boxes_ref, pl.program_id(0), box_count, lanes_ref)
-    for d in range(9):
-        out_ref[0, :, d * CELLS : (d + 1) * CELLS] = lifts[d].astype(BF16)
 
 
 def pool_kernel(canv, box_count, boxes_ref, lanes_ref, cells_ref, x_ref, w_ref, pooled_ref, lift_ref, own_ref, send_ref, first_ref, last_ref, kept, zs):
@@ -180,9 +187,11 @@
     pooled = (dot(select.astype(BF16), x_ref[...]) / count).astype(BF16)
     pooled_ref[...] = pooled
     kept[pl.ds(pl.multiple_of(n * CELLS, CELLS), CELLS), :] = pooled
-    lifts = gated_lifts(boxes_ref, n, box_count, lanes_ref)
-    for d in range(9):
-        lift_ref[0, :, d * CELLS : (d + 1) * CELLS] = lifts[d].astype(BF16)
+
+    def store(d, y, block):
+        lift_ref[0, y * CW : (y + 1) * CW, d * CELLS : (d + 1) * CELLS] = block
+
+    gated_lifts(boxes_ref, n, box_count, lanes_ref, store)
 
     @pl.when(n == canv - 1)
     def _():
@@ -314,44 +323,45 @@
             keep[rows, level * width : (level + 1) * width] = mine.astype(BF16)
 
 
-def join_kernel(canv, box_count, boxes_ref, cells_ref, x_ref, y_ref, lift_ref, wfx_ref, wfb_ref, own_ref, send_ref, q, gy, zp, ye):
-    d = pl.program_id(0)
-    dy = d // 3
-    dx = d % 3
-    mid = wfx_ref.shape[2]
+def join_kernel(canv, box_count, boxes_ref, cells_ref, x_ref, y_ref, lift_ref, wfx_ref, wfb_ref, own_ref, send_ref, xs, ye, terms, f):
+    t = pl.program_id(0)
+    mid = wfx_ref.shape[3]
     reps = mid // CELLS
 
-    @pl.when(d == 0)
+    @pl.when(t == 0)
     def _():
-        q[...] = jnp.zeros_like(q)
-        zp[...] = jnp.zeros_like(zp)
         expand(y_ref[...], cells_ref, ye)
         for n in range(canv):
-            gate = pixel_gates(boxes_ref, n, box_count, (PX, CELLS), 0)
-            for step in range(3):
-                gy[step, n] = gate(step - 1, 0)
-
-    wfb = wfb_ref[0].reshape(ye.shape[1], mid)
-    terms = dot(ye[...], wfb).astype(BF16)
+            rows_down(boxes_ref, n, box_count, x_ref, xs, n * PX)
+
     for n in range(canv):
-        zp[n, CW : CW + PX] = dot(x_ref[n * PX : (n + 1) * PX], wfx_ref[0])
-        q[1, n] += dot(lift_ref[n], terms[n * CELLS : (n + 1) * CELLS])
-    for n in range(canv):
-        moved = zp[n, pl.ds(pl.multiple_of(dy * CW, CW), PX)]
-        q[dx, n] += wide(gy[dy, n], reps) * moved
-
-    @pl.when(d == 8)
+        rows = slice(n * PX, (n + 1) * PX)
+        q = dot(xs[0, rows], wfx_ref[0, 0]) + dot(xs[1, rows], wfx_ref[1, 0]) + dot(xs[2, rows], wfx_ref[2, 0])
+        gate = wide(pixel_gates(boxes_ref, n, box_count, (PX, CELLS), 0)(0, t - 1), reps)
+        q = gate * pltpu.roll(q, (PX + 1 - t) % PX, 0)
+
+        @pl.when(t == 0)
+        def _():
+            f[n] = q
+
+        @pl.when(t > 0)
+        def _():
+            f[n] += q
+
+    for dy in range(3):
+        term = dot(ye[...], wfb_ref[dy, 0].reshape(ye.shape[1], mid)).astype(BF16)
+        for n in range(canv):
+            terms[n, pl.ds(pl.multiple_of((dy * 3 + t) * CELLS, CELLS), CELLS)] = term[n * CELLS : (n + 1) * CELLS]
+
+    @pl.when(t == 2)
     def _():
         half = own_ref.shape[1]
         chan = lax.axis_index("chan")
         for n in range(canv):
-            gate = pixel_gates(boxes_ref, n, box_count, (PX, CELLS), 0)
-            f = q[1, n] + wide(gate(0, -1), reps) * pltpu.roll(q[0, n], 1, 0)
-            f = f + wide(gate(0, 1), reps) * pltpu.roll(q[2, n], PX - 1, 0)
-            zp[n, CW : CW + PX] = f
+            f[n] += dot(lift_ref[n], terms[n])
             rows = slice(n * PX, (n + 1) * PX)
-            own_ref[rows] = zp[n, CW : CW + PX, pl.ds(pl.multiple_of(chan * half, half), half)]
-            send_ref[rows] = zp[n, CW : CW + PX, pl.ds(pl.multiple_of((1 - chan) * half, half), half)].astype(BF16)
+            own_ref[rows] = f[n, :, pl.ds(pl.multiple_of(chan * half, half), half)]
+            send_ref[rows] = f[n, :, pl.ds(pl.multiple_of((1 - chan) * half, half), half)].astype(BF16)
 
 
 def join_sums_kernel(canv, box_count, boxes_ref, own_ref, got_ref, f_ref, part_ref):
@@ -442,63 +452,29 @@
     split_rows(flip, half // (4 * each), each, own_a, send_a, own_b, send_b, send_d)
 
 
-def dx_kernel(canv, box_count, boxes_ref, own_ref, got_ref, w_ref, out_ref, acc, gy, e3):
-    d = pl.program_id(0)
-    dy = d // 3
-    dx = d % 3
-    half = own_ref.shape[1]
-    reps = half // CELLS
-    chan = lax.axis_index("chan")
-
-    @pl.when(d == 0)
-    def _():
-        e3[...] = jnp.zeros_like(e3)
-        for n in range(canv):
-            gate = pixel_gates(boxes_ref, n, box_count, (PX, CELLS), 0)
-            for step in range(3):
-                gy[step, n] = gate(1 - step, 0).astype(BF16)
-            rows = slice(n * PX, (n + 1) * PX)
-            for side, ref in enumerate((own_ref, got_ref)):
-                df = ref[rows].astype(F32)
-                e3[side, 1, n, CW : CW + PX] = df.astype(BF16)
-                e3[side, 0, n, CW : CW + PX] = (wide(gate(0, 1), reps) * pltpu.roll(df, PX - 1, 0)).astype(BF16)
-                e3[side, 2, n, CW : CW + PX] = (wide(gate(0, -1), reps) * pltpu.roll(df, 1, 0)).astype(BF16)
-
-    for n in range(canv):
-        total = None
-        for side, which in ((0, chan), (1, 1 - chan)):
-            e = e3[side, dx, n, pl.ds(pl.multiple_of((2 - dy) * CW, CW), PX)] * wide(gy[dy, n], reps)
-            w = w_ref[0, :, pl.ds(pl.multiple_of(which * half, half), half)]
-            part = dot_nt(e, w)
-            total = part if total is None else total + part
-
-        @pl.when(d == 0)
-        def _():
-            acc[n] = total
-
-        @pl.when(d > 0)
-        def _():
-            acc[n] += total
-
-    @pl.when(d == 8)
-    def _():
-        for n in range(canv):
-            out_ref[n * PX : (n + 1) * PX] = acc[n].astype(BF16)
-
-
-def branch_back_kernel(canv, boxes_unused, cells_ref, lanes_ref, own_ref, got_ref, lift_ref, w_ref, norm_ref, act_ref, da_ref, part_ref, acc):
+def branch_back_kernel(canv, cells_ref, lanes_ref, own_ref, got_ref, lift_ref, w_ref, norm_ref, act_ref, da_ref, part_ref, acc, grads):
     d = pl.program_id(0)
     half = own_ref.shape[0]
     chan = lax.axis_index("chan")
 
     @pl.when(d == 0)
     def _():
-        acc[...] = jnp.zeros_like(acc)
-
-    for ref, which in ((own_ref, chan), (got_ref, 1 - chan)):
-        cells = [dot(ref[:, n * PX : (n + 1) * PX], lift_ref[n]).astype(BF16) for n in range(canv)]
-        w = w_ref[0, :, :, pl.ds(pl.multiple_of(which * half, half), half)].reshape(acc.shape[0], half)
-        acc[...] += dot(w, jnp.concatenate(cells, axis=1))
+        for ref, which in ((own_ref, chan), (got_ref, 1 - chan)):
+            for n in range(canv):
+                found = dot(ref[:, n * PX : (n + 1) * PX], lift_ref[n]).astype(BF16)
+                for e in range(9):
+                    into = pl.ds(pl.multiple_of(which * half, half), half)
+                    grads[e, into, n * CELLS : (n + 1) * CELLS] = found[:, e * CELLS : (e + 1) * CELLS]
+
+    part = dot(w_ref[0].reshape(acc.shape[0], 2 * half), grads[d])
+
+    @pl.when(d == 0)
+    def _():
+        acc[...] = part
+
+    @pl.when(d > 0)
+    def _():
+        acc[...] += part
 
     @pl.when(d == 8)
     def _():
@@ -540,145 +516,301 @@
     split_rows(flip, half // (4 * each), each, pack_ref.at[0 : half // 2], send_a, pack_ref.at[half // 2 : half], send_b)
 
 
-def grad_x_kernel(canv, box_count, boxes_ref, lanes_ref, cells_ref, own_ref, got_ref, w_ref, dx_ref, out_ref, kept):
-    n = pl.program_id(0)
-    half = own_ref.shape[1]
-    chan = lax.axis_index("chan")
-
-    @pl.when(n == 0)
-    def _():
-        total = 0.0
-        for level in range(4):
-            for ref, which in ((own_ref, chan), (got_ref, 1 - chan)):
-                mine = [
-                    jnp.where(cells_ref[:, 4:5] == level, ref[m * CELLS : (m + 1) * CELLS].astype(F32), 0.0).astype(BF16)
-                    for m in range(canv)
-                ]
-                w = w_ref[level, :, pl.ds(pl.multiple_of(which * half, half), half)]
-                total = total + dot_nt(jnp.concatenate(mine, axis=0), w)
-        for m in range(canv):
-            top, left, height, width = by_box(boxes_ref, m, cells_ref[:, 0:1], box_count)
-            r0, r1, c0, c1 = member_bounds(lambda row: cells_ref[:, row : row + 1], height, width)
-            kept[m] = (total[m * CELLS : (m + 1) * CELLS] / ((r1 - r0) * (c1 - c0))).astype(BF16)
-
-    select, _ = members(boxes_ref, n, box_count, lambda row: lanes_ref[row : row + 1, :], (PX, CELLS), 0)
-    out_ref[...] = (dx_ref[...].astype(F32) + dot(select.astype(BF16), kept[n])).astype(BF16)
-
-
-def put_rows(out, index, own_ref, other_ref, scale=None):
+def put_rows(out, index, own_ref, other_ref):
     chan = lax.axis_index("chan")
     size = own_ref.shape[0]
+    width = own_ref.shape[1]
     for ref, which in ((own_ref, chan), (other_ref, 1 - chan)):
-        value = ref[...] if scale is None else (ref[...].astype(F32) * scale).astype(BF16)
-        out[index, pl.ds(pl.multiple_of(which * size, size), size), :] = value
-
-
-def wgrad_kernel(
-    canv, box_count, bit_of, boxes0, boxes1, cells_ref, own0, other0, own1, other1, x0, x1, keep_ref, send_ref, pooled_ref, acc, lhs, xd
-):
-    pixels = x0.shape[0]
-    reps = x0.shape[1] // CELLS
-    for source, (boxes_ref, own_ref, other_ref, x_ref) in enumerate(((boxes0, own0, other0, x0), (boxes1, own1, other1, x1))):
-        down = []
-        for n in range(canv):
-            rows = slice(n * PX, (n + 1) * PX)
-            into = slice(CW + n * PX, CW + (n + 1) * PX)
-            gate = pixel_gates(boxes_ref, n, box_count, (PX, CELLS), 0)
-            x = x_ref[rows].astype(F32)
-            xd[0, into] = (wide(gate(0, -1), reps) * pltpu.roll(x, 1, 0)).astype(BF16)
-            xd[1, into] = x_ref[rows]
-            xd[2, into] = (wide(gate(0, 1), reps) * pltpu.roll(x, PX - 1, 0)).astype(BF16)
-            across = pixel_gates(boxes_ref, n, box_count, (8, PX), 1)
-            down.append([across(step, 0)[0:1, :] for step in (-1, 0, 1)])
-        if source == 0:
-            for step in range(3):
-                xd[step, 0:CW] = jnp.zeros((CW, x0.shape[1]), BF16)
-                xd[step, CW + pixels : 2 * CW + pixels] = jnp.zeros((CW, x0.shape[1]), BF16)
-        else:
-            for n in range(canv):
-                select, count = members(
-                    boxes_ref, n, box_count, lambda row: cells_ref[:, row : row + 1], (CELLS, PX), 1
-                )
-                sums = dot(select.astype(BF16), x_ref[n * PX : (n + 1) * PX])
-                pooled_ref[n * CELLS : (n + 1) * CELLS] = (sums / count).astype(BF16)
-        for step in range(3):
-            put_rows(lhs, step, own_ref, other_ref, jnp.concatenate([found[step] for found in down], axis=1))
-
-        def offset(d, carry):
-            dy = d // 3
-            part = dot(lhs[dy], xd[d % 3, pl.ds(pl.multiple_of(dy * CW, CW), pixels), :])
-            if source == 0:
-                acc[d] = part
-            else:
-                acc[d] += part
-            return carry
-
-        lax.fori_loop(0, 9, offset, 0)
-    split_out(9, bit_of, acc, keep_ref, send_ref)
-
-
-def split_out(count, bit_of, acc, keep_ref, send_ref):
-    bit = (lax.axis_index("dp") // bit_of) % 2
-    size = keep_ref.shape[2]
+        out[index, pl.ds(pl.multiple_of(which * size, size), size), :width] = ref[...]
+
+
+def cols_across(boxes_ref, canvas, at, box_count, own_ref, other_ref, lhs):
+    chan = lax.axis_index("chan")
+    size = own_ref.shape[0]
+    span = slice(at * PX, (at + 1) * PX)
+    gate = pixel_gates(boxes_ref, canvas, box_count, (8, PX), 1)
+    for ref, which in ((own_ref, chan), (other_ref, 1 - chan)):
+        into = pl.ds(pl.multiple_of(which * size, size), size)
+        value = ref[:, span].astype(F32)
+        lhs[0, into, span] = (pltpu.roll(value, PX - 1, 1) * gate(0, 1)[0:1]).astype(BF16)
+        lhs[1, into, span] = ref[:, span]
+        lhs[2, into, span] = (pltpu.roll(value, 1, 1) * gate(0, -1)[0:1]).astype(BF16)
+
+
+def split_out(count, bit, acc, keep, send):
+    parts, _, each, _ = keep.shape
+    groups = parts // 2
+    block = groups * each
 
     def one(d, carry):
         for half in range(2):
-            for ref, which in ((keep_ref, bit), (send_ref, 1 - bit)):
-                ref[d, half] = acc[d, pl.ds(pl.multiple_of((half * 2 + which) * size, size), size), :].astype(BF16)
+            for ref, which in ((keep, bit), (send, 1 - bit)):
+                for group in range(groups):
+                    at = (half * 2 + which) * block + group * each
+                    ref[half * groups + group, d] = acc[d, pl.ds(pl.multiple_of(at, each), each), :].astype(BF16)
         return carry
 
     lax.fori_loop(0, count, one, 0)
 
 
-def wgrad_fb_kernel(
-    canv, cells_ref, own0, oth0, own1, oth1, own2, oth2, own3, oth3, lift0_ref, lift1_ref, y_ref, out_ref, ye, lhs
+def tail_kernel(
+    canv, box_count,
+    boxes_ref, lanes_ref, cells_ref, qa0, qa1, qb0, qb1, ga0, ga1, gb0, gb1, gd0, gd1, y_ref, pooled_ref,
+    za0, za1, zb0, zb1, zga0, zga1, zgb0, zgb1, dz0, dz1, df0, df1, x_any, xm_any, ym_any, wfx_any, wbr_any,
+    gx_ref, out_fx, out_fb, out_br,
+    lhs4, lift, grads, xbuf, wbuf, xd, lhs, acc, pool_mate, kept,
+    fb_send, fb_recv, keep_a, send_a, recv_a, zrecv_a, keep_b, send_b, recv_b, zrecv_b,
+    bkeep_a, bsend_a, brecv_a, bzrecv_a, bkeep_b, bsend_b, brecv_b, bzrecv_b,
+    load_sem, w_sem, mate_send, mate_recv, part_send, part_recv,
 ):
-    d = pl.program_id(0)
-
-    @pl.when(d == 0)
-    def _():
-        expand(y_ref[...], cells_ref, ye)
-        me = lax.axis_index("dp")
-        x_bit, y_bit = me % 2, (me // 2) % 2
-        size = own3.shape[0]
-        sources = ((own0, oth0, y_bit), (own1, oth1, y_bit), (own2, oth2, x_bit), (own3, oth3, 0))
-        for source, (own_ref, oth_ref, bit) in enumerate(sources):
-            mine = pl.ds(pl.multiple_of(bit * size, size), size)
-            put_rows(lhs, source, own_ref.at[mine], oth_ref.at[mine])
-
-    cells = []
-    for n in range(PLANE * canv):
-        lift = lift0_ref[n] if n < canv else lift1_ref[n - canv]
-        grads = lhs[n // canv, :, (n % canv) * PX : (n % canv + 1) * PX]
-        cells.append(dot(grads, lift).astype(BF16))
-    result = dot(jnp.concatenate(cells, axis=1), ye[...])
-    parts, _, each, _ = out_ref.shape
-    for part in range(parts):
-        out_ref[part, 0] = result[part * each : (part + 1) * each].astype(BF16)
-
-
-def wgrad_br_kernel(canv, lanes_ref, own_ref, oth_ref, owna, otha, ownb, othb, pooled_ref, poola, poolb, keepa, senda, keepb, sendb, acc, lhs):
+    me = lax.axis_index("dp")
+    chan = lax.axis_index("chan")
+    parts = fb_send.shape[0]
+    pixels = df0.shape[0]
+    half = df0.shape[1]
+    span = xbuf.shape[2]
+    group, place = me // PLANE, me % PLANE
+    x_bit, y_bit = me % 2, (me // 2) % 2
+    x_mate = me + 1 - 2 * x_bit
+    y_mate = me + 2 - 4 * y_bit
+
+    def peer(step):
+        return lax.rem(group + step, parts) * PLANE + place
+
+    barrier = pltpu.get_barrier_semaphore()
+    for other in [x_mate, y_mate] + [peer(step) for step in range(1, parts)]:
+        pl.semaphore_signal(barrier, inc=1, device_id=(other, chan), device_id_type=MESH)
+
+    def load(source, slot, which):
+        return pltpu.make_async_copy(source, xbuf.at[slot], load_sem.at[which])
+
+    loads = [
+        load(x_any.at[:, pl.ds(0, span)], 0, 0),
+        load(xm_any, 1, 1),
+        load(x_any.at[:, pl.ds(span, span)], 0, 2),
+        load(ym_any, 1, 3),
+    ]
+    loads[0].start()
+    loads[1].start()
+
+    def tile_load(tile):
+        width = wbuf.shape[1]
+        return pltpu.make_async_copy(
+            wfx_any.at[:, pl.ds(pl.multiple_of(tile * width, width), width), :],
+            wbuf.at[pl.ds(pl.multiple_of(lax.rem(tile, 2) * 9, 9), 9)],
+            w_sem.at[lax.rem(tile, 2)],
+        )
+
+    tile_load(0).start()
+
+    def mate_copy(number, source, target, mate):
+        return pltpu.make_async_remote_copy(
+            src_ref=source, dst_ref=target, send_sem=mate_send.at[number], recv_sem=mate_recv.at[number],
+            device_id=(mate, chan), device_id_type=MESH,
+        )
+
+    def part_copy(number, step, source, target):
+        return pltpu.make_async_remote_copy(
+            src_ref=source.at[lax.rem(group + step, parts)], dst_ref=target.at[step - 1],
+            send_sem=part_send.at[number * (parts - 1) + step - 1], recv_sem=part_recv.at[number * (parts - 1) + step - 1],
+            device_id=(peer(step), chan), device_id_type=MESH,
+        )
+
+    ye = gx_ref
+    expand(y_ref[...], cells_ref, ye)
+    size = gd0.shape[0]
+    for source, (own_ref, oth_ref, bit) in enumerate(((qa0, qa1, y_bit), (ga0, ga1, y_bit), (gb0, gb1, x_bit), (gd0, gd1, 0))):
+        mine = pl.ds(pl.multiple_of(bit * size, size), size)
+        put_rows(lhs4, source, own_ref.at[mine], oth_ref.at[mine])
+
+    def canvas(n, carry):
+        def store(d, y, block):
+            lift[y * CW : (y + 1) * CW, d * CELLS : (d + 1) * CELLS] = block
+
+        gated_lifts(boxes_ref, n, box_count, lanes_ref, store)
+        rows = lhs4[n // canv, :, pl.ds(pl.multiple_of((n % canv) * PX, PX), PX)]
+        found = dot(rows, lift[...]).astype(BF16)
+        for d in range(9):
+            grads[d, :, pl.ds(pl.multiple_of(n * CELLS, CELLS), CELLS)] = found[:, d * CELLS : (d + 1) * CELLS]
+        return carry
+
+    lax.fori_loop(0, PLANE * canv, canvas, 0)
+    each = fb_send.shape[2]
+    for d in range(9):
+        result = dot(grads[d], ye[...])
+        for part in range(parts):
+            fb_send[part, d] = result[part * each : (part + 1) * each].astype(BF16)
+    pl.semaphore_wait(barrier, parts + 1)
+    fb_copies = [part_copy(0, step, fb_send, fb_recv) for step in range(1, parts)]
+    for copy in fb_copies:
+        copy.start()
+
+    mate_copies = []
+    sides = (
+        (0, ((0, qa0, qa1, 0), (1, ga0, ga1, 1)), y_bit, keep_a, send_a, recv_a, y_mate),
+        (1, ((0, qb0, qb1, 0), (2, gb0, gb1, 1)), x_bit, keep_b, send_b, recv_b, x_mate),
+    )
+    for side, sources, bit, keep, send, recv, mate in sides:
+        for number, (device, own_ref, oth_ref, slot) in enumerate(sources):
+            loads[2 * side + slot].wait()
+            for n in range(canv):
+                rows_down(boxes_ref, device * canv + n, box_count, xbuf.at[slot], xd, n * PX)
+                cols_across(boxes_ref, device * canv + n, n, box_count, own_ref, oth_ref, lhs)
+                if number:
+                    select, count = members(
+                        boxes_ref, device * canv + n, box_count, lambda row: cells_ref[:, row : row + 1], (CELLS, PX), 1
+                    )
+                    sums = dot(select.astype(BF16), xbuf[slot, n * PX : (n + 1) * PX])
+                    pool_mate[side, n * CELLS : (n + 1) * CELLS] = (sums / count).astype(BF16)
+            if side == 0:
+                loads[2 + slot].start()
+            for d in range(9):
+                part = dot(lhs[d % 3], xd[d // 3])
+                acc[d] = part if number == 0 else acc[d] + part
+        split_out(9, bit, acc, keep, send)
+        mate_copies.append(mate_copy(side, send, recv, mate))
+        mate_copies[-1].start()
+
     levels = jnp.concatenate([lanes_ref[4:5, :]] * canv, axis=1)
-    size = owna.shape[0]
-    wide_by = poola.shape[1]
-    sides = ((0, owna, otha, poola, keepa, senda, 2), (1, ownb, othb, poolb, keepb, sendb, 1))
-    for side, own1, oth1, pool1, keep_ref, send_ref, bit_of in sides:
-        mine = slice(side * size, (side + 1) * size)
-        put_rows(lhs, 0, own_ref.at[mine], oth_ref.at[mine])
+    rows = canv * CELLS
+    sides = (
+        (0, za0, za1, zga0, zga1, y_bit, bkeep_a, bsend_a, brecv_a, y_mate),
+        (1, zb0, zb1, zgb0, zgb1, x_bit, bkeep_b, bsend_b, brecv_b, x_mate),
+    )
+    for side, own0, oth0, own1, oth1, bit, keep, send, recv, mate in sides:
+        put_rows(lhs, 0, own0, oth0)
         put_rows(lhs, 1, own1, oth1)
-        pool0 = pooled_ref[:, side * wide_by : (side + 1) * wide_by]
         for level in range(4):
-            left = [jnp.where(levels == level, lhs[source].astype(F32), 0.0).astype(BF16) for source in range(2)]
-            acc[level] = dot(left[0], pool0) + dot(left[1], pool1[...])
-        split_out(4, bit_of, acc, keep_ref, send_ref)
-
-
-def launch(kernel, in_specs, after=(), **rest):
+            left = [jnp.where(levels == level, lhs[k, :, :rows].astype(F32), 0.0).astype(BF16) for k in range(2)]
+            acc[level] = dot(left[0], pooled_ref[:, side * span : (side + 1) * span]) + dot(left[1], pool_mate[side])
+        split_out(4, bit, acc, keep, send)
+        mate_copies.append(mate_copy(2 + side, send, recv, mate))
+        mate_copies[-1].start()
+
+    part_copies = []
+
+    def pass_on(number, keep, recv, target):
+        mate_copies[number].wait_recv()
+
+        def add(d, carry):
+            for part in range(parts):
+                keep[part, d] = (keep[part, d].astype(F32) + recv[part, d].astype(F32)).astype(BF16)
+            return carry
+
+        lax.fori_loop(0, keep.shape[1], add, 0)
+        for step in range(1, parts):
+            part_copies.append(part_copy(1 + number, step, keep, target))
+            part_copies[-1].start()
+
+    for n in range(canv):
+        gate = pixel_gates(boxes_ref, n, box_count, (PX, CELLS), 0)
+        at = slice(n * PX, (n + 1) * PX)
+        for which, ref in ((chan, df0), (1 - chan, df1)):
+            into = pl.ds(pl.multiple_of(which * half, half), half)
+            df = ref[at].astype(F32)
+            xd[1, at, into] = ref[at]
+            xd[0, at, into] = (wide(gate(0, 1), half // CELLS) * pltpu.roll(df, PX - 1, 0)).astype(BF16)
+            xd[2, at, into] = (wide(gate(0, -1), half // CELLS) * pltpu.roll(df, 1, 0)).astype(BF16)
+
+    width = wbuf.shape[1]
+    tiles = wfx_any.shape[1] // width
+
+    def tile(t, carry):
+        tile_load(t).wait()
+
+        @pl.when(t + 1 < tiles)
+        def _():
+            tile_load(t + 1).start()
+
+        first = lax.rem(t, 2) * 9
+        for n in range(canv):
+            at = slice(n * PX, (n + 1) * PX)
+            gate = pixel_gates(boxes_ref, n, box_count, (PX, CELLS), 0)
+            total = None
+            for dy in range(3):
+                part = dot_nt(xd[0, at], wbuf[first + dy * 3])
+                for dx in range(1, 3):
+                    part = part + dot_nt(xd[dx, at], wbuf[first + dy * 3 + dx])
+                if dy != 1:
+                    part = wide(gate(1 - dy, 0), width // CELLS) * pltpu.roll(part, ((dy - 1) * CW) % PX, 0)
+                total = part if total is None else total + part
+            gx_ref[at, pl.ds(pl.multiple_of(t * width, width), width)] = total.astype(BF16)
+        return carry
+
+    lax.fori_loop(0, 1, tile, 0)
+    pass_on(0, keep_a, recv_a, zrecv_a)
+    lax.fori_loop(1, 3, tile, 0)
+    pass_on(1, keep_b, recv_b, zrecv_b)
+    lax.fori_loop(3, tiles, tile, 0)
+
+    wbr_load = pltpu.make_async_copy(wbr_any, wbuf.at[pl.ds(0, wbr_any.shape[0])], load_sem.at[4])
+    wbr_load.start()
+    wbr_load.wait()
+    per_level = wbr_any.shape[0] // 4
+    total = 0.0
+    for level in range(4):
+        w = wbuf[level * per_level : (level + 1) * per_level].reshape(per_level * width, 2 * half)
+        mine = []
+        for which, ref in ((0, dz0), (1, dz1)):
+            blocks = [
+                jnp.where(cells_ref[:, 4:5] == level, ref[m * CELLS : (m + 1) * CELLS].astype(F32), 0.0).astype(BF16)
+                for m in range(canv)
+            ]
+            mine.append(jnp.concatenate(blocks, axis=0))
+        first = jnp.where(chan == 0, mine[0].astype(F32), mine[1].astype(F32)).astype(BF16)
+        last = jnp.where(chan == 0, mine[1].astype(F32), mine[0].astype(F32)).astype(BF16)
+        total = total + dot_nt(jnp.concatenate([first, last], axis=1), w)
+    for m in range(canv):
+        _, _, high, across = by_box(boxes_ref, m, cells_ref[:, 0:1], box_count)
+        r0, r1, c0, c1 = member_bounds(lambda row: cells_ref[:, row : row + 1], high, across)
+        kept[m] = (total[m * CELLS : (m + 1) * CELLS] / ((r1 - r0) * (c1 - c0))).astype(BF16)
+    for n in range(canv):
+        at = slice(n * PX, (n + 1) * PX)
+        select, _ = members(boxes_ref, n, box_count, lambda row: lanes_ref[row : row + 1, :], (PX, CELLS), 0)
+        gx_ref[at] = (gx_ref[at].astype(F32) + dot(select.astype(BF16), kept[n])).astype(BF16)
+
+    pass_on(2, bkeep_a, brecv_a, bzrecv_a)
+    pass_on(3, bkeep_b, brecv_b, bzrecv_b)
+
+    def finish(copies, keep, recv, out, spot):
+        for copy in copies:
+            copy.wait_recv()
+
+        def add(d, carry):
+            total = keep[group, d].astype(F32)
+            for step in range(parts - 1):
+                total = total + recv[step, d].astype(F32)
+            out[d, :, spot] = total
+            return carry
+
+        lax.fori_loop(0, out.shape[0], add, 0)
+
+    first, last = slice(0, span), slice(span, 2 * span)
+    steps = parts - 1
+    finish(fb_copies, fb_send, fb_recv, out_fb, slice(0, out_fb.shape[2]))
+    finish(part_copies[:steps], keep_a, zrecv_a, out_fx, first)
+    finish(part_copies[steps : 2 * steps], keep_b, zrecv_b, out_fx, last)
+    finish(part_copies[2 * steps : 3 * steps], bkeep_a, bzrecv_a, out_br, first)
+    finish(part_copies[3 * steps :], bkeep_b, bzrecv_b, out_br, last)
+    for copy in fb_copies + mate_copies + part_copies:
+        copy.wait_send()
+
+
+def launch(kernel, in_specs, after=(), through=(), **rest):
     used = len(in_specs)
-    extra = len(after)
+    extra = len(after) + len(through)
+    if through:
+        outs = len(rest["out_specs"])
+        rest["out_specs"] = list(rest["out_specs"]) + [ANY_SPEC] * len(through)
+        rest["out_shape"] = list(rest["out_shape"]) + [jax.ShapeDtypeStruct(a.shape, a.dtype) for a in through]
+        rest["input_output_aliases"] = {used + len(after) + i: outs + i for i in range(len(through))}
+        after = tuple(after) + tuple(through)
+    else:
+        outs = 0
 
     def body(*refs):
-        kernel(*refs[:used], *refs[used + extra :])
+        refs = refs[:used] + refs[used + extra :]
+        kernel(*(refs[: used + outs] + refs[used + outs + len(through) :] if through else refs))
 
     cost = pl.CostEstimate(flops=COST_UNIT * COSTS.get(rest["name"], 10), bytes_accessed=0, transcendentals=0)
     call = pl.pallas_call(body, cost_estimate=cost, in_specs=list(in_specs) + [ANY_SPEC] * extra, **rest)
@@ -719,12 +851,9 @@
     def swap(array):
         return lax.ppermute(array, "chan", [(0, 1), (1, 0)])
 
-    def to_part(array, step):
-        return lax.ppermute(array, "dp", [(i, ((i // PLANE + step) % parts) * PLANE + i % PLANE) for i in range(dp)])
-
     flat = boxes.reshape(-1)
     flat_of = [flat] + [to_mate(flat, m) for m in (1, 2, 3)]
-    flat_mates = jnp.concatenate(flat_of[1:])
+    flat_all = jnp.concatenate(flat_of)
 
     pooled, lifts, z_own, z_send, x_first, x_last = launch(
         functools.partial(pool_kernel, canv, box_count),
@@ -766,8 +895,9 @@
         name="branch_sums",
     )(cells, z_own, z_got)
     z_total = dp_sum(z_part, dp, 0)
-    y, z_norm, z_act = launch(
+    y, z_norm, z_act, x_first, x_last = launch(
         functools.partial(branch_act_kernel, canv, rows_all),
+        through=(x_first, x_last),
         in_specs=[VMEM_SPEC] * 5,
         out_specs=[VMEM_SPEC] * 3,
         out_shape=[shaped((rows, bw), BF16), shaped((rows, bw), F32), shaped((rows, bw), F32)],
@@ -780,27 +910,27 @@
 
     f_own, f_send = launch(
         functools.partial(join_kernel, canv, box_count),
-        grid=(9,),
+        grid=(3,),
         in_specs=[
             SMEM_SPEC,
             whole(cells.shape),
             whole((pixels, cin)),
             whole((rows, bw)),
-            pl.BlockSpec((canv, PX, CELLS), lambda i: (0, 0, i)),
-            pl.BlockSpec((1, cin, mid), lambda i: (i, 0, 0)),
-            pl.BlockSpec((1, 4, bw, mid), lambda i: (i, 0, 0, 0)),
+            whole((canv, PX, 9 * CELLS)),
+            pl.BlockSpec((3, 1, cin, mid), lambda i: (0, i, 0, 0)),
+            pl.BlockSpec((3, 1, 4, bw, mid), lambda i: (0, i, 0, 0, 0)),
         ],
         out_specs=[whole((pixels, half)), whole((pixels, half))],
         out_shape=[shaped((pixels, half), F32), shaped((pixels, half), BF16)],
         scratch_shapes=[
-            pltpu.VMEM((3, canv, PX, mid), F32),
-            pltpu.VMEM((3, canv, PX, CELLS), F32),
-            pltpu.VMEM((canv, PX + 2 * CW, mid), F32),
+            pltpu.VMEM((3, pixels, cin), BF16),
             pltpu.VMEM((rows, 4 * bw), BF16),
+            pltpu.VMEM((canv, 9 * CELLS, mid), BF16),
+            pltpu.VMEM((canv, PX, mid), F32),
         ],
         compiler_params=params(),
         name="join",
-    )(flat, cells, features, y, lifts, w_fx, w_fb)
+    )(flat, cells, features, y, lifts, w_fx.reshape(3, 3, cin, mid), w_fb.reshape(3, 3, 4, bw, mid))
     f_got = swap(f_send)
     by_canvas = pl.BlockSpec((PX, half), lambda i: (i, 0))
     f, f_part = launch(
@@ -863,22 +993,21 @@
         functools.partial(branch_back_kernel, canv),
         grid=(9,),
         in_specs=[
-            SMEM_SPEC,
             whole(cells.shape),
             whole(lanes.shape),
             half_rows,
             half_rows,
-            pl.BlockSpec((canv, PX, CELLS), lambda i: (0, 0, i)),
+            whole((canv, PX, 9 * CELLS)),
             pl.BlockSpec((1, 4, bw, mid), lambda i: (i, 0, 0, 0)),
             whole((rows, bw)),
             whole((rows, bw)),
         ],
         out_specs=[whole((rows, bw)), whole((8, bw))],
         out_shape=[shaped((rows, bw), F32), shaped((8, bw), F32)],
-        scratch_shapes=[pltpu.VMEM((4 * bw, rows), F32)],
+        scratch_shapes=[pltpu.VMEM((4 * bw, rows), F32), pltpu.VMEM((9, mid, rows), BF16)],
         compiler_params=params(),
         name="branch_back",
-    )(flat, cells, lanes, pack, pack_other, lifts, w_fb, z_norm, z_act)
+    )(cells, lanes, pack, pack_other, lifts, w_fb, z_norm, z_act)
     da_total = dp_sum(da_part, dp, 3, (other_a, other_b, other_d))
     dz, zpack, zsend_a, zsend_b = launch(
         functools.partial(branch_dz_kernel, canv, rows_all, each),
@@ -897,147 +1026,92 @@
     zgot_a, zgot_b = to_mate(zsend_a, 1), to_mate(zsend_b, 2)
     dz_got, zpack_other, zother_a, zother_b = swap(dz), swap(zpack), swap(zgot_a), swap(zgot_b)
 
-    steps = PLANE * canv
-    lifts_mates = launch(
-        functools.partial(lifts_kernel, box_count),
-        grid=(steps - canv,),
-        in_specs=[SMEM_SPEC, whole(lanes.shape)],
-        out_specs=pl.BlockSpec((1, PX, 9 * CELLS), lambda i: (i, 0, 0)),
-        out_shape=shaped((steps - canv, PX, 9 * CELLS), BF16),
-        compiler_params=params(),
-        name="lifts",
-    )(flat_mates, lanes)
-    quarter_at = [pl.BlockSpec((quarter, pixels), lambda i, at=at: (at, 0)) for at in (2, 0, 0)]
-    fb_parts = launch(
-        functools.partial(wgrad_fb_kernel, canv),
-        grid=(9,),
-        in_specs=[
-            whole(cells.shape),
-            quarter_at[0],
-            quarter_at[0],
-            quarter_at[1],
-            quarter_at[1],
-            quarter_at[2],
-            quarter_at[2],
-            whole((quarter // 2, pixels)),
-            whole((quarter // 2, pixels)),
-            pl.BlockSpec((canv, PX, CELLS), lambda i: (0, 0, i)),
-            pl.BlockSpec((steps - canv, PX, CELLS), lambda i: (0, 0, i)),
-            whole((steps * CELLS, bw)),
-        ],
-        out_specs=pl.BlockSpec((parts, 1, each, 4 * bw), lambda i: (0, i, 0, 0)),
-        out_shape=shaped((parts, 9, each, 4 * bw), BF16),
-        scratch_shapes=[pltpu.VMEM((steps * CELLS, 4 * bw), BF16), pltpu.VMEM((PLANE, cols, pixels), BF16)],
-        compiler_params=params(),
-        name="wgrad_fb",
-        after=(da_total,),
-    )(cells, pack, pack_other, got_a, other_a, got_b, other_b, got_d, other_d, lifts, lifts_mates, y_all)
-
     span = cin // 2
-
-    def wgrad(side, bit_of, boxes_mate, got, other, x_got, after):
-        own = pl.BlockSpec((quarter, pixels), lambda i: (2 + side, 0))
-        return launch(
-            functools.partial(wgrad_kernel, canv, box_count, bit_of),
-            grid=(1,),
-            in_specs=[
-                SMEM_SPEC,
-                SMEM_SPEC,
-                whole(cells.shape),
-                own,
-                own,
-                whole((quarter, pixels)),
-                whole((quarter, pixels)),
-                pl.BlockSpec((pixels, span), lambda i: (0, side)),
-                whole((pixels, span)),
-            ],
-            out_specs=[whole((9, 2, quarter // 2, span))] * 2 + [whole((rows, span))],
-            out_shape=[shaped((9, 2, quarter // 2, span), BF16)] * 2 + [shaped((rows, span), BF16)],
-            scratch_shapes=[
-                pltpu.VMEM((9, half, span), F32),
-                pltpu.VMEM((3, half, pixels), BF16),
-                pltpu.VMEM((3, pixels + 2 * CW, span), BF16),
-            ],
-            compiler_params=params(),
-            name="wgrad_fx%d" % side,
-            after=after,
-        )(flat, boxes_mate, cells, pack, pack_other, got, other, features, x_got)
-
-    keep_fa, send_fa, pool_a = wgrad(0, 2, flat_of[1], got_a, other_a, x_mate, (fb_parts,))
-    keep_fb, send_fb, pool_b = wgrad(1, 1, flat_of[2], got_b, other_b, y_mate, (send_fa,))
-    quarter_shape = (4, 2, quarter // 2, span)
-    keep_ba, send_ba, keep_bb, send_bb = launch(
-        functools.partial(wgrad_br_kernel, canv),
-        in_specs=[VMEM_SPEC] * 10,
-        out_specs=[VMEM_SPEC] * 4,
-        out_shape=[shaped(quarter_shape, BF16)] * 4,
-        scratch_shapes=[pltpu.VMEM((4, half, span), F32), pltpu.VMEM((2, half, rows), BF16)],
-        compiler_params=params(),
-        name="wgrad_br",
-    )(lanes, zpack, zpack_other, zgot_a, zother_a, zgot_b, zother_b, pooled, pool_a, pool_b)
-
-    def across_groups(pick):
-        group = me // PLANE
-        total = pick(group)
-        for step in range(1, parts):
-            total = total + to_part(pick((group + step) % parts).astype(BF16), step).astype(F32)
-        return total
-
-    def through_mate(keep, send, mate):
-        got = to_mate(send, mate)
-        shape = (keep.shape[0], parts, each, span)
-
-        def pick(part):
-            mine = [lax.dynamic_index_in_dim(a.reshape(shape), part, 1, keepdims=False) for a in (keep, got)]
-            return mine[0].astype(F32) + mine[1].astype(F32)
-
-        return across_groups(pick)
-
-    sum_fb = across_groups(lambda part: lax.dynamic_index_in_dim(fb_parts, part, 0, keepdims=False).astype(F32))
-    out_fb = jnp.transpose(sum_fb.reshape(9, each, 4, bw), (0, 2, 3, 1))
-    out_fx = [through_mate(keep_fa, send_fa, 2), through_mate(keep_fb, send_fb, 1)]
-    out_fx = jnp.transpose(jnp.concatenate(out_fx, 2), (0, 2, 1))
-    out_br = [through_mate(keep_ba, send_ba, 2), through_mate(keep_bb, send_bb, 1)]
-    out_br = jnp.transpose(jnp.concatenate(out_br, 2), (0, 2, 1))
-
-    dx = launch(
-        functools.partial(dx_kernel, canv, box_count),
-        grid=(9,),
-        in_specs=[
-            SMEM_SPEC,
-            whole((pixels, half)),
-            whole((pixels, half)),
-            pl.BlockSpec((1, cin, mid), lambda i: (i, 0, 0)),
-        ],
-        out_specs=whole((pixels, cin)),
-        out_shape=shaped((pixels, cin), BF16),
-        scratch_shapes=[
-            pltpu.VMEM((canv, PX, cin), F32),
-            pltpu.VMEM((3, canv, PX, CELLS), BF16),
-            pltpu.VMEM((2, 3, canv, PX + 2 * CW, half), BF16),
-        ],
-        compiler_params=params(),
-        name="dx",
-        after=(send_bb,),
-    )(flat, df, df_got, w_fx)
-    grad_features = launch(
-        functools.partial(grad_x_kernel, canv, box_count),
-        grid=(canv,),
+    bundle = quarter // 2
+    tile = cin // 4
+
+    def quarter_at(at):
+        return pl.BlockSpec((quarter, pixels), lambda i: (at, 0))
+
+    def zquarter_at(at):
+        return pl.BlockSpec((quarter, rows), lambda i: (at, 0))
+
+    def buffers(count, width):
+        return [
+            pltpu.VMEM((parts, count, each, width), BF16),
+            pltpu.VMEM((parts, count, each, width), BF16),
+            pltpu.VMEM((parts, count, each, width), BF16),
+            pltpu.VMEM((parts - 1, count, each, width), BF16),
+        ]
+
+    grad_features, sum_fx, sum_fb, sum_br = launch(
+        functools.partial(tail_kernel, canv, box_count),
+        grid=(1,),
         in_specs=[
             SMEM_SPEC,
             whole(lanes.shape),
             whole(cells.shape),
-            whole((rows, bw)),
-            whole((rows, bw)),
-            whole(w_branch.shape),
-            pl.BlockSpec((PX, cin), lambda i: (i, 0)),
-        ],
-        out_specs=pl.BlockSpec((PX, cin), lambda i: (i, 0)),
-        out_shape=shaped((pixels, cin), BF16),
-        scratch_shapes=[pltpu.VMEM((canv, CELLS, cin), BF16)],
-        compiler_params=params(),
-        name="grad_x",
-    )(flat, lanes, cells, dz, dz_got, w_branch, dx)
+            quarter_at(2),
+            quarter_at(2),
+            quarter_at(3),
+            quarter_at(3),
+        ]
+        + [whole((quarter, pixels))] * 4
+        + [whole((bundle, pixels))] * 2
+        + [whole((PLANE * rows, bw)), whole((rows, cin))]
+        + [zquarter_at(0), zquarter_at(0), zquarter_at(1), zquarter_at(1)]
+        + [whole((quarter, rows))] * 4
+        + [whole((rows, bw))] * 2
+        + [whole((pixels, half))] * 2
+        + [ANY_SPEC] * 5,
+        out_specs=[
+            whole((pixels, cin)),
+            whole((9, each, cin)),
+            whole((9, each, 4 * bw)),
+            whole((4, each, cin)),
+        ],
+        out_shape=[
+            shaped((pixels, cin), BF16),
+            shaped((9, each, cin), F32),
+            shaped((9, each, 4 * bw), F32),
+            shaped((4, each, cin), F32),
+        ],
+        scratch_shapes=[
+            pltpu.VMEM((PLANE, cols, pixels), BF16),
+            pltpu.VMEM((PX, 9 * CELLS), BF16),
+            pltpu.VMEM((9, cols, PLANE * rows), BF16),
+            pltpu.VMEM((2, pixels, span), BF16),
+            pltpu.VMEM((18, tile, mid), BF16),
+            pltpu.VMEM((3, pixels, mid), BF16),
+            pltpu.VMEM((3, half, pixels), BF16),
+            pltpu.VMEM((9, half, span), F32),
+            pltpu.VMEM((2, rows, span), BF16),
+            pltpu.VMEM((canv, CELLS, cin), BF16),
+            pltpu.VMEM((parts, 9, each, 4 * bw), BF16),
+            pltpu.VMEM((parts - 1, 9, each, 4 * bw), BF16),
+        ]
+        + buffers(9, span)
+        + buffers(9, span)
+        + buffers(4, span)
+        + buffers(4, span)
+        + [
+            pltpu.SemaphoreType.DMA((5,)),
+            pltpu.SemaphoreType.DMA((2,)),
+            pltpu.SemaphoreType.DMA((4,)),
+            pltpu.SemaphoreType.DMA((4,)),
+            pltpu.SemaphoreType.DMA((5 * (parts - 1),)),
+            pltpu.SemaphoreType.DMA((5 * (parts - 1),)),
+        ],
+        compiler_params=pltpu.CompilerParams(vmem_limit_bytes=62 * 2**20, collective_id=4, has_side_effects=True),
+        name="tail",
+    )(
+        flat_all, lanes, cells, pack, pack_other, pack, pack_other, got_a, other_a, got_b, other_b, got_d, other_d,
+        y_all, pooled, zpack, zpack_other, zpack, zpack_other, zgot_a, zother_a, zgot_b, zother_b, dz, dz_got, df, df_got,
+        features, x_mate, y_mate, w_fx, w_branch.reshape(16, tile, br),
+    )
+    out_fx = jnp.transpose(sum_fx, (0, 2, 1))
+    out_fb = jnp.transpose(sum_fb.reshape(9, each, 4, bw), (0, 2, 3, 1))
+    out_br = jnp.transpose(sum_br, (0, 2, 1))
 
     small = db_total[:2]
     small_got = swap(small)

time: 455 us -> 358 us (0.79)
  waiting for transfers between devices: 88.6 us -> 27.7 us
  starting transfers between devices: 48.9 us -> 15.4 us
  other arithmetic: 9.12 us -> 1.48 us
  local copies, waits for them, and re-layouts: 12.8 us -> 18.8 us
    ppermute x15 -> x0, waiting for transfers between devices: 45.5 us -> none  [to_part(): lax.ppermute(array, 'dp', [(i, (i // PLANE + step) % parts * PLANE + i %...]
    ppermute x15 -> x0, starting transfers between devices: 25.3 us -> none  [to_part(): lax.ppermute(array, 'dp', [(i, (i // PLANE + step) % parts * PLANE + i %...]
    ppermute x17 -> x13, waiting for transfers between devices: 42.8 us -> 25.2 us  [to_mate(): return lax.ppermute(array, 'dp', [(i, i ^ mate) for i in range(dp)])]
    ppermute x17 -> x13, starting transfers between devices: 21 us -> 13.7 us  [to_mate(): return lax.ppermute(array, 'dp', [(i, i ^ mate) for i in range(dp)])]
    unnamed x71 -> x62, local copies, waits for them, and re-layouts: 8.21 us -> 13.2 us
    pallas_call x20 -> x14, Pallas kernels: 275 us -> 275 us  [launch(): return lambda *operands: call(*operands, *after)]
  transfers between devices with their start and end apart: 46 -> 27, of which waited for: 17 -> 13; matrix products, arithmetic and copies ran while one was open for 3% -> 3% of each run, Pallas kernels for 51% -> 62%
where the time goes in v2:
time: 358 us; the launch traced here: 353 us
  Pallas kernels  275 us (77%)
  waiting for transfers between devices  27.7 us (8%)
  local copies, waits for them, and re-layouts  18.8 us (5%)
  starting transfers between devices  15.4 us (4%)
  between operations  14.6 us (4%)
    pallas_call x14, Pallas kernels, launch(): return lambda *operands: call(*operands, *after)  275 us
    ppermute x13, waiting for transfers between devices, to_mate(): return lax.ppermute(array, 'dp', [(i, i ^ mate) for i in range(dp)])  25.2 us
    ppermute x13, starting transfers between devices, to_mate(): return lax.ppermute(array, 'dp', [(i, i ^ mate) for i in range(dp)])  13.7 us
    unnamed x62, local copies, waits for them, and re-layouts  13.2 us
  transfers between devices with their start and end apart: 27, of which 13 were waited for; matrix products, arithmetic and copies ran while one was open for 3% of the time, Pallas kernels for 62%

profile of v2, /device:TPU:8, one launch (start us, length us, event | category | flops | bytes accessed | tf_op | source)
XLA Modules:
  0.0 353.4 jit_solution(978857285266197044)
XLA Ops:
  7.2 1.3 reshape.44.refs_0_
  8.5 9.9 %pool.1 = (bf16[384,1024]{1,0:T(8,128)(2,1)}, bf16[3,512,1152]{2,1,0:T(8,128)(2,1)}, f32[384,256]{1,0:T(8,128)}, bf16[384,256]{1,0:T(8,128)(2,1)}, bf16[1536,512]{1,0:T(8,128)(2,1)}, /*index=5*/bf16[1536,512]{1,0:T(8,128)(2,1)}) custom-call(s32[24]{0:T(128)} %reshape.44.refs_0_, f32[8,128]{1,0:T(8,128)} %constant.16.clone.refs_1_, ...), custom_call_target="tpu_custom_call" | custom-call | flops 12000000000 | tf_op jit(solution)/shard_map/pool/pallas_call | solution.py:817
  18.4 1.6 collective-permute-done.refs_2_
  20.1 0.7 copy-done.21
  20.7 2.0 branch_sums.1
  22.8 9.8 %dp_sum0.1.refs_2_.refs_3_ = f32[8,256]{1,0:T(8,128)} custom-call(f32[8,256]{1,0:T(8,128)} %get-tuple-element.50.refs_0_), custom_call_target="tpu_custom_call" | custom-call | flops 10000000000 | tf_op jit(solution)/shard_map/dp_sum0/pallas_call | solution.py:817
  32.6 2.5 branch_act.1
  35.1 1.6 collective-permute-start.2
  36.7 1.7 collective-permute-start.3
  38.4 44.0 %join.1 = (f32[1536,256]{1,0:T(8,128)}, bf16[1536,256]{1,0:T(8,128)(2,1)}) custom-call(s32[24]{0:T(128)} %reshape.44.refs_0_, f32[128,128]{1,0:T(8,128)} %constant.17.clone.refs_2_.refs_0_.refs_1_, bf16[1536,1024]{1,0:T(8,128)(2,1)} %refs_27_.1, bf16[384,256]{1,0:T(8,128)(2,1)} %get-tuple-element.53.refs_3_, ...), custom_call_target="tpu_custom_call" | custom-call | flops 41999998976 | tf_op jit(solution)/shard_map/join/pallas_call | solution.py:817
  82.5 0.6 collective-permute-start.4
  83.1 0.8 copy.32.refs_5_
  84.0 1.2 copy.33.refs_6_
  85.1 0.2 collective-permute-start.5
  85.4 4.5 %collective-permute-done.4 = bf16[384,256]{1,0:T(8,128)(2,1)S(1)} collective-permute-done((bf16[384,256]{1,0:T(8,128)(2,1)S(1)}, bf16[384,256]{1,0:T(8,128)(2,1)S(1)}, u32[]{:S(2)}, u32[]{:S(2)}) %collective-permute-start.4) | collective-permute-done | bytes 196640 | tf_op jit(solution)/shard_map/ppermute | solution.py:849
  89.8 0.2 collective-permute-start.6
  90.0 2.1 collective-permute-done.5
  92.1 5.1 %collective-permute-done.6 = bf16[384,256]{1,0:T(8,128)(2,1)S(1)} collective-permute-done((bf16[384,256]{1,0:T(8,128)(2,1)S(1)}, bf16[384,256]{1,0:T(8,128)(2,1)S(1)}, u32[]{:S(2)}, u32[]{:S(2)}) %collective-permute-start.6) | collective-permute-done | bytes 196640 | tf_op jit(solution)/shard_map/ppermute | solution.py:849
  97.2 0.8 copy-done.9
  98.1 0.5 copy-done.14
  98.6 3.6 %join_sums.1 = (f32[1536,256]{1,0:T(8,128)}, f32[8,256]{1,0:T(8,128)}) custom-call(s32[24]{0:T(128)} %reshape.44.refs_0_, f32[1536,256]{1,0:T(8,128)} %get-tuple-element.55.refs_1_, bf16[1536,256]{1,0:T(8,128)(2,1)} %collective-permute-done.1.refs_2_, bf16[1536,512]{1,0:T(8,128)(2,1)} %copy-done.14, ...), custom_call_target="tpu_custom_call" | custom-call | flops 4000000000 | tf_op jit(solution)/shard_map/join_sums/pallas_call | solution.py:817
  102.2 9.3 %dp_sum1.1.refs_2_.refs_3_ = f32[8,256]{1,0:T(8,128)} custom-call(f32[8,256]{1,0:T(8,128)} %get-tuple-element.60.refs_0_), custom_call_target="tpu_custom_call" | custom-call | flops 10000000000 | tf_op jit(solution)/shard_map/dp_sum1/pallas_call | solution.py:817
  111.6 4.9 %head.1 = (bf16[1536,150]{1,0:T(8,128)(2,1)}, f32[1536,256]{1,0:T(8,128)}, f32[8,256]{1,0:T(8,128)}, f32[256,150]{1,0:T(8,128)}) custom-call(s32[24]{0:T(128)} %reshape.44.refs_0_, f32[1536,256]{1,0:T(8,128)} %get-tuple-element.59.refs_1_, f32[8,256]{1,0:T(8,128)} %dp_sum1.1.refs_2_.refs_3_, f32[1,512]{1,0:T(1,128)} %bitcast.28, f32[1,512]{1,0:T(1,128)} %bitcast.27, ...), custom_call_target="tpu_custom_call" | custom-call | flops 5000000000 | tf_op jit(solution)/shard_map/head/pallas_call | solution.py:817
  116.5 9.6 %dp_sum2.1.refs_4_ = f32[8,256]{1,0:T(8,128)} custom-call(f32[8,256]{1,0:T(8,128)} %get-tuple-element.63.refs_0_), custom_call_target="tpu_custom_call" | custom-call | flops 10000000000 | tf_op jit(solution)/shard_map/dp_sum2/pallas_call | solution.py:817
  126.1 5.2 %join_grad.1 = (bf16[1536,256]{1,0:T(8,128)(2,1)}, bf16[512,1536]{1,0:T(8,128)(2,1)}, bf16[128,1536]{1,0:T(8,128)(2,1)}, bf16[128,1536]{1,0:T(8,128)(2,1)}, bf16[64,1536]{1,0:T(8,128)(2,1)}) custom-call(s32[24]{0:T(128)} %reshape.44.refs_0_, f32[1536,256]{1,0:T(8,128)} %get-tuple-element.59.refs_1_, f32[1536,256]{1,0:T(8,128)} %get-tuple-element.62.refs_2_, ...), custom_call_target="tpu_custom_call" | custom-call | flops 5000000000 | tf_op jit(solution)/shard_map/join_grad/pallas_call | solution.py:817
  131.4 1.1 collective-permute-start.10
  132.5 1.2 collective-permute-start.9
  133.7 1.2 collective-permute-start.8
  135.0 0.2 copy.34
  135.3 0.6 collective-permute-done.10
  135.9 0.2 collective-permute-done.9
  136.1 1.2 collective-permute-done.8
  137.3 0.7 pad_add_fusion.refs_0_
  137.9 1.2 collective-permute-start.12
  139.1 0.8 collective-permute-start.14
  140.2 0.6 slice.23
  140.9 0.2 collective-permute-done.25
  141.1 1.4 collective-permute-start.16
  142.6 0.6 pad_maximum_fusion
  143.2 9.5 %collective-permute-done.16.refs_11_ = bf16[64,1536]{1,0:T(8,128)(2,1)S(1)} collective-permute-done((bf16[64,1536]{1,0:T(8,128)(2,1)}, bf16[64,1536]{1,0:T(8,128)(2,1)S(1)}, u32[]{:S(2)}, u32[]{:S(2)}) %collective-permute-start.16) | collective-permute-done | bytes 196640 | tf_op jit(solution)/shard_map/ppermute | solution.py:849
  152.7 0.5 collective-permute-start.17
  153.2 0.3 collective-permute-done.14.refs_9_
  153.5 0.5 collective-permute-start.15
  154.1 0.3 copy.35
  154.3 15.8 %branch_back.1 = (f32[384,256]{1,0:T(8,128)}, f32[8,256]{1,0:T(8,128)}) custom-call(f32[128,128]{1,0:T(8,128)} %constant.17.clone.refs_2_.refs_0_.refs_1_, f32[8,128]{1,0:T(8,128)} %constant.16.clone.refs_1_, bf16[512,1536]{1,0:T(8,128)(2,1)} %get-tuple-element.64.refs_2_.refs_3_.refs_5_, bf16[512,1536]{1,0:T(8,128)(2,1)} %collective-permute-done.11.refs_3_.refs_4_.refs_6_, ...), custom_call_target="tpu_custom_call" | custom-call | flops 16000000000 | tf_op jit(solution)/shard_map/branch_back/pallas_call | solution.py:817
  170.2 0.7 copy-done.16
  170.9 10.2 %dp_sum3.1.refs_4_ = f32[8,256]{1,0:T(8,128)} custom-call(f32[8,256]{1,0:T(8,128)} %get-tuple-element.72.refs_0_, bf16[128,1536]{1,0:T(8,128)(2,1)} %copy-done.16, bf16[128,1536]{1,0:T(8,128)(2,1)} %collective-permute-done.15.refs_2_.refs_10_, bf16[64,1536]{1,0:T(8,128)(2,1)} %collective-permute-done.17.refs_3_.refs_12_), custom_call_target="tpu_custom_call" | custom-call | flops 10000000000 | tf_op jit(solution)/shard_map/dp_sum3/pallas_call | solution.py:817
  181.2 2.6 branch_dz.1
  183.7 1.0 collective-permute-start.19
  184.7 1.3 collective-permute-start.21
  186.1 0.2 add_convert_fusion
  186.3 1.0 copy.38
  187.3 0.5 collective-permute-start.23
  187.8 0.7 collective-permute-done.19.refs_19_
  188.6 1.0 collective-permute-done.21.refs_21_
  189.6 0.6 fusion.1
  190.2 0.6 collective-permute-done.22.refs_22_
  190.9 0.6 copy-done.25
  191.6 145.8 %tail.1 = (bf16[1536,1024]{1,0:T(8,128)(2,1)}, f32[9,32,1024]{2,1,0:T(8,128)}, f32[9,32,1024]{2,1,0:T(8,128)}, f32[4,32,1024]{2,1,0:T(8,128)}) custom-call(s32[96]{0:T(128)} %pad_add_fusion.refs_0_, f32[8,128]{1,0:T(8,128)} %constant.16.clone.refs_1_, f32[128,128]{1,0:T(8,128)} %constant.17.clone.refs_2_.refs_0_.refs_1_, ...), custom_call_target="tpu_custom_call" | custom-call | flops 10000000000 | tf_op jit(solution)/shard_map/tail/pallas_call | solution.py:817
  337.4 2.5 copy.41
  339.8 4.0 %copy.52 = bf16[1536,1024]{1,0:T(8,128)(2,1)} copy(bf16[1536,1024]{1,0:T(8,128)(2,1)} %get-tuple-element.123) | data formatting | bytes 6291456
  343.8 0.8 copy.53
  344.6 1.0 copy.54
  345.6 0.7 copy.55
  (82 shorter events, 0.8 us)
Async XLA Ops:
  7.2 332.7 %all-reduce.2.cloned.1.call-start = ((), (), s32[]{:S(2)}) async-start(), calls=%async_computation | async-start | bytes 622592 | tf_op jit(solution)/shard_map/psum | solution.py:1120
  18.4 1.7 collective-permute-start
  20.1 0.7 copy-start.21
  35.1 62.1 %collective-permute-start.2 = (bf16[1536,512]{1,0:T(8,128)(2,1)}, bf16[1536,512]{1,0:T(8,128)(2,1)S(1)}, u32[]{:S(2)}, u32[]{:S(2)}) collective-permute-start(bf16[1536,512]{1,0:T(8,128)(2,1)} %get-tuple-element.57), channel_id=1, source_target_pairs={{0,2},{2,0},{4,6},{6,4},{8,10},{10,8},{12,14},{14,12},{16,18},{18,... | collective-permute-start | bytes 4718600 | tf_op jit(solution)/shard_map/ppermute | solution.py:849
  36.7 60.5 %collective-permute-start.3 = (bf16[1536,512]{1,0:T(8,128)(2,1)}, bf16[1536,512]{1,0:T(8,128)(2,1)}, u32[]{:S(2)}, u32[]{:S(2)}) collective-permute-start(bf16[1536,512]{1,0:T(8,128)(2,1)} %get-tuple-element.58), channel_id=1, source_target_pairs={{0,4},{2,6},{4,0},{6,2},{8,12},{10,14},{12,8},{14,10},{16,20},{18,... | collective-permute-start | bytes 4718600 | tf_op jit(solution)/shard_map/ppermute | solution.py:849
  38.4 44.1 %copy-start.7 = (bf16[384,256]{1,0:T(8,128)(2,1)S(1)}, bf16[384,256]{1,0:T(8,128)(2,1)}, u32[]{:S(2)}) copy-start(bf16[384,256]{1,0:T(8,128)(2,1)} %get-tuple-element.53.refs_3_) | copy-start | bytes 589828
  38.4 44.7 %copy-start.8 = (bf16[512,150]{0,1:T(8,128)(2,1)S(1)}, bf16[512,150]{0,1:T(8,128)(2,1)}, u32[]{:S(2)}) copy-start(bf16[512,150]{0,1:T(8,128)(2,1)} %param.23) | copy-start | bytes 460804
  38.4 45.6 %copy-start.4 = (bf16[1536,150]{0,1:T(8,128)(2,1)S(1)}, bf16[1536,150]{0,1:T(8,128)(2,1)}, u32[]{:S(2)}) copy-start(bf16[1536,150]{0,1:T(8,128)(2,1)} %param.25) | copy-start | bytes 1382404
  82.4 14.8 %collective-permute-start.1 = (bf16[1536,256]{1,0:T(8,128)(2,1)}, bf16[1536,256]{1,0:T(8,128)(2,1)}, u32[]{:S(2)}, u32[]{:S(2)}) collective-permute-start(bf16[1536,256]{1,0:T(8,128)(2,1)} %get-tuple-element.56), channel_id=1, source_target_pairs={{0,1},{1,0},{2,3},{3,2},{4,5},{5,4},{6,7},{7,6},{8,9},{9,8},{10,11... | collective-permute-start | bytes 2359304 | tf_op jit(solution)/shard_map/ppermute | solution.py:852
  82.5 7.3 %collective-permute-start.4 = (bf16[384,256]{1,0:T(8,128)(2,1)S(1)}, bf16[384,256]{1,0:T(8,128)(2,1)S(1)}, u32[]{:S(2)}, u32[]{:S(2)}) collective-permute-start(bf16[384,256]{1,0:T(8,128)(2,1)S(1)} %copy-done.7), channel_id=1, source_target_pairs={{0,2},{2,0},{4,6},{6,4},{8,10},{10,8},{12,14},{14,12},{16,18},{18,... | collective-permute-start | bytes 589832 | tf_op jit(solution)/shard_map/ppermute | solution.py:849
  85.1 7.0 %collective-permute-start.5 = (bf16[384,256]{1,0:T(8,128)(2,1)S(1)}, bf16[384,256]{1,0:T(8,128)(2,1)S(1)}, u32[]{:S(2)}, u32[]{:S(2)}) collective-permute-start(bf16[384,256]{1,0:T(8,128)(2,1)S(1)} %copy-done.7), channel_id=1, source_target_pairs={{0,4},{2,6},{4,0},{6,2},{8,12},{10,14},{12,8},{14,10},{16,20},{18,... | collective-permute-start | bytes 589832 | tf_op jit(solution)/shard_map/ppermute | solution.py:849
  89.8 7.3 %collective-permute-start.6 = (bf16[384,256]{1,0:T(8,128)(2,1)S(1)}, bf16[384,256]{1,0:T(8,128)(2,1)S(1)}, u32[]{:S(2)}, u32[]{:S(2)}) collective-permute-start(bf16[384,256]{1,0:T(8,128)(2,1)S(1)} %copy-done.7), channel_id=1, source_target_pairs={{0,6},{2,4},{4,2},{6,0},{8,14},{10,12},{12,10},{14,8},{16,22},{18,... | collective-permute-start | bytes 589832 | tf_op jit(solution)/shard_map/ppermute | solution.py:849
  97.2 0.9 copy-start.9
  97.2 1.4 copy-start.14
  126.1 5.3 %copy-start.12 = (s32[24]{0:T(128)S(1)}, s32[24]{0:T(128)}, u32[]{:S(2)}) copy-start(s32[24]{0:T(128)} %reshape.44.refs_0_) | copy-start | bytes 292
  126.1 8.9 %copy-start = (bf16[1536,150]{1,0:T(8,128)(2,1)S(1)}, bf16[1536,150]{1,0:T(8,128)(2,1)}, u32[]{:S(2)}) copy-start(bf16[1536,150]{1,0:T(8,128)(2,1)} %get-tuple-element.61) | copy-start | bytes 1382404
  126.1 11.8 %copy-start.11 = (f32[8,256]{1,0:T(8,128)S(1)}, f32[8,256]{1,0:T(8,128)}, u32[]{:S(2)}) copy-start(f32[8,256]{1,0:T(8,128)} %dp_sum2.1.refs_4_) | copy-start | bytes 24580
  126.1 13.9 %copy-start.6 = (f32[256,150]{1,0:T(8,128)S(1)}, f32[256,150]{1,0:T(8,128)}, u32[]{:S(2)}) copy-start(f32[256,150]{1,0:T(8,128)} %get-tuple-element.82) | copy-start | bytes 460804
  131.3 21.4 %copy-start.15 = (bf16[1536,256]{1,0:T(8,128)(2,1)S(1)}, bf16[1536,256]{1,0:T(8,128)(2,1)}, u32[]{:S(2)}) copy-start(bf16[1536,256]{1,0:T(8,128)(2,1)} %get-tuple-element.77.refs_25_) | copy-start | bytes 2359300
  131.3 23.0 %collective-permute-start.11 = (bf16[512,1536]{1,0:T(8,128)(2,1)}, bf16[512,1536]{1,0:T(8,128)(2,1)}, u32[]{:S(2)}, u32[]{:S(2)}) collective-permute-start(bf16[512,1536]{1,0:T(8,128)(2,1)} %get-tuple-element.64.refs_2_.refs_3_.refs_5_), channel_id=1, source_target_pairs={{0,1},{1,0},{2,3},{3,2},{4,5},{5,4},{6,7},{7,6},{8,9},{9,8},{10,11... | collective-permute-start | bytes 4718600 | tf_op jit(solution)/shard_map/ppermute | solution.py:852
  131.4 4.5 %collective-permute-start.10 = (s32[24]{0:T(128)S(1)}, s32[24]{0:T(128)S(1)}, u32[]{:S(2)}, u32[]{:S(2)}) collective-permute-start(s32[24]{0:T(128)S(1)} %copy-done.12), channel_id=1, source_target_pairs={{0,6},{2,4},{4,2},{6,0},{8,14},{10,12},{12,10},{14,8},{16,22},{18,... | collective-permute-start | bytes 296 | tf_op jit(solution)/shard_map/ppermute | solution.py:849
  132.5 3.5 %collective-permute-start.9 = (s32[24]{0:T(128)S(1)}, s32[24]{0:T(128)S(1)}, u32[]{:S(2)}, u32[]{:S(2)}) collective-permute-start(s32[24]{0:T(128)S(1)} %copy-done.12), channel_id=1, source_target_pairs={{0,4},{2,6},{4,0},{6,2},{8,12},{10,14},{12,8},{14,10},{16,20},{18,... | collective-permute-start | bytes 296 | tf_op jit(solution)/shard_map/ppermute | solution.py:849
  133.7 3.5 %collective-permute-start.8 = (s32[24]{0:T(128)S(1)}, s32[24]{0:T(128)S(1)}, u32[]{:S(2)}, u32[]{:S(2)}) collective-permute-start(s32[24]{0:T(128)S(1)} %copy-done.12), channel_id=1, source_target_pairs={{0,2},{2,0},{4,6},{6,4},{8,10},{10,8},{12,14},{14,12},{16,18},{18,... | collective-permute-start | bytes 296 | tf_op jit(solution)/shard_map/ppermute | solution.py:849
  135.2 18.4 %collective-permute-start.7 = (bf16[1536,150]{0,1:T(8,128)(2,1)S(1)}, bf16[1536,150]{0,1:T(8,128)(2,1)S(1)}, u32[]{:S(2)}, u32[]{:S(2)}) collective-permute-start(bf16[1536,150]{0,1:T(8,128)(2,1)S(1)} %copy.34), channel_id=1, source_target_pairs={{0,1},{1,0},{2,3},{3,2},{4,5},{5,4},{6,7},{7,6},{8,9},{9,8},{10,11... | collective-permute-start | bytes 1382408 | tf_op jit(solution)/shard_map/ppermute | solution.py:852
  137.9 14.8 %collective-permute-start.12 = (bf16[128,1536]{1,0:T(8,128)(2,1)}, bf16[128,1536]{1,0:T(8,128)(2,1)}, u32[]{:S(2)}, u32[]{:S(2)}) collective-permute-start(bf16[128,1536]{1,0:T(8,128)(2,1)} %get-tuple-element.65), channel_id=1, source_target_pairs={{0,2},{2,0},{4,6},{6,4},{8,10},{10,8},{12,14},{14,12},{16,18},{18,... | collective-permute-start | bytes 1179656 | tf_op jit(solution)/shard_map/ppermute | solution.py:849
  139.1 14.4 %collective-permute-start.14 = (bf16[128,1536]{1,0:T(8,128)(2,1)}, bf16[128,1536]{1,0:T(8,128)(2,1)}, u32[]{:S(2)}, u32[]{:S(2)}) collective-permute-start(bf16[128,1536]{1,0:T(8,128)(2,1)} %get-tuple-element.66), channel_id=1, source_target_pairs={{0,4},{2,6},{4,0},{6,2},{8,12},{10,14},{12,8},{14,10},{16,20},{18,... | collective-permute-start | bytes 1179656 | tf_op jit(solution)/shard_map/ppermute | solution.py:849
  140.0 1.2 collective-permute-start.25
  140.1 0.7 copy-start.1
  141.1 11.6 %collective-permute-start.16 = (bf16[64,1536]{1,0:T(8,128)(2,1)}, bf16[64,1536]{1,0:T(8,128)(2,1)S(1)}, u32[]{:S(2)}, u32[]{:S(2)}) collective-permute-start(bf16[64,1536]{1,0:T(8,128)(2,1)} %get-tuple-element.67), channel_id=1, source_target_pairs={{0,6},{2,4},{4,2},{6,0},{8,14},{10,12},{12,10},{14,8},{16,22},{18,... | collective-permute-start | bytes 589832 | tf_op jit(solution)/shard_map/ppermute | solution.py:849
  152.7 17.5 %copy-start.17 = (bf16[64,1536]{1,0:T(8,128)(2,1)}, bf16[64,1536]{1,0:T(8,128)(2,1)S(1)}, u32[]{:S(2)}) copy-start(bf16[64,1536]{1,0:T(8,128)(2,1)S(1)} %collective-permute-done.16.refs_11_) | copy-start | bytes 589828
  152.7 37.5 %collective-permute-start.24 = (bf16[1536,256]{1,0:T(8,128)(2,1)S(1)}, bf16[1536,256]{1,0:T(8,128)(2,1)}, u32[]{:S(2)}, u32[]{:S(2)}) collective-permute-start(bf16[1536,256]{1,0:T(8,128)(2,1)S(1)} %copy-done.15), channel_id=1, source_target_pairs={{0,1},{1,0},{2,3},{3,2},{4,5},{5,4},{6,7},{7,6},{8,9},{9,8},{10,11... | collective-permute-start | bytes 2359304 | tf_op jit(solution)/shard_map/ppermute | solution.py:852
  152.7 17.4 %collective-permute-start.17 = (bf16[64,1536]{1,0:T(8,128)(2,1)S(1)}, bf16[64,1536]{1,0:T(8,128)(2,1)}, u32[]{:S(2)}, u32[]{:S(2)}) collective-permute-start(bf16[64,1536]{1,0:T(8,128)(2,1)S(1)} %collective-permute-done.16.refs_11_), channel_id=1, source_target_pairs={{0,1},{1,0},{2,3},{3,2},{4,5},{5,4},{6,7},{7,6},{8,9},{9,8},{10,11... | collective-permute-start | bytes 589832 | tf_op jit(solution)/shard_map/ppermute | solution.py:852
  153.5 16.6 %collective-permute-start.13 = (bf16[128,1536]{1,0:T(8,128)(2,1)}, bf16[128,1536]{1,0:T(8,128)(2,1)S(1)}, u32[]{:S(2)}, u32[]{:S(2)}) collective-permute-start(bf16[128,1536]{1,0:T(8,128)(2,1)} %collective-permute-done.12.refs_7_), channel_id=1, source_target_pairs={{0,1},{1,0},{2,3},{3,2},{4,5},{5,4},{6,7},{7,6},{8,9},{9,8},{10,11... | collective-permute-start | bytes 1179656 | tf_op jit(solution)/shard_map/ppermute | solution.py:852
  153.5 16.6 %collective-permute-start.15 = (bf16[128,1536]{1,0:T(8,128)(2,1)}, bf16[128,1536]{1,0:T(8,128)(2,1)}, u32[]{:S(2)}, u32[]{:S(2)}) collective-permute-start(bf16[128,1536]{1,0:T(8,128)(2,1)} %collective-permute-done.14.refs_9_), channel_id=1, source_target_pairs={{0,1},{1,0},{2,3},{3,2},{4,5},{5,4},{6,7},{7,6},{8,9},{9,8},{10,11... | collective-permute-start | bytes 1179656 | tf_op jit(solution)/shard_map/ppermute | solution.py:852
  170.2 0.7 copy-start.16
  181.2 4.9 %copy-start.13 = (f32[150]{0:T(256)S(1)}, f32[150]{0:T(256)}, u32[]{:S(2)}) copy-start(f32[150]{0:T(256)} %param.24) | copy-start | bytes 1804
  183.7 4.8 %collective-permute-start.19 = (bf16[128,384]{1,0:T(8,128)(2,1)}, bf16[128,384]{1,0:T(8,128)(2,1)S(1)}, u32[]{:S(2)}, u32[]{:S(2)}) collective-permute-start(bf16[128,384]{1,0:T(8,128)(2,1)} %get-tuple-element.74), channel_id=1, source_target_pairs={{0,2},{2,0},{4,6},{6,4},{8,10},{10,8},{12,14},{14,12},{16,18},{18,... | collective-permute-start | bytes 294920 | tf_op jit(solution)/shard_map/ppermute | solution.py:849
  184.7 2.6 copy-start.18
  184.7 4.8 %copy-start.10 = (f32[8,256]{1,0:T(8,128)S(1)}, f32[8,256]{1,0:T(8,128)}, u32[]{:S(2)}) copy-start(f32[8,256]{1,0:T(8,128)} %dp_sum3.1.refs_4_) | copy-start | bytes 24580
  184.7 4.8 %collective-permute-start.21 = (bf16[128,384]{1,0:T(8,128)(2,1)}, bf16[128,384]{1,0:T(8,128)(2,1)S(1)}, u32[]{:S(2)}, u32[]{:S(2)}) collective-permute-start(bf16[128,384]{1,0:T(8,128)(2,1)} %get-tuple-element.75), channel_id=1, source_target_pairs={{0,4},{2,6},{4,0},{6,2},{8,12},{10,14},{12,8},{14,10},{16,20},{18,... | collective-permute-start | bytes 294920 | tf_op jit(solution)/shard_map/ppermute | solution.py:849
  187.3 2.9 collective-permute-start.18
  187.3 3.6 %collective-permute-start.23 = (bf16[384,256]{1,0:T(8,128)(2,1)S(1)}, bf16[384,256]{1,0:T(8,128)(2,1)S(1)}, u32[]{:S(2)}, u32[]{:S(2)}) collective-permute-start(bf16[384,256]{1,0:T(8,128)(2,1)S(1)} %copy-done.18), channel_id=1, source_target_pairs={{0,1},{1,0},{2,3},{3,2},{4,5},{5,4},{6,7},{7,6},{8,9},{9,8},{10,11... | collective-permute-start | bytes 589832 | tf_op jit(solution)/shard_map/ppermute | solution.py:852
  188.6 2.3 copy-start.22
  188.6 1.6 collective-permute-start.20
  189.6 1.3 copy-start.23
  189.6 1.3 collective-permute-start.22
  190.2 0.7 copy-start.19
  190.2 0.7 copy-start.24
  190.9 0.6 copy-start.25
  190.9 0.7 copy-start.20
  339.8 4.0 %copy-start.3 = (f32[4,32,1024]{2,1,0:T(8,128)S(1)}, f32[4,32,1024]{2,1,0:T(8,128)}, u32[]{:S(2)}) copy-start(f32[4,32,1024]{2,1,0:T(8,128)} %get-tuple-element.79) | copy-start | bytes 1572868
  339.8 4.8 %copy-start.2 = (f32[9,32,1024]{2,1,0:T(8,128)S(1)}, f32[9,32,1024]{2,1,0:T(8,128)}, u32[]{:S(2)}) copy-start(f32[9,32,1024]{2,1,0:T(8,128)} %get-tuple-element.80) | copy-start | bytes 3538948
  343.8 1.8 copy-start.5
Sparse Core Ops, SparseCore 0:
  141.0 167.5 all-reduce.1

commit v3 on v2

--- a/solution.py
+++ b/solution.py
@@ -111,17 +111,19 @@
     return jnp.concatenate([column_block] * times, axis=1)
 
 
-def rows_down(boxes_ref, canvas, box_count, x_ref, xs, at):
+def rows_down(boxes_ref, canvas, box_count, x_ref, xs, n):
     gate = pixel_gates(boxes_ref, canvas, box_count, (PX, CELLS), 0)
+    canv = xs.shape[0] // 3
     reps = xs.shape[2] // CELLS
     blank = jnp.zeros((CW, xs.shape[2]), BF16)
     up = wide(gate(-1, 0).astype(BF16), reps)
     down = wide(gate(1, 0).astype(BF16), reps)
-    xs[0, at : at + CW] = blank
-    xs[0, at + CW : at + PX] = x_ref[at : at + PX - CW] * up[CW:]
-    xs[1, at : at + PX] = x_ref[at : at + PX] * wide(gate(0, 0).astype(BF16), reps)
-    xs[2, at : at + PX - CW] = x_ref[at + CW : at + PX] * down[: PX - CW]
-    xs[2, at + PX - CW : at + PX] = blank
+    at = n * PX
+    xs[n, 0:CW] = blank
+    xs[n, CW:PX] = x_ref[at : at + PX - CW] * up[CW:]
+    xs[canv + n] = x_ref[at : at + PX] * wide(gate(0, 0).astype(BF16), reps)
+    xs[2 * canv + n, 0 : PX - CW] = x_ref[at + CW : at + PX] * down[: PX - CW]
+    xs[2 * canv + n, PX - CW : PX] = blank
 
 
 def member_bounds(table_at, height, width):
@@ -220,7 +222,7 @@
         part_ref[4 + level : 5 + level, :] = second
 
 
-def exchange_kernel(total, own_ref, out_ref, slots, send_sem, recv_sem):
+def signal_all(total, chan_too=False):
     me = lax.axis_index("dp")
     chan = lax.axis_index("chan")
     barrier = pltpu.get_barrier_semaphore()
@@ -230,49 +232,96 @@
         return carry
 
     lax.fori_loop(1, total, signal, 0)
-    slots[me] = own_ref[...]
-    pl.semaphore_wait(barrier, total - 1)
-
-    def copy_to(step):
+    if chan_too:
+        pl.semaphore_signal(barrier, inc=1, device_id=(me, 1 - chan), device_id_type=MESH)
+    return total if chan_too else total - 1
+
+
+class Exchange:
+    def __init__(self, total, own, slots, send_sem, recv_sem, parted=False):
+        self.total, self.own, self.slots, self.send_sem, self.recv_sem = total, own, slots, send_sem, recv_sem
+        self.me = lax.axis_index("dp")
+        self.parted = parted
+
+    def block(self, device):
+        return self.own.at[device] if self.parted else self.own
+
+    def copy_to(self, step):
         return pltpu.make_async_remote_copy(
-            src_ref=own_ref,
-            dst_ref=slots.at[me],
-            send_sem=send_sem.at[step],
-            recv_sem=recv_sem.at[me],
-            device_id=(lax.rem(me + step, total), chan),
+            src_ref=self.block(lax.rem(self.me + step, self.total)),
+            dst_ref=self.slots.at[self.me],
+            send_sem=self.send_sem.at[step],
+            recv_sem=self.recv_sem.at[self.me],
+            device_id=(lax.rem(self.me + step, self.total), lax.axis_index("chan")),
             device_id_type=MESH,
         )
 
-    def copy_from(step):
-        other = lax.rem(me + total - step, total)
+    def copy_from(self, step):
+        other = lax.rem(self.me + self.total - step, self.total)
         return pltpu.make_async_remote_copy(
-            src_ref=own_ref,
-            dst_ref=slots.at[other],
-            send_sem=send_sem.at[step],
-            recv_sem=recv_sem.at[other],
-            device_id=(other, chan),
+            src_ref=self.block(other),
+            dst_ref=self.slots.at[other],
+            send_sem=self.send_sem.at[step],
+            recv_sem=self.recv_sem.at[other],
+            device_id=(other, lax.axis_index("chan")),
             device_id_type=MESH,
         )
 
-    def start(step, carry):
-        copy_to(step).start()
-        return carry
-
-    def finish(step, carry):
-        copy_from(step).wait_recv()
-        return carry
-
-    def sent(step, carry):
-        copy_to(step).wait_send()
-        return carry
-
-    lax.fori_loop(1, total, start, 0)
-    lax.fori_loop(1, total, finish, 0)
-    lax.fori_loop(1, total, sent, 0)
-    value = slots[0]
-    for other in range(1, total):
-        value = value + slots[other]
-    out_ref[...] = value
+    def start(self):
+        self.slots[self.me] = self.block(self.me)[...]
+
+        def one(step, carry):
+            self.copy_to(step).start()
+            return carry
+
+        lax.fori_loop(1, self.total, one, 0)
+
+    def arrive(self):
+        def one(step, carry):
+            self.copy_from(step).wait_recv()
+            return carry
+
+        def sent(step, carry):
+            self.copy_to(step).wait_send()
+            return carry
+
+        lax.fori_loop(1, self.total, one, 0)
+        lax.fori_loop(1, self.total, sent, 0)
+
+    def finish(self):
+        self.arrive()
+        value = self.slots[0]
+        for other in range(1, self.total):
+            value = value + self.slots[other]
+        return value
+
+
+def exchange_kernel(total, own_ref, out_ref, slots, send_sem, recv_sem):
+    expected = signal_all(total)
+    pl.semaphore_wait(pltpu.get_barrier_semaphore(), expected)
+    exchange = Exchange(total, own_ref, slots, send_sem, recv_sem)
+    exchange.start()
+    out_ref[...] = exchange.finish()
+
+
+def exchange_scratch(total, width, times):
+    return [
+        pltpu.VMEM((times, 8, width), F32),
+        pltpu.VMEM((times, total, 8, width), F32),
+        pltpu.SemaphoreType.DMA((times, total)),
+        pltpu.SemaphoreType.DMA((times, total)),
+    ]
+
+
+def core_copy(source, target, send_sem, recv_sem):
+    return pltpu.make_async_remote_copy(
+        src_ref=source,
+        dst_ref=target,
+        send_sem=send_sem,
+        recv_sem=recv_sem,
+        device_id=(lax.axis_index("dp"), 1 - lax.axis_index("chan")),
+        device_id_type=MESH,
+    )
 
 
 def dp_sum(part, total, number, after=()):
@@ -332,21 +381,23 @@
     def _():
         expand(y_ref[...], cells_ref, ye)
         for n in range(canv):
-            rows_down(boxes_ref, n, box_count, x_ref, xs, n * PX)
+            rows_down(boxes_ref, n, box_count, x_ref, xs, n)
 
     for n in range(canv):
-        rows = slice(n * PX, (n + 1) * PX)
-        q = dot(xs[0, rows], wfx_ref[0, 0]) + dot(xs[1, rows], wfx_ref[1, 0]) + dot(xs[2, rows], wfx_ref[2, 0])
-        gate = wide(pixel_gates(boxes_ref, n, box_count, (PX, CELLS), 0)(0, t - 1), reps)
-        q = gate * pltpu.roll(q, (PX + 1 - t) % PX, 0)
+        q = dot(xs[n], wfx_ref[0, 0]) + dot(xs[canv + n], wfx_ref[1, 0]) + dot(xs[2 * canv + n], wfx_ref[2, 0])
+        gate = pixel_gates(boxes_ref, n, box_count, (PX, CELLS), 0)
 
         @pl.when(t == 0)
         def _():
-            f[n] = q
-
-        @pl.when(t > 0)
+            f[n] = wide(gate(0, -1), reps) * pltpu.roll(q, 1, 0)
+
+        @pl.when(t == 1)
         def _():
             f[n] += q
+
+        @pl.when(t == 2)
+        def _():
+            f[n] += wide(gate(0, 1), reps) * pltpu.roll(q, PX - 1, 0)
 
     for dy in range(3):
         term = dot(ye[...], wfb_ref[dy, 0].reshape(ye.shape[1], mid)).astype(BF16)
@@ -364,57 +415,83 @@
             send_ref[rows] = f[n, :, pl.ds(pl.multiple_of((1 - chan) * half, half), half)].astype(BF16)
 
 
-def join_sums_kernel(canv, box_count, boxes_ref, own_ref, got_ref, f_ref, part_ref):
-    n = pl.program_id(0)
-    f = own_ref[...] + got_ref[...].astype(F32)
-    f_ref[...] = f
-
-    @pl.when(n == 0)
-    def _():
-        part_ref[...] = jnp.zeros_like(part_ref)
-
+def head_kernel(
+    canv, box_count, total, each,
+    boxes_ref, own_ref, send_ref, gain_ref, bias_ref, w_ref, bcls_ref, g_ref,
+    logits_ref, df_ref, pack_ref, send_a, send_b, send_d, dw_ref, sums_ref,
+    dw, got, f, db, score, score_got, flip, part, slots, send_sem, recv_sem, core_send, core_recv,
+):
+    half = own_ref.shape[1]
+    ncls = g_ref.shape[1]
+    chan = lax.axis_index("chan")
+    own = pl.ds(pl.multiple_of(chan * half, half), half)
+    expected = signal_all(total, True)
+    pl.semaphore_wait(pltpu.get_barrier_semaphore(), expected)
+    swap_f = core_copy(send_ref, got, core_send.at[0], core_recv.at[0])
+    swap_f.start()
+    part[...] = jnp.zeros_like(part)
+    dw[...] = jnp.zeros_like(dw)
     area = 0
-    for box in range(box_count):
-        side = box_at(boxes_ref, n, box, box_count)
-        area = area + side[2] * side[3]
-    part_ref[0:1, :] += jnp.sum(f, 0, keepdims=True)
-    part_ref[1:2, :] += jnp.sum(f * f, 0, keepdims=True)
-    part_ref[2:3, :] += jnp.full((1, f.shape[1]), area.astype(F32), F32)
-
-
-def join_stat(total_ref):
-    count = total_ref[2:3, :]
-    mean = total_ref[0:1, :] / count
-    var = total_ref[1:2, :] / count - mean * mean
-    return mean, lax.rsqrt(var + EPS), count
-
-
-def head_kernel(box_count, boxes_ref, f_ref, total_ref, gain_ref, bias_ref, w_ref, g_ref, score_ref, db_ref, part_ref, dw_ref):
-    n = pl.program_id(0)
-    half = f_ref.shape[1]
-    chan = lax.axis_index("chan")
-    w = w_ref[pl.ds(pl.multiple_of(chan * half, half), half), :]
-    own = pl.ds(pl.multiple_of(chan * half, half), half)
-    valid = wide(pixel_gates(boxes_ref, n, box_count, (PX, CELLS), 0)(0, 0), half // CELLS)
-    mean, rstd, _ = join_stat(total_ref)
-    norm = (f_ref[...] - mean) * rstd
-    act = gain_ref[:, own] * norm + bias_ref[:, own]
-    sig = jax.nn.sigmoid(act)
-    hidden = (act * sig * valid).astype(BF16)
-    g = g_ref[...]
-    score_ref[...] = dot(hidden, w).astype(BF16)
-    db = dot_nt(g, w) * valid * sig * (1.0 + act * (1.0 - sig))
-    db_ref[...] = db
-
-    @pl.when(n == 0)
-    def _():
-        part_ref[...] = jnp.zeros_like(part_ref)
-        dw_ref[...] = jnp.zeros_like(dw_ref)
-
-    part_ref[0:1, :] += jnp.sum(db * norm, 0, keepdims=True)
-    part_ref[1:2, :] += jnp.sum(db, 0, keepdims=True)
-    part_ref[2:3, : g.shape[1]] += jnp.sum(g.astype(F32), 0, keepdims=True)
-    dw_ref[...] += dot_tn(hidden, g)
+    for n in range(canv):
+        for box in range(box_count):
+            side = box_at(boxes_ref, n, box, box_count)
+            area = area + side[2] * side[3]
+    part[0, 2:3, :] = jnp.full((1, half), area.astype(F32), F32)
+    swap_f.wait()
+    for n in range(canv):
+        rows = slice(n * PX, (n + 1) * PX)
+        value = own_ref[rows] + got[rows].astype(F32)
+        f[rows] = value
+        part[0, 0:1, :] += jnp.sum(value, 0, keepdims=True)
+        part[0, 1:2, :] += jnp.sum(value * value, 0, keepdims=True)
+    first = Exchange(total, part.at[0], slots.at[0], send_sem.at[0], recv_sem.at[0])
+    first.start()
+    f_total = first.finish()
+    count = f_total[2:3, :]
+    mean = f_total[0:1, :] / count
+    rstd = lax.rsqrt(f_total[1:2, :] / count - mean * mean + EPS)
+    gain, bias, w = gain_ref[:, own], bias_ref[:, own], w_ref[own, :]
+    valid = [wide(pixel_gates(boxes_ref, n, box_count, (PX, CELLS), 0)(0, 0), half // CELLS) for n in range(canv)]
+    for n in range(canv):
+        rows = slice(n * PX, (n + 1) * PX)
+        norm = (f[rows] - mean) * rstd
+        f[rows] = norm
+        act = gain * norm + bias
+        sig = jax.nn.sigmoid(act)
+        hidden = (act * sig * valid[n]).astype(BF16)
+        g = g_ref[rows]
+        score[rows] = dot(hidden, w).astype(BF16)
+        value = dot_nt(g, w) * valid[n] * sig * (1.0 + act * (1.0 - sig))
+        db[rows] = value
+        part[1, 0:1, :] += jnp.sum(value * norm, 0, keepdims=True)
+        part[1, 1:2, :] += jnp.sum(value, 0, keepdims=True)
+        part[1, 2:3, :ncls] += jnp.sum(g.astype(F32), 0, keepdims=True)
+        dw[...] += dot_tn(hidden, g)
+    second = Exchange(total, part.at[1], slots.at[1], send_sem.at[1], recv_sem.at[1])
+    second.start()
+    swap_score = core_copy(score, score_got, core_send.at[1], core_recv.at[1])
+    swap_score.start()
+    sums = second.finish()
+    sums_ref[...] = sums
+    scale = gain * rstd
+    for n in range(canv):
+        rows = slice(n * PX, (n + 1) * PX)
+        df = scale * (db[rows] - sums[1:2, :] / count - f[rows] * (sums[0:1, :] / count)) * valid[n]
+        df_ref[rows] = df.astype(BF16)
+        flip[...] = pltranspose(df)
+        span = pl.ds(n * PX, PX)
+        pack_ref[0:half, span] = flip[...].astype(BF16)
+        views = [pack_ref.at[half : half + half // 2, span], send_a.at[:, span]]
+        views += [pack_ref.at[half + half // 2 : 2 * half, span], send_b.at[:, span], send_d.at[:, span]]
+        split_rows(flip, half // (4 * each), each, *views)
+    strip = dw_ref.shape[1]
+    for device in range(total):
+        dw_ref[device] = dw[device * strip : (device + 1) * strip]
+    swap_score.wait()
+    for n in range(canv):
+        rows = slice(n * PX, (n + 1) * PX)
+        both = score[rows].astype(F32) + score_got[rows].astype(F32)
+        logits_ref[rows] = (both + bcls_ref[...]).astype(BF16)
 
 
 def split_rows(rows, groups, each, own_a, send_a, own_b, send_b, send_d=None):
@@ -436,92 +513,16 @@
             send_d[group * each : (group + 1) * each] = piece(group, 1 - y_bit, 1 - x_bit)
 
 
-def join_grad_kernel(box_count, each, boxes_ref, f_ref, db_ref, total_ref, sums_ref, gain_ref, df_ref, pack_ref, send_a, send_b, send_d, flip):
-    n = pl.program_id(0)
-    half = f_ref.shape[1]
-    own = pl.ds(pl.multiple_of(lax.axis_index("chan") * half, half), half)
-    valid = wide(pixel_gates(boxes_ref, n, box_count, (PX, CELLS), 0)(0, 0), half // CELLS)
-    mean, rstd, count = join_stat(total_ref)
-    norm = (f_ref[...] - mean) * rstd
-    df = gain_ref[:, own] * rstd * (db_ref[...] - sums_ref[1:2, :] / count - norm * (sums_ref[0:1, :] / count)) * valid
-    df_ref[...] = df.astype(BF16)
-    flip[...] = pltranspose(df)
-    pack_ref[0:half] = flip[...].astype(BF16)
-    own_a = pack_ref.at[half : half + half // 2]
-    own_b = pack_ref.at[half + half // 2 : 2 * half]
-    split_rows(flip, half // (4 * each), each, own_a, send_a, own_b, send_b, send_d)
-
-
-def branch_back_kernel(canv, cells_ref, lanes_ref, own_ref, got_ref, lift_ref, w_ref, norm_ref, act_ref, da_ref, part_ref, acc, grads):
-    d = pl.program_id(0)
-    half = own_ref.shape[0]
-    chan = lax.axis_index("chan")
-
-    @pl.when(d == 0)
-    def _():
-        for ref, which in ((own_ref, chan), (got_ref, 1 - chan)):
-            for n in range(canv):
-                found = dot(ref[:, n * PX : (n + 1) * PX], lift_ref[n]).astype(BF16)
-                for e in range(9):
-                    into = pl.ds(pl.multiple_of(which * half, half), half)
-                    grads[e, into, n * CELLS : (n + 1) * CELLS] = found[:, e * CELLS : (e + 1) * CELLS]
-
-    part = dot(w_ref[0].reshape(acc.shape[0], 2 * half), grads[d])
-
-    @pl.when(d == 0)
-    def _():
-        acc[...] = part
-
-    @pl.when(d > 0)
-    def _():
-        acc[...] += part
-
-    @pl.when(d == 8)
-    def _():
-        width = norm_ref.shape[1]
-        levels = jnp.concatenate([lanes_ref[4:5, :]] * canv, axis=1)
-        dy = 0.0
-        for level in range(4):
-            dy = dy + jnp.where(levels == level, acc[level * width : (level + 1) * width], 0.0)
-        dy = pltranspose(dy)
-        act = act_ref[...]
-        sig = jax.nn.sigmoid(act)
-        da = dy * sig * (1.0 + act * (1.0 - sig))
-        da_ref[...] = da
-        for level in range(4):
-            gain = bias = 0.0
-            for n in range(canv):
-                rows = slice(n * CELLS, (n + 1) * CELLS)
-                mine = jnp.where(cells_ref[:, 4:5] == level, da[rows], 0.0)
-                gain = gain + jnp.sum(mine * norm_ref[rows], 0, keepdims=True)
-                bias = bias + jnp.sum(mine, 0, keepdims=True)
-            part_ref[level : level + 1, :] = gain
-            part_ref[4 + level : 5 + level, :] = bias
-
-
-def branch_dz_kernel(canv, rows_all, each, cells_ref, da_ref, norm_ref, total_ref, sums_ref, gain_ref, dz_ref, pack_ref, send_a, send_b, flip):
-    for n in range(canv):
-        rows = slice(n * CELLS, (n + 1) * CELLS)
-        dz = 0.0
-        for level in range(4):
-            _, rstd = branch_stat(total_ref, level, rows_all[level])
-            here = jnp.where(cells_ref[:, 4:5] == level, 1.0, 0.0)
-            mean_gain = sums_ref[level : level + 1, :] / rows_all[level]
-            mean_bias = sums_ref[4 + level : 5 + level, :] / rows_all[level]
-            mine = gain_ref[level : level + 1, :] * rstd * (da_ref[rows] - mean_bias - norm_ref[rows] * mean_gain)
-            dz = dz + here * mine
-        dz_ref[rows] = dz.astype(BF16)
-        flip[:, rows] = pltranspose(dz)
-    half = flip.shape[0]
-    split_rows(flip, half // (4 * each), each, pack_ref.at[0 : half // 2], send_a, pack_ref.at[half // 2 : half], send_b)
-
-
 def put_rows(out, index, own_ref, other_ref):
     chan = lax.axis_index("chan")
     size = own_ref.shape[0]
     width = own_ref.shape[1]
     for ref, which in ((own_ref, chan), (other_ref, 1 - chan)):
-        out[index, pl.ds(pl.multiple_of(which * size, size), size), :width] = ref[...]
+        into = pl.ds(pl.multiple_of(which * size, size), size)
+        if index is None:
+            out[into, :width] = ref[...]
+        else:
+            out[index, into, :width] = ref[...]
 
 
 def cols_across(boxes_ref, canvas, at, box_count, own_ref, other_ref, lhs):
@@ -537,6 +538,10 @@
         lhs[2, into, span] = (pltpu.roll(value, 1, 1) * gate(0, -1)[0:1]).astype(BF16)
 
 
+def reversed_bits(number, bits):
+    return sum(((number >> bit) & 1) << (bits - 1 - bit) for bit in range(bits))
+
+
 def split_out(count, bit, acc, keep, send):
     parts, _, each, _ = keep.shape
     groups = parts // 2
@@ -547,7 +552,7 @@
             for ref, which in ((keep, bit), (send, 1 - bit)):
                 for group in range(groups):
                     at = (half * 2 + which) * block + group * each
-                    ref[half * groups + group, d] = acc[d, pl.ds(pl.multiple_of(at, each), each), :].astype(BF16)
+                    ref[reversed_bits(half * groups + group, parts.bit_length() - 1), d] = acc[d, pl.ds(pl.multiple_of(at, each), each), :].astype(BF16)
         return carry
 
     lax.fori_loop(0, count, one, 0)
@@ -555,13 +560,16 @@
 
 def tail_kernel(
     canv, box_count,
-    boxes_ref, lanes_ref, cells_ref, qa0, qa1, qb0, qb1, ga0, ga1, gb0, gb1, gd0, gd1, y_ref, pooled_ref,
-    za0, za1, zb0, zb1, zga0, zga1, zgb0, zgb1, dz0, dz1, df0, df1, x_any, xm_any, ym_any, wfx_any, wbr_any,
-    gx_ref, out_fx, out_fb, out_br,
-    lhs4, lift, grads, xbuf, wbuf, xd, lhs, acc, pool_mate, kept,
+    total_dp, rows_all,
+    boxes_ref, lanes_ref, cells_ref, pack0, sa, sb, sd, df0, y_ref, pooled_ref, norm_ref, act_ref, ztotal_ref, zgain_ref, dw_ref,
+    x_any, xm_any, ym_any, wfx_any, wfb_any, wbr_any,
+    gx_ref, out_fx, out_fb, out_br, sums_ref, dw_own, dw_other,
+    dw_slots, dw_sum, dw_send, dw_recv, pack1, df1, ga0, ga1, gb0, gb1, gd0, gd1, zpack0, zpack1, zsa, zsb, zga0, zga1, zgb0, zgb1, dz0, dz1, da,
+    part, slots, sum_send, sum_recv, core_send, core_recv, near_send, near_recv,
+    lift, grads, xbuf, wbuf, xd, lhs, acc, pool_mate,
     fb_send, fb_recv, keep_a, send_a, recv_a, zrecv_a, keep_b, send_b, recv_b, zrecv_b,
     bkeep_a, bsend_a, brecv_a, bzrecv_a, bkeep_b, bsend_b, brecv_b, bzrecv_b,
-    load_sem, w_sem, mate_send, mate_recv, part_send, part_recv,
+    load_sem, store_sem, w_sem, fb_sem, mate_send, mate_recv, part_send, part_recv,
 ):
     me = lax.axis_index("dp")
     chan = lax.axis_index("chan")
@@ -574,12 +582,16 @@
     x_mate = me + 1 - 2 * x_bit
     y_mate = me + 2 - 4 * y_bit
 
-    def peer(step):
-        return lax.rem(group + step, parts) * PLANE + place
-
-    barrier = pltpu.get_barrier_semaphore()
-    for other in [x_mate, y_mate] + [peer(step) for step in range(1, parts)]:
-        pl.semaphore_signal(barrier, inc=1, device_id=(other, chan), device_id_type=MESH)
+    stages = parts.bit_length() - 1
+
+    def group_bit(stage):
+        return (group // 2**stage) % 2
+
+    def group_mate(stage):
+        return (group + 2**stage * (1 - 2 * group_bit(stage))) * PLANE + place
+
+    d_mate = x_mate + y_mate - me
+    expected = signal_all(total_dp, True)
 
     def load(source, slot, which):
         return pltpu.make_async_copy(source, xbuf.at[slot], load_sem.at[which])
@@ -601,7 +613,14 @@
             w_sem.at[lax.rem(tile, 2)],
         )
 
-    tile_load(0).start()
+    levels_at_once = wfb_any.shape[1]
+
+    def fb_load(d):
+        at = lax.rem(d, 4) * levels_at_once
+        return pltpu.make_async_copy(wfb_any.at[d], wbuf.at[pl.ds(at, levels_at_once)], fb_sem.at[lax.rem(d, 4)])
+
+    for d in range(3):
+        fb_load(d).start()
 
     def mate_copy(number, source, target, mate):
         return pltpu.make_async_remote_copy(
@@ -609,27 +628,150 @@
             device_id=(mate, chan), device_id_type=MESH,
         )
 
-    def part_copy(number, step, source, target):
+    class Halving:
+        def __init__(self, number, keep, recv):
+            self.number, self.keep, self.recv = number, keep, recv
+            self.copies = []
+
+        def kept(self, stage):
+            at = 0
+            for bit in range(stage):
+                at = at + group_bit(bit) * (parts >> (bit + 1))
+            return at
+
+        def send(self):
+            stage = len(self.copies)
+            count = parts >> (stage + 1)
+            from_at = self.kept(stage) + (1 - group_bit(stage)) * count
+            number = self.number * stages + stage
+            copy = pltpu.make_async_remote_copy(
+                src_ref=self.keep.at[pl.ds(from_at, count)],
+                dst_ref=self.recv.at[pl.ds(parts - 2 * count, count)],
+                send_sem=part_send.at[number],
+                recv_sem=part_recv.at[number],
+                device_id=(group_mate(stage), chan),
+                device_id_type=MESH,
+            )
+            copy.start()
+            self.copies.append(copy)
+
+        def receive(self):
+            stage = len(self.copies)
+            self.copies[-1].wait_recv()
+            if stage == stages:
+                return
+            count = parts >> stage
+            at = self.kept(stage)
+
+            def add(d, carry):
+                for part in range(count):
+                    got = self.recv[parts - 2 * count + part, d].astype(F32)
+                    self.keep[at + part, d] = (self.keep[at + part, d].astype(F32) + got).astype(BF16)
+                return carry
+
+            lax.fori_loop(0, self.keep.shape[1], add, 0)
+            self.send()
+
+    def near_copy(number, source, target, mate):
         return pltpu.make_async_remote_copy(
-            src_ref=source.at[lax.rem(group + step, parts)], dst_ref=target.at[step - 1],
-            send_sem=part_send.at[number * (parts - 1) + step - 1], recv_sem=part_recv.at[number * (parts - 1) + step - 1],
-            device_id=(peer(step), chan), device_id_type=MESH,
+            src_ref=source, dst_ref=target, send_sem=near_send.at[number], recv_sem=near_recv.at[number],
+            device_id=(mate, chan), device_id_type=MESH,
         )
 
+    def swap_copy(number, source, target):
+        return core_copy(source, target, core_send.at[number], core_recv.at[number])
+
+    pl.semaphore_wait(pltpu.get_barrier_semaphore(), expected)
+    swaps = [swap_copy(0, pack0, pack1), swap_copy(1, df0, df1)]
+    near = [near_copy(0, sa, ga0, x_mate), near_copy(1, sb, gb0, y_mate), near_copy(2, sd, gd0, d_mate)]
+    for copy in swaps + near:
+        copy.start()
+    dw_parts = Exchange(total_dp, dw_ref, dw_slots, dw_send.at[0], dw_recv.at[0], True)
+    dw_parts.start()
+
+    def lift_of(n):
+        def store(d, y, block):
+            lift[y * CW : (y + 1) * CW, d * CELLS : (d + 1) * CELLS] = block
+
+        gated_lifts(boxes_ref, n, box_count, lanes_ref, store)
+
+    rows = canv * CELLS
+    for n in range(canv):
+        lift_of(n)
+        for ref, which in ((pack0, chan), (pack1, 1 - chan)):
+            if n == 0 and ref is pack1:
+                swaps[0].wait_recv()
+            found = dot(ref[:half, n * PX : (n + 1) * PX], lift[...]).astype(BF16)
+            into = pl.ds(pl.multiple_of(which * half, half), half)
+            for e in range(9):
+                xd[e, into, n * CELLS : (n + 1) * CELLS] = found[:, e * CELLS : (e + 1) * CELLS]
+
+    def back(d, carry):
+        fb_load(d).wait()
+
+        @pl.when(d + 3 < 9)
+        def _():
+            fb_load(d + 3).start()
+
+        for level in range(4):
+            found = dot(wbuf[lax.rem(d, 4) * levels_at_once + level], xd[d, :, :rows])
+
+            @pl.when(d == 0)
+            def _():
+                acc[level, :, :rows] = found
+
+            @pl.when(d > 0)
+            def _():
+                acc[level, :, :rows] += found
+
+        return carry
+
+    lax.fori_loop(0, 9, back, 0)
+    tile_load(0).start()
+    levels = jnp.concatenate([lanes_ref[4:5, :]] * canv, axis=1)
+    dy = 0.0
+    for level in range(4):
+        dy = dy + jnp.where(levels == level, acc[level, :, :rows], 0.0)
+    dy = pltranspose(dy)
+    sig = jax.nn.sigmoid(act_ref[...])
+    da[...] = dy * sig * (1.0 + act_ref[...] * (1.0 - sig))
+    for level in range(4):
+        gain = bias = 0.0
+        for n in range(canv):
+            at = slice(n * CELLS, (n + 1) * CELLS)
+            mine = jnp.where(cells_ref[:, 4:5] == level, da[at], 0.0)
+            gain = gain + jnp.sum(mine * norm_ref[at], 0, keepdims=True)
+            bias = bias + jnp.sum(mine, 0, keepdims=True)
+        part[0, level : level + 1, :] = gain
+        part[0, 4 + level : 5 + level, :] = bias
+    exchange = Exchange(total_dp, part.at[0], slots.at[0], sum_send.at[0], sum_recv.at[0])
+    exchange.start()
+    dw_sum[...] = dw_parts.finish()
+    dw_sums = Exchange(total_dp, dw_sum, dw_own, dw_send.at[1], dw_recv.at[1])
+    dw_sums.start()
+    for number, (source, target) in enumerate(((ga0, ga1), (gb0, gb1), (gd0, gd1))):
+        near[number].wait_recv()
+        swaps.append(swap_copy(2 + number, source, target))
+        swaps[-1].start()
+    for number in range(2, 5):
+        swaps[number].wait_recv()
+
+    half_a, half_b = half, half + half // 2
+    qa0, qa1 = pack0.at[half_a:half_b], pack1.at[half_a:half_b]
+    qb0, qb1 = pack0.at[half_b : 2 * half], pack1.at[half_b : 2 * half]
     ye = gx_ref
     expand(y_ref[...], cells_ref, ye)
     size = gd0.shape[0]
+    cols = 2 * size
     for source, (own_ref, oth_ref, bit) in enumerate(((qa0, qa1, y_bit), (ga0, ga1, y_bit), (gb0, gb1, x_bit), (gd0, gd1, 0))):
         mine = pl.ds(pl.multiple_of(bit * size, size), size)
-        put_rows(lhs4, source, own_ref.at[mine], oth_ref.at[mine])
+        put_rows(lhs.at[source // 2, source % 2 * cols : (source % 2 + 1) * cols], None, own_ref.at[mine], oth_ref.at[mine])
 
     def canvas(n, carry):
-        def store(d, y, block):
-            lift[y * CW : (y + 1) * CW, d * CELLS : (d + 1) * CELLS] = block
-
-        gated_lifts(boxes_ref, n, box_count, lanes_ref, store)
-        rows = lhs4[n // canv, :, pl.ds(pl.multiple_of((n % canv) * PX, PX), PX)]
-        found = dot(rows, lift[...]).astype(BF16)
+        lift_of(n)
+        source = n // canv
+        at = pl.ds(pl.multiple_of(lax.rem(source, 2) * cols, cols), cols)
+        found = dot(lhs[source // 2, at, pl.ds(pl.multiple_of((n % canv) * PX, PX), PX)], lift[...]).astype(BF16)
         for d in range(9):
             grads[d, :, pl.ds(pl.multiple_of(n * CELLS, CELLS), CELLS)] = found[:, d * CELLS : (d + 1) * CELLS]
         return carry
@@ -639,10 +781,33 @@
     for d in range(9):
         result = dot(grads[d], ye[...])
         for part in range(parts):
-            fb_send[part, d] = result[part * each : (part + 1) * each].astype(BF16)
-    pl.semaphore_wait(barrier, parts + 1)
-    fb_copies = [part_copy(0, step, fb_send, fb_recv) for step in range(1, parts)]
-    for copy in fb_copies:
+            fb_send[reversed_bits(part, stages), d] = result[part * each : (part + 1) * each].astype(BF16)
+    fb_way = Halving(0, fb_send, fb_recv)
+    fb_way.send()
+
+    sums = exchange.finish()
+    sums_ref[...] = sums
+    dw_sums.arrive()
+    zflip = acc.at[4, :, 0:rows]
+    for n in range(canv):
+        at = slice(n * CELLS, (n + 1) * CELLS)
+        dz = 0.0
+        for level in range(4):
+            _, rstd = branch_stat(ztotal_ref, level, rows_all[level])
+            here = jnp.where(cells_ref[:, 4:5] == level, 1.0, 0.0)
+            mean_gain = sums[level : level + 1, :] / rows_all[level]
+            mean_bias = sums[4 + level : 5 + level, :] / rows_all[level]
+            mine = zgain_ref[level : level + 1, :] * rstd * (da[at] - mean_bias - norm_ref[at] * mean_gain)
+            dz = dz + here * mine
+        dz0[at] = dz.astype(BF16)
+        zflip[:, at] = pltranspose(dz)
+    quarter = half // 2
+    split_rows(zflip, half // (4 * each), each, zpack0.at[0:quarter], zsa, zpack0.at[quarter:half], zsb)
+    swaps += [swap_copy(5, zpack0, zpack1), swap_copy(6, dz0, dz1)]
+    dw_swap = swap_copy(9, dw_own, dw_other)
+    dw_swap.start()
+    near += [near_copy(3, zsa, zga0, x_mate), near_copy(4, zsb, zgb0, y_mate)]
+    for copy in swaps[5:] + near[3:]:
         copy.start()
 
     mate_copies = []
@@ -654,7 +819,7 @@
         for number, (device, own_ref, oth_ref, slot) in enumerate(sources):
             loads[2 * side + slot].wait()
             for n in range(canv):
-                rows_down(boxes_ref, device * canv + n, box_count, xbuf.at[slot], xd, n * PX)
+                rows_down(boxes_ref, device * canv + n, box_count, xbuf.at[slot], xd, n)
                 cols_across(boxes_ref, device * canv + n, n, box_count, own_ref, oth_ref, lhs)
                 if number:
                     select, count = members(
@@ -665,14 +830,22 @@
             if side == 0:
                 loads[2 + slot].start()
             for d in range(9):
-                part = dot(lhs[d % 3], xd[d // 3])
-                acc[d] = part if number == 0 else acc[d] + part
+                across = xd[d // 3 * canv : (d // 3 + 1) * canv].reshape(pixels, span)
+                found = dot(lhs[d % 3], across)
+                acc[d] = found if number == 0 else acc[d] + found
         split_out(9, bit, acc, keep, send)
         mate_copies.append(mate_copy(side, send, recv, mate))
         mate_copies[-1].start()
-
-    levels = jnp.concatenate([lanes_ref[4:5, :]] * canv, axis=1)
-    rows = canv * CELLS
+        if side == 0:
+            for number, (source, target) in enumerate(((zga0, zga1), (zgb0, zgb1))):
+                near[3 + number].wait_recv()
+                swaps.append(swap_copy(7 + number, source, target))
+                swaps[-1].start()
+
+    for number in (5, 7, 8):
+        swaps[number].wait_recv()
+    za0, za1 = zpack0.at[0:quarter], zpack1.at[0:quarter]
+    zb0, zb1 = zpack0.at[quarter:half], zpack1.at[quarter:half]
     sides = (
         (0, za0, za1, zga0, zga1, y_bit, bkeep_a, bsend_a, brecv_a, y_mate),
         (1, zb0, zb1, zgb0, zgb1, x_bit, bkeep_b, bsend_b, brecv_b, x_mate),
@@ -687,7 +860,7 @@
         mate_copies.append(mate_copy(2 + side, send, recv, mate))
         mate_copies[-1].start()
 
-    part_copies = []
+    ways = [fb_way]
 
     def pass_on(number, keep, recv, target):
         mate_copies[number].wait_recv()
@@ -698,19 +871,22 @@
             return carry
 
         lax.fori_loop(0, keep.shape[1], add, 0)
-        for step in range(1, parts):
-            part_copies.append(part_copy(1 + number, step, keep, target))
-            part_copies[-1].start()
-
+        ways.append(Halving(1 + number, keep, target))
+        ways[-1].send()
+
+    fb_way.receive()
+
+    swaps[1].wait_recv()
+    swaps[6].wait_recv()
     for n in range(canv):
         gate = pixel_gates(boxes_ref, n, box_count, (PX, CELLS), 0)
         at = slice(n * PX, (n + 1) * PX)
         for which, ref in ((chan, df0), (1 - chan, df1)):
             into = pl.ds(pl.multiple_of(which * half, half), half)
             df = ref[at].astype(F32)
-            xd[1, at, into] = ref[at]
-            xd[0, at, into] = (wide(gate(0, 1), half // CELLS) * pltpu.roll(df, PX - 1, 0)).astype(BF16)
-            xd[2, at, into] = (wide(gate(0, -1), half // CELLS) * pltpu.roll(df, 1, 0)).astype(BF16)
+            xd[canv + n, :, into] = ref[at]
+            xd[n, :, into] = (wide(gate(0, 1), half // CELLS) * pltpu.roll(df, PX - 1, 0)).astype(BF16)
+            xd[2 * canv + n, :, into] = (wide(gate(0, -1), half // CELLS) * pltpu.roll(df, 1, 0)).astype(BF16)
 
     width = wbuf.shape[1]
     tiles = wfx_any.shape[1] // width
@@ -728,20 +904,19 @@
             gate = pixel_gates(boxes_ref, n, box_count, (PX, CELLS), 0)
             total = None
             for dy in range(3):
-                part = dot_nt(xd[0, at], wbuf[first + dy * 3])
+                found = dot_nt(xd[n], wbuf[first + dy * 3])
                 for dx in range(1, 3):
-                    part = part + dot_nt(xd[dx, at], wbuf[first + dy * 3 + dx])
+                    found = found + dot_nt(xd[dx * canv + n], wbuf[first + dy * 3 + dx])
                 if dy != 1:
-                    part = wide(gate(1 - dy, 0), width // CELLS) * pltpu.roll(part, ((dy - 1) * CW) % PX, 0)
-                total = part if total is None else total + part
+                    found = wide(gate(1 - dy, 0), width // CELLS) * pltpu.roll(found, ((dy - 1) * CW) % PX, 0)
+                total = found if total is None else total + found
             gx_ref[at, pl.ds(pl.multiple_of(t * width, width), width)] = total.astype(BF16)
         return carry
 
-    lax.fori_loop(0, 1, tile, 0)
+    lax.fori_loop(0, 2, tile, 0)
     pass_on(0, keep_a, recv_a, zrecv_a)
-    lax.fori_loop(1, 3, tile, 0)
+    lax.fori_loop(2, tiles, tile, 0)
     pass_on(1, keep_b, recv_b, zrecv_b)
-    lax.fori_loop(3, tiles, tile, 0)
 
     wbr_load = pltpu.make_async_copy(wbr_any, wbuf.at[pl.ds(0, wbr_any.shape[0])], load_sem.at[4])
     wbr_load.start()
@@ -763,36 +938,55 @@
     for m in range(canv):
         _, _, high, across = by_box(boxes_ref, m, cells_ref[:, 0:1], box_count)
         r0, r1, c0, c1 = member_bounds(lambda row: cells_ref[:, row : row + 1], high, across)
-        kept[m] = (total[m * CELLS : (m + 1) * CELLS] / ((r1 - r0) * (c1 - c0))).astype(BF16)
+        mean = (total[m * CELLS : (m + 1) * CELLS] / ((r1 - r0) * (c1 - c0))).astype(BF16)
+        for side in range(2):
+            pool_mate[side, m * CELLS : (m + 1) * CELLS] = mean[:, side * span : (side + 1) * span]
     for n in range(canv):
         at = slice(n * PX, (n + 1) * PX)
         select, _ = members(boxes_ref, n, box_count, lambda row: lanes_ref[row : row + 1, :], (PX, CELLS), 0)
-        gx_ref[at] = (gx_ref[at].astype(F32) + dot(select.astype(BF16), kept[n])).astype(BF16)
+        for side in range(2):
+            into = slice(side * span, (side + 1) * span)
+            pooled = dot(select.astype(BF16), pool_mate[side, n * CELLS : (n + 1) * CELLS])
+            gx_ref[at, into] = (gx_ref[at, into].astype(F32) + pooled).astype(BF16)
 
     pass_on(2, bkeep_a, brecv_a, bzrecv_a)
     pass_on(3, bkeep_b, brecv_b, bzrecv_b)
-
-    def finish(copies, keep, recv, out, spot):
-        for copy in copies:
-            copy.wait_recv()
+    for stage in range(1, stages):
+        for way in ways:
+            if len(way.copies) == stage:
+                way.receive()
+
+    stores = []
+
+    def finish(way, out, at, sides):
+        way.receive()
+        keep, recv = way.keep, way.recv
+        count = keep.shape[1]
+        lanes_of = keep.shape[3] // len(sides)
 
         def add(d, carry):
-            total = keep[group, d].astype(F32)
-            for step in range(parts - 1):
-                total = total + recv[step, d].astype(F32)
-            out[d, :, spot] = total
+            total = keep[way.kept(stages), d].astype(F32) + recv[parts - 2, d].astype(F32)
+            for place_at, _ in enumerate(sides):
+                row = at + place_at * each
+                acc[d, row : row + each] = total[:, place_at * lanes_of : (place_at + 1) * lanes_of]
             return carry
 
-        lax.fori_loop(0, out.shape[0], add, 0)
-
-    first, last = slice(0, span), slice(span, 2 * span)
-    steps = parts - 1
-    finish(fb_copies, fb_send, fb_recv, out_fb, slice(0, out_fb.shape[2]))
-    finish(part_copies[:steps], keep_a, zrecv_a, out_fx, first)
-    finish(part_copies[steps : 2 * steps], keep_b, zrecv_b, out_fx, last)
-    finish(part_copies[2 * steps : 3 * steps], bkeep_a, bzrecv_a, out_br, first)
-    finish(part_copies[3 * steps :], bkeep_b, bzrecv_b, out_br, last)
-    for copy in fb_copies + mate_copies + part_copies:
+        lax.fori_loop(0, count, add, 0)
+        for place_at, side in enumerate(sides):
+            source = acc.at[pl.ds(0, count), pl.ds(at + place_at * each, each), :]
+            target = out.at[:, :, pl.ds(side * lanes_of, lanes_of)]
+            stores.append(pltpu.make_async_copy(source, target, store_sem.at[len(stores)]))
+            stores[-1].start()
+
+    finish(ways[0], out_fb, 0, (0, 1))
+    finish(ways[1], out_fx, 2 * each, (0,))
+    finish(ways[2], out_fx, 3 * each, (1,))
+    finish(ways[3], out_br, 4 * each, (0,))
+    finish(ways[4], out_br, 5 * each, (1,))
+    for copy in stores:
+        copy.wait()
+    dw_swap.wait()
+    for copy in mate_copies + swaps + near + [copy for way in ways for copy in way.copies]:
         copy.wait_send()
 
 
@@ -923,7 +1117,7 @@
         out_specs=[whole((pixels, half)), whole((pixels, half))],
         out_shape=[shaped((pixels, half), F32), shaped((pixels, half), BF16)],
         scratch_shapes=[
-            pltpu.VMEM((3, pixels, cin), BF16),
+            pltpu.VMEM((3 * canv, PX, cin), BF16),
             pltpu.VMEM((rows, 4 * bw), BF16),
             pltpu.VMEM((canv, 9 * CELLS, mid), BF16),
             pltpu.VMEM((canv, PX, mid), F32),
@@ -931,110 +1125,41 @@
         compiler_params=params(),
         name="join",
     )(flat, cells, features, y, lifts, w_fx.reshape(3, 3, cin, mid), w_fb.reshape(3, 3, 4, bw, mid))
-    f_got = swap(f_send)
-    by_canvas = pl.BlockSpec((PX, half), lambda i: (i, 0))
-    f, f_part = launch(
-        functools.partial(join_sums_kernel, canv, box_count),
-        grid=(canv,),
-        in_specs=[SMEM_SPEC, by_canvas, by_canvas],
-        out_specs=[by_canvas, whole((8, half))],
-        out_shape=[shaped((pixels, half), F32), shaped((8, half), F32)],
-        compiler_params=params(),
-        name="join_sums",
-        after=(x_mate, y_mate, y_all),
-    )(flat, f_own, f_got)
-    f_total = dp_sum(f_part, dp, 1)
-    gain_row = gain_join.reshape(1, mid)
-    bias_row = bias_join.reshape(1, mid)
-    score, db, db_part, dw_cls = launch(
-        functools.partial(head_kernel, box_count),
-        grid=(canv,),
-        in_specs=[
-            SMEM_SPEC,
-            by_canvas,
-            whole((8, half)),
-            whole((1, mid)),
-            whole((1, mid)),
-            whole((mid, ncls)),
-            pl.BlockSpec((PX, ncls), lambda i: (i, 0)),
-        ],
-        out_specs=[pl.BlockSpec((PX, ncls), lambda i: (i, 0)), by_canvas, whole((8, half)), whole((half, ncls))],
+    quarter = half // 2
+    bundle = quarter // 2
+    logits, df, pack, send_a, send_b, send_d, dw_cls, db_total = launch(
+        functools.partial(head_kernel, canv, box_count, dp, each),
+        in_specs=[SMEM_SPEC] + [VMEM_SPEC] * 7,
+        out_specs=[VMEM_SPEC] * 8,
         out_shape=[
             shaped((pixels, ncls), BF16),
-            shaped((pixels, half), F32),
+            shaped((pixels, half), BF16),
+            shaped((2 * half, pixels), BF16),
+            shaped((quarter, pixels), BF16),
+            shaped((quarter, pixels), BF16),
+            shaped((bundle, pixels), BF16),
+            shaped((dp, half // dp, ncls), F32),
             shaped((8, half), F32),
-            shaped((half, ncls), F32),
         ],
-        compiler_params=params(),
+        scratch_shapes=[
+            pltpu.VMEM((half, ncls), F32),
+            pltpu.VMEM((pixels, half), BF16),
+            pltpu.VMEM((pixels, half), F32),
+            pltpu.VMEM((pixels, half), F32),
+            pltpu.VMEM((pixels, ncls), BF16),
+            pltpu.VMEM((pixels, ncls), BF16),
+            pltpu.VMEM((half, PX), F32),
+        ]
+        + exchange_scratch(dp, half, 2)
+        + [pltpu.SemaphoreType.DMA((2,)), pltpu.SemaphoreType.DMA((2,))],
+        compiler_params=params(collective_id=1, has_side_effects=True),
         name="head",
-    )(flat, f, f_total, gain_row, bias_row, w_cls, grad_logits)
-    db_total = dp_sum(db_part, dp, 2)
-    logits = (score.astype(F32) + swap(score).astype(F32) + b_cls).astype(BF16)
-    quarter = half // 2
-    df, pack, send_a, send_b, send_d = launch(
-        functools.partial(join_grad_kernel, box_count, each),
-        grid=(canv,),
-        in_specs=[SMEM_SPEC, by_canvas, by_canvas, whole((8, half)), whole((8, half)), whole((1, mid))],
-        out_specs=[by_canvas]
-        + [pl.BlockSpec((size, PX), lambda i: (0, i)) for size in (2 * half, quarter, quarter, quarter // 2)],
-        out_shape=[shaped((pixels, half), BF16)]
-        + [shaped((size, pixels), BF16) for size in (2 * half, quarter, quarter, quarter // 2)],
-        scratch_shapes=[pltpu.VMEM((half, PX), F32)],
-        compiler_params=params(),
-        name="join_grad",
-    )(flat, f, db, f_total, db_total, gain_row)
-    got_a, got_b, got_d = to_mate(send_a, 1), to_mate(send_b, 2), to_mate(send_d, 3)
-    pack_other = swap(pack)
-    df_got = swap(df)
-    other_a, other_b, other_d = swap(got_a), swap(got_b), swap(got_d)
-    half_rows = pl.BlockSpec((half, pixels), lambda i: (0, 0))
-
-    da, da_part = launch(
-        functools.partial(branch_back_kernel, canv),
-        grid=(9,),
-        in_specs=[
-            whole(cells.shape),
-            whole(lanes.shape),
-            half_rows,
-            half_rows,
-            whole((canv, PX, 9 * CELLS)),
-            pl.BlockSpec((1, 4, bw, mid), lambda i: (i, 0, 0, 0)),
-            whole((rows, bw)),
-            whole((rows, bw)),
-        ],
-        out_specs=[whole((rows, bw)), whole((8, bw))],
-        out_shape=[shaped((rows, bw), F32), shaped((8, bw), F32)],
-        scratch_shapes=[pltpu.VMEM((4 * bw, rows), F32), pltpu.VMEM((9, mid, rows), BF16)],
-        compiler_params=params(),
-        name="branch_back",
-    )(cells, lanes, pack, pack_other, lifts, w_fb, z_norm, z_act)
-    da_total = dp_sum(da_part, dp, 3, (other_a, other_b, other_d))
-    dz, zpack, zsend_a, zsend_b = launch(
-        functools.partial(branch_dz_kernel, canv, rows_all, each),
-        in_specs=[VMEM_SPEC] * 6,
-        out_specs=[VMEM_SPEC] * 4,
-        out_shape=[
-            shaped((rows, bw), BF16),
-            shaped((bw, rows), BF16),
-            shaped((quarter, rows), BF16),
-            shaped((quarter, rows), BF16),
-        ],
-        scratch_shapes=[pltpu.VMEM((bw, rows), F32)],
-        compiler_params=params(),
-        name="branch_dz",
-    )(cells, da, z_norm, z_total, da_total, gain_branch)
-    zgot_a, zgot_b = to_mate(zsend_a, 1), to_mate(zsend_b, 2)
-    dz_got, zpack_other, zother_a, zother_b = swap(dz), swap(zpack), swap(zgot_a), swap(zgot_b)
+        after=(x_mate, y_mate, y_all),
+    )(flat, f_own, f_send, gain_join.reshape(1, mid), bias_join.reshape(1, mid), w_cls, b_cls.reshape(1, ncls), grad_logits)
 
     span = cin // 2
-    bundle = quarter // 2
     tile = cin // 4
-
-    def quarter_at(at):
-        return pl.BlockSpec((quarter, pixels), lambda i: (at, 0))
-
-    def zquarter_at(at):
-        return pl.BlockSpec((quarter, rows), lambda i: (at, 0))
+    stages = parts.bit_length() - 1
 
     def buffers(count, width):
         return [
@@ -1044,49 +1169,47 @@
             pltpu.VMEM((parts - 1, count, each, width), BF16),
         ]
 
-    grad_features, sum_fx, sum_fb, sum_br = launch(
-        functools.partial(tail_kernel, canv, box_count),
-        grid=(1,),
-        in_specs=[
-            SMEM_SPEC,
-            whole(lanes.shape),
-            whole(cells.shape),
-            quarter_at(2),
-            quarter_at(2),
-            quarter_at(3),
-            quarter_at(3),
-        ]
-        + [whole((quarter, pixels))] * 4
-        + [whole((bundle, pixels))] * 2
-        + [whole((PLANE * rows, bw)), whole((rows, cin))]
-        + [zquarter_at(0), zquarter_at(0), zquarter_at(1), zquarter_at(1)]
-        + [whole((quarter, rows))] * 4
-        + [whole((rows, bw))] * 2
-        + [whole((pixels, half))] * 2
-        + [ANY_SPEC] * 5,
-        out_specs=[
-            whole((pixels, cin)),
-            whole((9, each, cin)),
-            whole((9, each, 4 * bw)),
-            whole((4, each, cin)),
-        ],
+    def sems(*counts):
+        return [pltpu.SemaphoreType.DMA((count,)) for count in counts]
+
+    near_rows = [pltpu.VMEM((quarter, pixels), BF16)] * 4 + [pltpu.VMEM((bundle, pixels), BF16)] * 2
+    near_cells = [pltpu.VMEM((quarter, rows), BF16)] * 6
+    grad_features, sum_fx, sum_fb, sum_br, da_total, dw_own, dw_other = launch(
+        functools.partial(tail_kernel, canv, box_count, dp, rows_all),
+        in_specs=[SMEM_SPEC] + [VMEM_SPEC] * 3 + [ANY_SPEC] * 3 + [VMEM_SPEC] * 8 + [ANY_SPEC] * 6,
+        out_specs=[VMEM_SPEC] + [ANY_SPEC] * 3 + [VMEM_SPEC] * 3,
         out_shape=[
             shaped((pixels, cin), BF16),
             shaped((9, each, cin), F32),
             shaped((9, each, 4 * bw), F32),
             shaped((4, each, cin), F32),
+            shaped((8, bw), F32),
+            shaped((dp, half // dp, ncls), F32),
+            shaped((dp, half // dp, ncls), F32),
         ],
         scratch_shapes=[
-            pltpu.VMEM((PLANE, cols, pixels), BF16),
+            pltpu.VMEM((dp, half // dp, ncls), F32),
+            pltpu.VMEM((half // dp, ncls), F32),
+            pltpu.SemaphoreType.DMA((2, dp)),
+            pltpu.SemaphoreType.DMA((2, dp)),
+            pltpu.VMEM((2 * half, pixels), BF16),
+            pltpu.VMEM((pixels, half), BF16),
+        ]
+        + near_rows
+        + [pltpu.VMEM((bw, rows), BF16), pltpu.VMEM((bw, rows), BF16)]
+        + near_cells
+        + [pltpu.VMEM((rows, bw), BF16), pltpu.VMEM((rows, bw), BF16), pltpu.VMEM((rows, bw), F32)]
+        + exchange_scratch(dp, bw, 1)
+        + sems(10, 10, 5, 5)
+        + [
             pltpu.VMEM((PX, 9 * CELLS), BF16),
             pltpu.VMEM((9, cols, PLANE * rows), BF16),
             pltpu.VMEM((2, pixels, span), BF16),
             pltpu.VMEM((18, tile, mid), BF16),
-            pltpu.VMEM((3, pixels, mid), BF16),
+            pltpu.VMEM((3 * canv, PX, mid), BF16),
             pltpu.VMEM((3, half, pixels), BF16),
             pltpu.VMEM((9, half, span), F32),
             pltpu.VMEM((2, rows, span), BF16),
-            pltpu.VMEM((canv, CELLS, cin), BF16),
             pltpu.VMEM((parts, 9, each, 4 * bw), BF16),
             pltpu.VMEM((parts - 1, 9, each, 4 * bw), BF16),
         ]
@@ -1094,20 +1217,12 @@
         + buffers(9, span)
         + buffers(4, span)
         + buffers(4, span)
-        + [
-            pltpu.SemaphoreType.DMA((5,)),
-            pltpu.SemaphoreType.DMA((2,)),
-            pltpu.SemaphoreType.DMA((4,)),
-            pltpu.SemaphoreType.DMA((4,)),
-            pltpu.SemaphoreType.DMA((5 * (parts - 1),)),
-            pltpu.SemaphoreType.DMA((5 * (parts - 1),)),
-        ],
-        compiler_params=pltpu.CompilerParams(vmem_limit_bytes=62 * 2**20, collective_id=4, has_side_effects=True),
+        + sems(5, 6, 2, 4, 4, 4, 5 * stages, 5 * stages),
+        compiler_params=pltpu.CompilerParams(vmem_limit_bytes=63 * 2**20, collective_id=4, has_side_effects=True),
         name="tail",
     )(
-        flat_all, lanes, cells, pack, pack_other, pack, pack_other, got_a, other_a, got_b, other_b, got_d, other_d,
-        y_all, pooled, zpack, zpack_other, zpack, zpack_other, zgot_a, zother_a, zgot_b, zother_b, dz, dz_got, df, df_got,
-        features, x_mate, y_mate, w_fx, w_branch.reshape(16, tile, br),
+        flat_all, lanes, cells, pack, send_a, send_b, send_d, df, y_all, pooled, z_norm, z_act, z_total, gain_branch, dw_cls,
+        features, x_mate, y_mate, w_fx, w_fb, w_branch.reshape(16, tile, br),
     )
     out_fx = jnp.transpose(sum_fx, (0, 2, 1))
     out_fb = jnp.transpose(sum_fb.reshape(9, each, 4, bw), (0, 2, 3, 1))
@@ -1116,8 +1231,8 @@
     small = db_total[:2]
     small_got = swap(small)
     small_all = jnp.concatenate([jnp.where(chan == 0, small, small_got), jnp.where(chan == 0, small_got, small)], 1)
-    placed = jnp.zeros((mid, ncls), F32)
-    grad_w_cls = lax.psum(lax.dynamic_update_slice_in_dim(placed, dw_cls, chan * half, 0), ("dp", "chan"))
+    dw_halves = [jnp.where(chan == 0, dw_own, dw_other), jnp.where(chan == 0, dw_other, dw_own)]
+    grad_w_cls = jnp.concatenate([a.reshape(half, ncls) for a in dw_halves], 0)
     return (
         logits,
         grad_features,

time: 358 us -> 280 us (0.78)
  Pallas kernels: 275 us -> 242 us
  waiting for transfers between devices: 27.7 us -> 1.52 us
  between operations: 14.6 us -> 1.23 us
  starting transfers between devices: 15.4 us -> 9.34 us
    pallas_call x14 -> x7, Pallas kernels: 275 us -> 242 us  [launch(): return lambda *operands: call(*operands, *after)]
    ppermute x13 -> x8, waiting for transfers between devices: 25.2 us -> 1.52 us  [to_mate(): return lax.ppermute(array, 'dp', [(i, i ^ mate) for i in range(dp)])]
    ppermute x13 -> x8, starting transfers between devices: 13.7 us -> 9.34 us  [to_mate(): return lax.ppermute(array, 'dp', [(i, i ^ mate) for i in range(dp)])]
    unnamed x62 -> x31, local copies, waits for them, and re-layouts: 13.2 us -> 10.3 us
  transfers between devices with their start and end apart: 27 -> 10, of which waited for: 13 -> 3; matrix products, arithmetic and copies ran while one was open for 3% -> 4% of each run, Pallas kernels for 62% -> 70%
where the time goes in v3:
time: 280 us; the launch traced here: 276 us
  Pallas kernels  242 us (86%)
  local copies, waits for them, and re-layouts  17.6 us (6%)
  starting transfers between devices  9.34 us (3%)
  other arithmetic  3.7 us (1%)
    pallas_call x7, Pallas kernels, launch(): return lambda *operands: call(*operands, *after)  242 us
    unnamed x31, local copies, waits for them, and re-layouts  10.3 us
    ppermute x8, starting transfers between devices, to_mate(): return lax.ppermute(array, 'dp', [(i, i ^ mate) for i in range(dp)])  9.34 us
  transfers between devices with their start and end apart: 10, of which 3 were waited for; matrix products, arithmetic and copies ran while one was open for 4% of the time, Pallas kernels for 70%

profile of v3, /device:TPU:8, one launch (start us, length us, event | category | flops | bytes accessed | tf_op | source)
XLA Modules:
  0.0 275.7 jit_solution(14797563914882582430)
XLA Ops:
  0.6 1.3 reshape.52.refs_0_
  1.9 0.0 copy-start.7
  1.9 0.0 copy-start.5
  1.9 0.0 copy-start.3
  1.9 9.9 %pool.1 = (bf16[384,1024]{1,0:T(8,128)(2,1)}, bf16[3,512,1152]{2,1,0:T(8,128)(2,1)}, f32[384,256]{1,0:T(8,128)}, bf16[384,256]{1,0:T(8,128)(2,1)}, bf16[1536,512]{1,0:T(8,128)(2,1)}, /*index=5*/bf16[1536,512]{1,0:T(8,128)(2,1)}) custom-call(s32[24]{0:T(128)} %reshape.52.refs_0_, f32[8,128]{1,0:T(8,128)} %constant.10.clone.refs_1_, ...), custom_call_target="tpu_custom_call" | custom-call | flops 12000000000 | tf_op jit(solution)/shard_map/pool/pallas_call | solution.py:1011
  11.8 0.0 collective-permute-start
  11.8 0.0 copy-done.7
  11.9 2.5 collective-permute-start.8
  14.4 0.5 collective-permute-start.7
  14.9 0.5 collective-permute-start.6
  15.4 0.0 copy-done.5
  15.4 0.8 copy.27.refs_5_
  16.3 0.0 copy-done.3
  16.3 1.2 copy.28.refs_7_
  17.5 0.0 collective-permute-done.8
  17.5 0.5 collective-permute-done.7
  17.9 0.5 collective-permute-done.6
  18.4 0.6 pad_add_fusion.refs_0_
  19.0 0.0 collective-permute-done.refs_2_
  19.0 0.0 copy-start.10
  19.0 0.7 copy-done.10
  19.7 2.0 branch_sums.1
  21.7 9.4 %dp_sum0.1.refs_2_.refs_12_ = f32[8,256]{1,0:T(8,128)} custom-call(f32[8,256]{1,0:T(8,128)} %get-tuple-element.44.refs_0_), custom_call_target="tpu_custom_call" | custom-call | flops 10000000000 | tf_op jit(solution)/shard_map/dp_sum0/pallas_call | solution.py:1011
  31.1 2.5 branch_act.1
  33.7 1.7 collective-permute-start.5
  35.4 0.4 collective-permute-start.4
  35.8 1.3 collective-permute-start.3
  37.1 0.7 collective-permute-start.1
  37.8 1.6 collective-permute-start.2
  39.4 0.0 copy-start.4
  39.4 37.2 %join.1 = (f32[1536,256]{1,0:T(8,128)}, bf16[1536,256]{1,0:T(8,128)(2,1)}) custom-call(s32[24]{0:T(128)} %reshape.52.refs_0_, f32[128,128]{1,0:T(8,128)} %constant.11.clone.refs_2_.refs_0_.refs_1_, bf16[1536,1024]{1,0:T(8,128)(2,1)} %refs_15_.1, bf16[384,256]{1,0:T(8,128)(2,1)} %get-tuple-element.47.refs_3_, ...), custom_call_target="tpu_custom_call" | custom-call | flops 41999998976 | tf_op jit(solution)/shard_map/join/pallas_call | solution.py:1011
  76.6 0.0 copy-done.4
  76.6 0.0 collective-permute-done.3
  76.6 0.0 collective-permute-done.4
  76.7 0.0 collective-permute-done.5
  76.7 0.0 copy-start.6
  76.7 0.5 collective-permute-done.1.refs_8_.refs_16_
  77.3 0.0 copy-start.8
  77.3 0.0 collective-permute-done.2.refs_9_.refs_17_
  77.3 0.0 copy-start.9
  77.3 0.3 copy-done.6
  77.6 0.8 copy-done.8
  78.4 0.5 copy-done.9
  79.0 25.5 %head.1 = (bf16[1536,150]{1,0:T(8,128)(2,1)}, bf16[1536,256]{1,0:T(8,128)(2,1)}, bf16[512,1536]{1,0:T(8,128)(2,1)}, bf16[128,1536]{1,0:T(8,128)(2,1)}, bf16[128,...) custom-call(s32[24]{0:T(128)} %reshape.52.refs_0_, ...), custom_call_target="tpu_custom_call" | custom-call | flops 5000000000 | tf_op jit(solution)/shard_map/head/pallas_call | solution.py:1011
  104.5 0.7 slice.20
  105.2 0.0 collective-permute-start.9
  105.2 155.8 %tail.1 = (bf16[1536,1024]{1,0:T(8,128)(2,1)}, f32[9,32,1024]{2,1,0:T(8,128)}, f32[9,32,1024]{2,1,0:T(8,128)}, f32[4,32,1024]{2,1,0:T(8,128)}, f32[8,256]{1,0:T(...) custom-call(s32[96]{0:T(128)} %pad_add_fusion.refs_0_, f32[8,128]{1,0:T(8,128)} %constant.10.clone.refs_1_, ...), custom_call_target="tpu_custom_call" | custom-call | flops 10000000000 | tf_op jit(solution)/shard_map/tail/pallas_call | solution.py:1011
  261.0 1.4 fusion.1
  262.4 1.1 broadcast_select_fusion.1
  263.4 0.1 copy.30
  263.5 0.1 copy.31
  263.6 0.8 pad_maximum_fusion
  264.4 1.3 slice.23
  265.7 2.3 copy.32
  268.0 2.5 copy.35
  270.4 0.0 collective-permute-done.9
  270.4 0.7 broadcast_select_fusion.2
  271.1 0.6 pad_maximum_fusion.1
  271.7 0.0 copy-done
  271.7 1.7 copy.44
  273.4 0.0 copy-done.2
  273.4 0.8 copy.45
  274.2 0.1 copy-done.1
  274.3 1.0 copy.46
  (7 shorter events, 0.1 us)
Async XLA Ops:
  1.9 9.9 %copy-start.7 = (s32[24]{0:T(128)S(1)}, s32[24]{0:T(128)}, u32[]{:S(2)}) copy-start(s32[24]{0:T(128)} %reshape.52.refs_0_) | copy-start | bytes 292
  1.9 13.5 %copy-start.5 = (bf16[512,150]{0,1:T(8,128)(2,1)S(1)}, bf16[512,150]{0,1:T(8,128)(2,1)}, u32[]{:S(2)}) copy-start(bf16[512,150]{0,1:T(8,128)(2,1)} %param.23) | copy-start | bytes 460804
  1.9 14.3 %copy-start.3 = (bf16[1536,150]{0,1:T(8,128)(2,1)S(1)}, bf16[1536,150]{0,1:T(8,128)(2,1)}, u32[]{:S(2)}) copy-start(bf16[1536,150]{0,1:T(8,128)(2,1)} %param.25) | copy-start | bytes 1382404
  11.8 7.2 %collective-permute-start = (bf16[384,256]{1,0:T(8,128)(2,1)}, bf16[384,256]{1,0:T(8,128)(2,1)S(1)}, u32[]{:S(2)}, u32[]{:S(2)}) collective-permute-start(bf16[384,256]{1,0:T(8,128)(2,1)} %get-tuple-element.42), channel_id=1, source_target_pairs={{0,1},{1,0},{2,3},{3,2},{4,5},{5,4},{6,7},{7,6},{8,9},{9,8},{10,11... | collective-permute-start | bytes 589832 | tf_op jit(solution)/shard_map/ppermute | solution.py:1046
  11.9 5.6 %collective-permute-start.8 = (s32[24]{0:T(128)S(1)}, s32[24]{0:T(128)S(1)}, u32[]{:S(2)}, u32[]{:S(2)}) collective-permute-start(s32[24]{0:T(128)S(1)} %copy-done.7), channel_id=1, source_target_pairs={{0,6},{2,4},{4,2},{6,0},{8,14},{10,12},{12,10},{14,8},{16,22},{18,... | collective-permute-start | bytes 296 | tf_op jit(solution)/shard_map/ppermute | solution.py:1043
  14.4 3.5 %collective-permute-start.7 = (s32[24]{0:T(128)S(1)}, s32[24]{0:T(128)S(1)}, u32[]{:S(2)}, u32[]{:S(2)}) collective-permute-start(s32[24]{0:T(128)S(1)} %copy-done.7), channel_id=1, source_target_pairs={{0,4},{2,6},{4,0},{6,2},{8,12},{10,14},{12,8},{14,10},{16,20},{18,... | collective-permute-start | bytes 296 | tf_op jit(solution)/shard_map/ppermute | solution.py:1043
  14.9 3.5 %collective-permute-start.6 = (s32[24]{0:T(128)S(1)}, s32[24]{0:T(128)S(1)}, u32[]{:S(2)}, u32[]{:S(2)}) collective-permute-start(s32[24]{0:T(128)S(1)} %copy-done.7), channel_id=1, source_target_pairs={{0,2},{2,0},{4,6},{6,4},{8,10},{10,8},{12,14},{14,12},{16,18},{18,... | collective-permute-start | bytes 296 | tf_op jit(solution)/shard_map/ppermute | solution.py:1043
  19.0 0.7 copy-start.10
  33.7 43.0 %collective-permute-start.5 = (bf16[384,256]{1,0:T(8,128)(2,1)}, bf16[384,256]{1,0:T(8,128)(2,1)S(1)}, u32[]{:S(2)}, u32[]{:S(2)}) collective-permute-start(bf16[384,256]{1,0:T(8,128)(2,1)} %get-tuple-element.47.refs_3_), channel_id=1, source_target_pairs={{0,6},{2,4},{4,2},{6,0},{8,14},{10,12},{12,10},{14,8},{16,22},{18,... | collective-permute-start | bytes 589832 | tf_op jit(solution)/shard_map/ppermute | solution.py:1043
  35.4 41.3 %collective-permute-start.4 = (bf16[384,256]{1,0:T(8,128)(2,1)}, bf16[384,256]{1,0:T(8,128)(2,1)S(1)}, u32[]{:S(2)}, u32[]{:S(2)}) collective-permute-start(bf16[384,256]{1,0:T(8,128)(2,1)} %get-tuple-element.47.refs_3_), channel_id=1, source_target_pairs={{0,4},{2,6},{4,0},{6,2},{8,12},{10,14},{12,8},{14,10},{16,20},{18,... | collective-permute-start | bytes 589832 | tf_op jit(solution)/shard_map/ppermute | solution.py:1043
  35.8 40.8 %collective-permute-start.3 = (bf16[384,256]{1,0:T(8,128)(2,1)}, bf16[384,256]{1,0:T(8,128)(2,1)S(1)}, u32[]{:S(2)}, u32[]{:S(2)}) collective-permute-start(bf16[384,256]{1,0:T(8,128)(2,1)} %get-tuple-element.47.refs_3_), channel_id=1, source_target_pairs={{0,2},{2,0},{4,6},{6,4},{8,10},{10,8},{12,14},{14,12},{16,18},{18,... | collective-permute-start | bytes 589832 | tf_op jit(solution)/shard_map/ppermute | solution.py:1043
  37.1 40.1 %collective-permute-start.1 = (bf16[1536,512]{1,0:T(8,128)(2,1)}, bf16[1536,512]{1,0:T(8,128)(2,1)S(1)}, u32[]{:S(2)}, u32[]{:S(2)}) collective-permute-start(bf16[1536,512]{1,0:T(8,128)(2,1)} %get-tuple-element.51), channel_id=1, source_target_pairs={{0,2},{2,0},{4,6},{6,4},{8,10},{10,8},{12,14},{14,12},{16,18},{18,... | collective-permute-start | bytes 4718600 | tf_op jit(solution)/shard_map/ppermute | solution.py:1043
  37.8 39.4 %collective-permute-start.2 = (bf16[1536,512]{1,0:T(8,128)(2,1)}, bf16[1536,512]{1,0:T(8,128)(2,1)S(1)}, u32[]{:S(2)}, u32[]{:S(2)}) collective-permute-start(bf16[1536,512]{1,0:T(8,128)(2,1)} %get-tuple-element.52), channel_id=1, source_target_pairs={{0,4},{2,6},{4,0},{6,2},{8,12},{10,14},{12,8},{14,10},{16,20},{18,... | collective-permute-start | bytes 4718600 | tf_op jit(solution)/shard_map/ppermute | solution.py:1043
  39.4 37.2 %copy-start.4 = (bf16[384,256]{1,0:T(8,128)(2,1)S(1)}, bf16[384,256]{1,0:T(8,128)(2,1)}, u32[]{:S(2)}) copy-start(bf16[384,256]{1,0:T(8,128)(2,1)} %get-tuple-element.47.refs_3_) | copy-start | bytes 589828
  76.7 0.9 copy-start.6
  77.3 1.1 copy-start.8
  77.3 1.7 copy-start.9
  105.2 165.3 %collective-permute-start.9 = (f32[2,256]{1,0:T(2,128)S(1)}, f32[2,256]{1,0:T(2,128)S(1)}, u32[]{:S(2)}, u32[]{:S(2)}) collective-permute-start(f32[2,256]{1,0:T(2,128)S(1)} %slice.20), channel_id=1, source_target_pairs={{0,1},{1,0},{2,3},{3,2},{4,5},{5,4},{6,7},{7,6},{8,9},{9,8},{10,11... | collective-permute-start | bytes 6152 | tf_op jit(solution)/shard_map/ppermute | solution.py:1046
  265.7 6.0 %copy-start = (bf16[1536,1024]{1,0:T(8,128)(2,1)S(1)}, bf16[1536,1024]{1,0:T(8,128)(2,1)}, u32[]{:S(2)}) copy-start(bf16[1536,1024]{1,0:T(8,128)(2,1)} %get-tuple-element.102) | copy-start | bytes 9437188
  271.7 1.7 copy-start.2
  271.7 2.6 copy-start.1
